TPU v7x, 32 devices: a whole 2x2x4 slice. The times are simulated.
32 devices in a mesh: dp: 2 (over y), fsdp: 16 (over z, x, core).
Axes of the slice: x: 2, y: 2, z: 4, core: 2. Of those that a mesh axis runs over, the one named last changes fastest.
Arguments:
- field_five: bfloat16 [192, 5, 5, 512], P(('dp', 'fsdp')), may hold values from -6 to 6
- field_seven: bfloat16 [64, 7, 7, 512], P(('dp', 'fsdp')), may hold values from -6 to 6
- field_nine: bfloat16 [64, 9, 9, 512], P(('dp', 'fsdp')), may hold values from -6 to 6
- mask_five: int32 [192, 5, 5], P(('dp', 'fsdp')), may hold values from 0 to 1, as said below
- mask_seven: int32 [64, 7, 7], P(('dp', 'fsdp')), may hold values from 0 to 1, as said below
- mask_nine: int32 [64, 9, 9], P(('dp', 'fsdp')), may hold values from 0 to 1, as said below
- back_five: bfloat16 [192, 5, 5, 512], P(('dp', 'fsdp')), may hold values from -6 to 6
- back_seven: bfloat16 [64, 7, 7, 512], P(('dp', 'fsdp')), may hold values from -6 to 6
- back_nine: bfloat16 [64, 9, 9, 512], P(('dp', 'fsdp')), may hold values from -6 to 6
- kernels: float32 [2, 3, 3, 512, 512], P(None, None, None, None, 'fsdp'), may hold values from -0.09375 to 0.09375
- norm_params: float32 [4, 512], P(None, 'fsdp'), may hold values from 0.4 to 1.6
- kernel_first: float32 [2, 3, 3, 512, 512], P(None, None, None, None, 'fsdp'), may hold values from -320 to 320
- kernel_second: float32 [2, 3, 3, 512, 512], P(None, None, None, None, 'fsdp'), may hold values from 2624 to 10496
- norm_first: float32 [4, 512], P(None, 'fsdp'), may hold values from -320 to 320
- norm_second: float32 [4, 512], P(None, 'fsdp'), may hold values from 2624 to 10496
Outputs:
- out_five: bfloat16 [192, 5, 5, 512], P(('dp', 'fsdp'))
- out_seven: bfloat16 [64, 7, 7, 512], P(('dp', 'fsdp'))
- out_nine: bfloat16 [64, 9, 9, 512], P(('dp', 'fsdp'))
- grad_five: float32 [192, 5, 5, 512], P(('dp', 'fsdp'))
- grad_seven: float32 [64, 7, 7, 512], P(('dp', 'fsdp'))
- grad_nine: float32 [64, 9, 9, 512], P(('dp', 'fsdp'))
- kernels_next: float32 [2, 3, 3, 512, 512], P(None, None, None, None, 'fsdp')
- kernel_first_next: float32 [2, 3, 3, 512, 512], P(None, None, None, None, 'fsdp')
- kernel_second_next: float32 [2, 3, 3, 512, 512], P(None, None, None, None, 'fsdp')
- norm_next: float32 [4, 512], P(None, 'fsdp')
- norm_first_next: float32 [4, 512], P(None, 'fsdp')
- norm_second_next: float32 [4, 512], P(None, 'fsdp')
Inputs may be any that keep to these rules, and one draw needn't show every extreme that they name: `mask_five`: 1 marks a valid pixel; the valid pixels of an image form a rectangle at its top-left corner, which may be empty. `mask_seven`: 1 marks a valid pixel; the valid pixels of an image form a rectangle at its top-left corner, which may be empty. `mask_nine`: 1 marks a valid pixel; the valid pixels of an image form a rectangle at its top-left corner, which may be empty.
All inputs are finite; a program needn't handle non-finite values.
Results may differ from a plain program's by a relative error of at most 0.0097.
Values may be sent and summed in bfloat16 or wider, within the bound.
No kernel may reach another device: no remote copies, remote signals or barrier semaphores. Data moves between devices by JAX's collectives and lax.ppermute only.
A program may use at most 128 MiB of HBM per device.

v0:
```python
import functools

import jax
import jax.numpy as jnp
from jax import lax
from jax.experimental import pallas as pl
from jax.experimental.pallas import tpu as pltpu
from jax.sharding import Mesh, PartitionSpec as P

STEP = 5
NORM_EPS = 1e-05
BETA_ONE = 0.5
BETA_TWO = 0.5
KERNEL_RATE = 0.03
NORM_RATE = 0.4
KERNEL_DECAY = 0.01
ADAM_EPS = 1e-08
TAPS = 9
LANES = 128
CELL = 2
VMEM_BYTES = 53 * 1024 * 1024
F32, BF16 = jnp.float32, jnp.bfloat16


def round_up(value, step):
    return (value + step - 1) // step * step


class Canvas:
    def __init__(self, shapes):
        self.shapes = shapes
        cells = [
            (side, group, first)
            for group, (count, side) in enumerate(shapes)
            for first in range(0, count, CELL)
        ]
        limit = max(
            sum(side + 1 for side, group, _ in cells if group == wanted)
            for wanted in range(len(shapes))
        )
        self.bands = []
        for side, group, first in sorted(cells, reverse=True):
            used = sum(cell[0] + 1 for cell in self.bands[-1]) if self.bands else limit
            if used + side + 1 > limit:
                self.bands.append([])
            self.bands[-1].append((side, group, first))
        self.width = limit
        self.right = CELL
        self.down = limit * CELL
        self.heights = [band[0][0] for band in self.bands]
        used_rows = (sum(self.heights) + len(self.bands) - 1) * self.down
        self.rows = round_up(used_rows, 16)
        self.halo = round_up(self.down + self.right, 8)
        self.lanes = round_up(self.rows + self.down + self.right, LANES)
        self.padded_rows = self.rows + 2 * self.halo
        self.sent_rows = self.rows + 16

    def cells(self):
        start = 0
        for band, height in zip(self.bands, self.heights):
            column = 0
            for side, group, first in band:
                yield side, group, first, start * self.down + column * CELL
                column += side + 1
            start += height + 1

    def shift(self, tap):
        return (tap // 3 - 1) * self.down + (tap % 3 - 1) * self.right

    def place(self, buffer, value):
        edge = jnp.zeros((self.halo, value.shape[1]), F32)
        buffer[0 : self.halo, :] = edge
        buffer[self.halo : self.halo + self.rows, :] = value
        buffer[self.halo + self.rows :, :] = edge

    def shifted(self, buffer, tap, sign):
        start = self.halo + sign * self.shift(tap)
        return buffer[start : start + self.rows, :].astype(BF16)


def wide(mask, channels):
    return jnp.concatenate([mask[...]] * (channels // LANES), axis=1)


def multiply(left, right, left_dim, right_dim):
    return lax.dot_general(
        left, right, (((left_dim,), (right_dim,)), ((), ())), preferred_element_type=F32
    )


def column_sum(value):
    return jnp.sum(value, axis=0, keepdims=True)


def spread_rows(rows, ref):
    ref[...] = jnp.broadcast_to(jnp.concatenate(rows, axis=0)[None], ref.shape)


def local_statistics(hidden, valid, *refs):
    total = column_sum(hidden * valid)
    centre = total / jnp.maximum(column_sum(valid), 1.0)
    squares = column_sum(jnp.square(hidden - centre) * valid)
    rows = jnp.concatenate([total, squares], axis=0)
    *info, ref = [ref[...] for ref in refs[:-1]] + [refs[-1]]
    rows = jnp.concatenate([rows, *info], axis=1)
    ref[...] = jnp.broadcast_to(rows[None], ref.shape)


def global_statistics(gathered, counts):
    channels = counts.shape[1]
    totals, squares = gathered[:, 0, :channels], gathered[:, 1, :channels]
    total = column_sum(counts)
    centre = column_sum(totals) / total
    between = column_sum(counts * jnp.square(totals / jnp.maximum(counts, 1.0) - centre))
    spread = (column_sum(squares) + between) / total
    return centre, lax.rsqrt(spread + NORM_EPS), total


def lay_out(canvas, field_refs, buffer):
    buffer[...] = jnp.zeros_like(buffer)
    for side, group, first, start in canvas.cells():
        for down in range(side):
            for right in range(side):
                row = start + down * canvas.down + right * CELL
                pair = field_refs[group][down, right, first : first + CELL, :]
                buffer[row : row + CELL, :] = pair.astype(F32)


def prepare(canvas, *refs):
    *field_refs, param_ref = refs[:4]
    mask_refs = refs[4:7]
    x_ref, mask_ref, info_ref, buffer = refs[7:]
    rows, channels = buffer.shape
    mask_ref[...] = jnp.zeros_like(mask_ref)
    for side, group, first, start in canvas.cells():
        for down in range(side):
            for right in range(side):
                for image in range(CELL):
                    row = start + down * canvas.down + right * CELL + image
                    value = mask_refs[group][down, first + image, right].astype(F32)
                    mask_ref[row : row + 1, :] = jnp.full((1, LANES), value, F32)
    lay_out(canvas, field_refs, buffer)
    x_ref[0:rows, :] = (buffer[...] * wide(mask_ref, channels)).astype(BF16)
    line = jnp.transpose(mask_ref[...])[0:1]
    rest = jnp.zeros((1, channels * 2 - rows), F32)
    lines = [line[:, :channels], jnp.concatenate([line[:, channels:], rest], axis=1)]
    lines.append(jnp.zeros((14, channels), F32))
    x_ref[rows:, :] = jnp.concatenate(lines, axis=0).astype(BF16)
    params = param_ref[...].astype(BF16).astype(F32)
    rows = [params[index : index + 1] for index in range(4)]
    if params.size < LANES:
        rows.append(jnp.zeros((1, LANES - params.size), F32))
    row = jnp.concatenate(rows, axis=1)
    info_ref[...] = jnp.concatenate([row, column_sum(mask_ref[...])], axis=0)


def sent_mask(canvas, lines):
    channels = lines.shape[1]
    turned = jnp.transpose(lines)
    column = jnp.concatenate([turned[:, 0:1], turned[: canvas.rows - channels, 1:2]], axis=0)
    return jnp.broadcast_to(column, (canvas.rows, channels))


def prepare_back(canvas, *refs):
    *field_refs, back_ref, buffer = refs
    lay_out(canvas, field_refs, buffer)
    back_ref[...] = buffer[...].astype(BF16)


def sigmoid(value):
    return 1.0 / (1.0 + jnp.exp(-value))


def swish_slope(value):
    logistic = sigmoid(value)
    return logistic * (1.0 + value * (1.0 - logistic))


class Whole:
    def __init__(self, array, width):
        self.arrays = self.last = [array]
        self.width = width

    @staticmethod
    def start(refs, weight, sems):
        for part in range(3):
            taps = pl.ds(3 * part, 3)
            pltpu.make_async_copy(refs[0].at[taps], weight.at[taps], sems.at[part]).start()


class Pieces:
    width = 32

    def __init__(self, pieces):
        self.arrays = [array for array, _, _ in pieces]
        self.last = self.arrays[-4:]
        self.places = [(slots, first) for _, slots, first in pieces]

    def start(self, refs, weight, sems):
        y, z, x, c = (lax.axis_index(name) for name in ("y", "z", "x", "c"))
        moves = []
        for ref, (slots, first) in zip(refs, self.places):
            _, _, rows, lanes = ref.shape
            for slot, (dy, dz, dx, dc) in enumerate(slots):
                shard = ((z ^ dz) * 2 + (x ^ dx)) * 2 + (c ^ dc)
                row = pl.multiple_of(shard * self.width + first, 16)
                lane = 0 if dy is None else pl.multiple_of((y ^ dy) * lanes, lanes)
                moves.append((ref.at[slot], pl.ds(row, rows), pl.ds(lane, lanes)))
        for part in range(3):
            taps = pl.ds(3 * part, 3)
            for source, row, lane in moves:
                target = weight.at[taps, row, lane]
                pltpu.make_async_copy(source.at[taps], target, sems.at[part]).start()


class Fetch:
    def __init__(self, source, refs, weight, sems, target=None):
        self.weight, self.sems, self.target = weight, sems, target
        self.waiting = [0, 1, 2]
        source.start(refs, weight, sems)

    def ready(self, tap, when=None):
        if tap % 3 or not self.waiting:
            return
        part = self.waiting.pop(0)

        def wait():
            taps = self.weight.at[pl.ds(3 * part, 3)]
            pltpu.make_async_copy(taps, taps, self.sems.at[part]).wait()
            if not self.waiting and self.target is not None:
                pltpu.make_async_copy(self.weight, self.target, self.sems.at[0]).start()

        wait() if when is None else pl.when(when)(wait)

    def finish(self):
        pltpu.make_async_copy(self.weight, self.target, self.sems.at[0]).wait()


def convolve(canvas, value, fetch, buffer, out_ref, sign, halves=False, when=None):
    canvas.place(buffer, value)
    if not halves:
        for tap in range(TAPS):
            part = canvas.shifted(buffer, tap, sign)
            fetch.ready(tap, when)
            product = multiply(part, fetch.weight[tap], 1, 1 if sign > 0 else 0)
            out_ref[...] = product if tap == 0 else out_ref[...] + product
        return
    for tap in range(TAPS):
        fetch.ready(tap)
    width = out_ref.shape[1] // 2

    def half(index, carry):
        columns = pl.ds(pl.multiple_of(index * width, width), width)
        for tap in range(TAPS):
            part = canvas.shifted(buffer, tap, sign)
            weight = fetch.weight[tap, columns] if sign > 0 else fetch.weight[tap, :, columns]
            product = multiply(part, weight, 1, 1 if sign > 0 else 0)
            out_ref[:, columns] = product if tap == 0 else out_ref[:, columns] + product
        return carry

    lax.fori_loop(0, 2, half, 0)


def activate(hidden, norm_ref, param_ref, valid):
    normed = (hidden - norm_ref[0:1, :]) * norm_ref[1:2, :]
    value = normed * param_ref[0:1, :] + param_ref[1:2, :]
    return value * sigmoid(value) * valid


def side_active(canvas, source, count, *refs):
    norm_ref, param_ref, *refs = refs
    weights, refs = refs[: len(source.arrays)], refs[len(source.arrays) :]
    sent_hbm, refs = refs[:count], refs[count:]
    active_ref, *full, buffer, weight, sems, hidden, sent, sent_sem = refs
    copies = [
        pltpu.make_async_copy(hbm, sent.at[index], sent_sem) for index, hbm in enumerate(sent_hbm)
    ]
    for copy in copies:
        copy.start()
    fetch = Fetch(source, weights, weight, sems, *full)
    for copy in copies:
        copy.wait()

    def image(index, carry):
        pixels = sent[index].astype(F32)
        convolve(canvas, pixels[: canvas.rows], fetch, buffer, hidden, 1, when=index == 0)
        valid = sent_mask(canvas, pixels[canvas.rows :])
        active = activate(hidden[...], norm_ref, param_ref, valid)
        active_ref[index] = active.astype(BF16)
        return carry

    lax.fori_loop(0, count, image, 0)
    if full:
        fetch.finish()


def forward_one(canvas, source, x_ref, mask_ref, info_ref, *refs):
    *weights, hidden_ref, stats_ref, buffer, weight, sem = refs
    fetch = Fetch(source, weights, weight, sem)
    convolve(canvas, x_ref[0 : canvas.rows, :].astype(F32), fetch, buffer, hidden_ref, 1)
    local_statistics(hidden_ref[...], wide(mask_ref, x_ref.shape[1]), info_ref, stats_ref)


def forward_two(canvas, source, hidden_ref, gathered_ref, mask_ref, *refs):
    *weights, active_ref, second_ref, norm_ref, param_ref, count_ref, stats_ref = refs[:-3]
    buffer, weight, sem = refs[-3:]
    fetch = Fetch(source, weights, weight, sem)
    channels = hidden_ref.shape[1]
    valid = wide(mask_ref, channels)
    width = source.width
    rows = []
    for index in range(4):
        start = channels + index * width
        rows.append(
            jnp.concatenate(
                [gathered_ref[shard, 0:1, start : start + width] for shard in range(channels // width)],
                axis=1,
            )
        )
    param_ref[...] = jnp.concatenate(rows, axis=0)
    counts = gathered_ref[:, 1, channels : channels + LANES]
    count_ref[...] = jnp.concatenate([counts] * (channels // LANES), axis=1)

    centre, inv, total = global_statistics(gathered_ref, count_ref[...])
    norm_ref[...] = jnp.concatenate([centre, inv, total, total], axis=0)
    value = activate(hidden_ref[...], norm_ref, param_ref, valid)
    active_ref[...] = value.astype(BF16)
    convolve(canvas, value, fetch, buffer, second_ref, 1)
    local_statistics(second_ref[...], valid, stats_ref)


def turn(
    second_ref,
    gathered_ref,
    count_ref,
    param_ref,
    mask_ref,
    x_ref,
    back_ref,
    result_ref,
    grad_ref,
    norm_ref,
    stats_ref,
):
    valid = wide(mask_ref, second_ref.shape[1])
    centre, inv, total = global_statistics(gathered_ref, count_ref[...])
    norm_ref[...] = jnp.concatenate([centre, inv, total, total], axis=0)
    normed = (second_ref[...] - centre) * inv
    rows = second_ref.shape[0]
    summed = normed * param_ref[2:3, :] + param_ref[3:4, :] + x_ref[0:rows, :].astype(F32)
    logistic = sigmoid(summed)
    result_ref[...] = (summed * logistic * valid).astype(BF16)
    slope = logistic * (1.0 + summed * (1.0 - logistic))
    grad = back_ref[...].astype(F32) * valid * slope
    grad_ref[...] = grad
    spread_rows([column_sum(grad), column_sum(grad * normed)], stats_ref)


def norm_back(row, norm_ref, gathered_ref, param_ref, sums_ref, *turned_refs, moving):
    grad_in, hidden, mask, inner_out = moving
    channels = norm_ref.shape[1]
    shift_grad = column_sum(gathered_ref[:, 0, :])
    gain_grad = column_sum(gathered_ref[:, 1, :])
    sums_ref[...] = jnp.concatenate([gain_grad, shift_grad], axis=0)
    centre, inv, total = norm_ref[0:1, :], norm_ref[1:2, :], norm_ref[2:3, :]
    gain = param_ref[row : row + 1, :] * inv
    full = turned_refs[-1]
    for part, (start, stop) in enumerate(inner_out.spans):
        normed = (hidden.part(part) - centre) * inv
        grad = grad_in.part(part) - shift_grad / total - normed * (gain_grad / total)
        inner = wide(mask.part(part), channels) * gain * grad
        inner_out.put(part, inner.astype(BF16))
        full[:, start:stop] = jnp.transpose(inner).astype(BF16)
    if len(turned_refs) == 1:
        return
    rows = inner_out.spans[-1][1]
    full[:, rows:] = jnp.zeros((channels, full.shape[1] - rows), BF16)
    y, x = lax.axis_index("y"), lax.axis_index("x")
    half = channels // 32
    for index, turned_ref in enumerate(turned_refs[:-1]):
        for c in range(2):
            for z in range(4):
                shard = (z * 2 + (x ^ (index % 2))) * 2 + c
                start = pl.multiple_of((shard * 2 + (y ^ (index // 2))) * half, half)
                turned_ref[c, z * half : (z + 1) * half, :] = full[pl.ds(start, half), :]


def backward_middle(canvas, source, inner_ref, hidden_ref, norm_ref, param_ref, mask_ref, *refs):
    *weights, grad_ref, stats_ref, buffer, weight, sem = refs
    valid = wide(mask_ref, hidden_ref.shape[1])
    fetch = Fetch(source, weights, weight, sem)
    convolve(canvas, inner_ref[...].astype(F32), fetch, buffer, grad_ref, -1)
    normed = (hidden_ref[...] - norm_ref[0:1, :]) * norm_ref[1:2, :]
    value = normed * param_ref[0:1, :] + param_ref[1:2, :]
    grad = grad_ref[...] * valid * swish_slope(value)
    grad_ref[...] = grad
    spread_rows([column_sum(grad), column_sum(grad * normed)], stats_ref)


def lay_back(canvas, flat, refs):
    for side, group, first, start in canvas.cells():
        for down in range(side):
            for right in range(side):
                row = start + down * canvas.down + right * CELL
                pair = flat[row : row + CELL, :].astype(refs[group].dtype)
                refs[group][down, right, first : first + CELL, :] = pair


def backward_input(canvas, source, inner_ref, residual_ref, mask_ref, result_ref, *refs):
    weights, refs = refs[: len(source.arrays)], refs[len(source.arrays) :]
    result_refs, grad_refs, (buffer, weight, sem, flat) = refs[:3], refs[3:6], refs[6:]
    fetch = Fetch(source, weights, weight, sem)
    convolve(canvas, inner_ref[...].astype(F32), fetch, buffer, flat, -1, True)
    flat[...] = residual_ref[...] + wide(mask_ref, flat.shape[1]) * flat[...]
    lay_back(canvas, flat, grad_refs)
    flat[...] = result_ref[...].astype(F32)
    lay_back(canvas, flat, result_refs)


def kernel_grad_whole(canvas, turned_ref, active_ref, out_ref, buffer):
    canvas.place(buffer, active_ref[0 : canvas.rows, :].astype(F32))
    for tap in range(TAPS):
        product = multiply(turned_ref[...], canvas.shifted(buffer, tap, 1), 1, 0)
        out_ref[tap] = product.astype(out_ref.dtype)


def kernel_grad_layer(canvas, *refs):
    turned_hbm, refs = refs[:4], refs[4:]
    active_hbm, (send_hbm, keep_hbm) = refs[:-9], refs[-9:-7]
    turned_ref, active_ref, left, total, send_ref, keep_ref, sems = refs[-7:]
    if len(active_hbm) < 4:
        own, pair, last = active_hbm
        active_hbm = (own, pair.at[0], pair.at[1], last.at[0])
    z, c = lax.axis_index("z"), lax.axis_index("c")
    rows, part = canvas.rows, turned_ref.shape[2]
    half = part // 4
    turns, copies = [], []
    for index, hbm in enumerate(turned_hbm):
        turns.append(pltpu.make_async_copy(hbm, turned_ref.at[index], sems.at[index]))
    for index, hbm in enumerate(active_hbm):
        target = active_ref.at[index, pl.ds(0, hbm.shape[0])]
        copies.append(pltpu.make_async_copy(hbm, target, sems.at[4 + index]))
    for pair in zip(turns, copies):
        for copy in pair:
            copy.start()
    def half_sum(core, wait):
        for index in range(4):
            slot = index % 2
            if wait:
                pl.when(core == 1)(turns[index].wait)
            turned = turned_ref[index, c ^ core].astype(F32)
            for tap in range(TAPS):
                shift = canvas.shift(tap) % canvas.lanes
                moved = pltpu.roll(turned, shift, 1) if shift else turned
                left[slot, tap * part : (tap + 1) * part, :] = moved[:, :rows].astype(BF16)
            if wait:
                pl.when(core == 1)(copies[index].wait)
            product = multiply(left[slot], active_ref[index, 0:rows, :], 1, 0)
            total[...] = product if index == 0 else total[...] + product

    def spread(ref):
        for tap in range(TAPS):
            for place in range(4):
                row = tap * part + (z ^ place) * half
                ref[place, tap] = total[pl.ds(row, half), :].astype(ref.dtype)

    send = pltpu.make_async_copy(send_ref, send_hbm, sems.at[8])
    keep = pltpu.make_async_copy(keep_ref, keep_hbm, sems.at[9])

    def both(step, carry):
        half_sum(1 - step, True)

        @pl.when(step == 0)
        def _():
            spread(send_ref)
            send.start()

        return carry

    lax.fori_loop(0, 2, both, 0)
    spread(keep_ref)
    keep.start()
    send.wait()
    keep.wait()


class Moving:
    def __init__(self, hbm, ref, sems, bounds, inward):
        self.ref, self.spans = ref, list(zip(bounds[:-1], bounds[1:]))
        self.copies, self.waited = [], set()
        for index, (start, stop) in enumerate(self.spans):
            far, near = hbm.at[pl.ds(start, stop - start)], ref.at[pl.ds(start, stop - start)]
            ends = (far, near) if inward else (near, far)
            self.copies.append(pltpu.make_async_copy(*ends, sems.at[index]))

    def start(self, index):
        self.copies[index].start()

    def part(self, index):
        if index not in self.waited:
            self.waited.add(index)
            self.copies[index].wait()
        start, stop = self.spans[index]
        return self.ref[start:stop, :]

    def put(self, index, value):
        start, stop = self.spans[index]
        self.ref[start:stop, :] = value
        self.copies[index].start()


def call(
    body,
    inputs,
    outputs,
    scratch=(),
    weights=(),
    after=(),
    scalars=(),
    kept=(),
    late=(),
    streams=(),
    bounds=(),
):
    whole = pl.BlockSpec(memory_space=pltpu.VMEM)
    anywhere = pl.BlockSpec(memory_space=pltpu.HBM)
    read = len(inputs) + len(scalars) + len(weights)
    moved = [(array.shape, array.dtype) for array in late] + list(streams)
    results = (*outputs, *kept, *streams)

    def split(refs, *counts):
        groups = []
        for count in counts:
            groups.append(refs[:count])
            refs = refs[count:]
        return groups

    def kernel(*refs):
        ins, far, _, outs, out_far, scratch_refs, near, sems = split(
            refs,
            read,
            len(late),
            len(after),
            len(outputs) + len(kept),
            len(streams),
            len(scratch),
            len(moved),
            len(moved),
        )
        if not moved:
            return body(*ins, *outs, *scratch_refs)
        moving = [
            Moving(hbm, ref, sem, bounds, index < len(late))
            for index, (hbm, ref, sem) in enumerate(zip((*far, *out_far), near, sems))
        ]
        for part in range(len(bounds) - 1 if len(bounds) > 2 else 0):
            for mover in moving[: len(late)]:
                mover.start(part)
        body(*ins, *outs, *scratch_refs, moving=moving)
        for mover in moving[len(late) :]:
            for copy in mover.copies:
                copy.wait()

    return pl.pallas_call(
        kernel,
        out_shape=[jax.ShapeDtypeStruct(shape, dtype) for shape, dtype in results],
        in_specs=[whole] * len(inputs)
        + [pl.BlockSpec(memory_space=pltpu.SMEM)] * len(scalars)
        + [anywhere] * (len(weights) + len(late) + len(after)),
        out_specs=[whole] * len(outputs) + [anywhere] * (len(kept) + len(streams)),
        scratch_shapes=list(scratch)
        + [pltpu.VMEM(shape, dtype) for shape, dtype in moved]
        + [pltpu.SemaphoreType.DMA((len(bounds) - 1,)) for _ in moved],
        compiler_params=pltpu.CompilerParams(vmem_limit_bytes=VMEM_BYTES),
    )(*inputs, *scalars, *weights, *late, *after)


def adamw(param, grad, first, second, rate, decay):
    first_new = BETA_ONE * first + (1.0 - BETA_ONE) * grad
    second_new = BETA_TWO * second + (1.0 - BETA_TWO) * grad * grad
    first_hat = first_new / (1.0 - BETA_ONE**STEP)
    second_hat = second_new / (1.0 - BETA_TWO**STEP)
    update = first_hat / (jnp.sqrt(second_hat) + ADAM_EPS)
    return (param - rate * (update + decay * param), first_new, second_new)


def flip(value, axis, bit, size):
    return lax.ppermute(value, axis, [(place, place ^ bit) for place in range(size)])


def diagonal(value):
    return lax.ppermute(value, ("y", "x"), [(place, place ^ 3) for place in range(4)])


def behind(value, others):
    return lax.optimization_barrier((value, *others))[0] if others else value


class Gather:
    def __init__(self, shard, half):
        self.shard, self.half = shard[None], half[None]

    def along_two(self, *others):
        self.second = flip(behind(self.half, others), "z", 2, 4)

    def beside(self, *others):
        self.nearest = flip(behind(self.shard, others), "x", 1, 2)

    def along_one(self, *others):
        both = jnp.concatenate([self.half, self.second], axis=0)
        self.line = flip(behind(both, others), "z", 1, 4)

    def across(self, *others):
        self.rest = rest = behind(jnp.concatenate([self.second, self.line], axis=0), others)
        self.over = flip(rest, "x", 1, 2), flip(rest, "y", 1, 2)

    def direct(self):
        self.corners = (diagonal(self.rest),)

    def corner(self, *others):
        rows = self.shard.shape[2] // 2
        over_x, over_y = self.over
        corners = (
            flip(behind(over_y[:, :, :rows], others), "x", 1, 2),
            flip(behind(over_x[:, :, rows:], others), "y", 1, 2),
        )
        self.corners = lax.optimization_barrier(corners)

    def cores(self, early=(), late=()):
        rows = self.shard.shape[2] // 2
        deep = (2, 1, 3)
        pieces = [
            (self.shard, [(None, 0, 0)], 0),
            (self.nearest, [(None, 0, 1)], 0),
            (self.rest, [(0, dz, 0) for dz in deep], 0),
            (self.over[0], [(0, dz, 1) for dz in deep], 0),
            (self.over[1], [(1, dz, 0) for dz in deep], 0),
        ]
        for index, array in enumerate(self.corners):
            pieces.append((array, [(1, dz, 1) for dz in deep], index * rows))
        self.found = []
        for index, (array, slots, first) in enumerate(pieces):
            others = late if index > 4 else early if index > 2 else ()
            other = flip(behind(array, others), "c", 1, 2)
            self.found.append((array, [slot + (0,) for slot in slots], first))
            self.found.append((other, [slot + (1,) for slot in slots], first))


class Grid:
    axes = ("y", "z", "x", "c")
    shard_axes = ("z", "x", "c")

    def weights(self, low, x, back):
        half = low.shape[3] // 2
        first, second = lax.dynamic_slice_in_dim(low, lax.axis_index("y") * half, half, 3)
        one, two = Gather(low[0], first), Gather(low[1], second)
        one.along_two()
        one.beside()
        self.pixels = x
        self.sides = flip(x, "x", 1, 2), flip(x, "y", 1, 2)
        one.along_one(x, one.nearest)
        two.along_two(one.line)
        one.across(back, *self.sides)
        two.along_one(*one.over)
        two.beside(*self.sides)
        one.corner()
        one.cores()
        two.across(two.nearest, *one.corners)
        two.direct()
        self.second = two
        return Pieces(one.found)

    def second_weights(self, stats, gathered, *others):
        self.second.cores((stats,), (gathered, *others))
        self.corners = (diagonal(behind(self.pixels, (stats,))),)
        return Pieces(self.second.found)

    def turned_shapes(self, canvas, channels):
        return (((2, channels // 8, canvas.lanes), BF16),) * 4

    def turned_scratch(self, canvas, channels):
        return (pltpu.VMEM((channels, canvas.lanes), BF16),)

    def send(self, own, over_x, over_y, corner):
        return own, flip(over_x, "x", 1, 2), flip(over_y, "y", 1, 2), diagonal(corner)

    def chip_sum(self, canvas, moved, layer, channels, after):
        out = (4, TAPS, channels // 32, channels)
        part = moved[0].shape[1]
        send, keep = call(
            functools.partial(kernel_grad_layer, canvas),
            (),
            (),
            (
                pltpu.VMEM((4, *moved[0].shape), BF16),
                pltpu.VMEM((4, canvas.sent_rows, channels), BF16),
                pltpu.VMEM((2, TAPS * part, canvas.rows), BF16),
                pltpu.VMEM((TAPS * part, channels), F32),
                pltpu.VMEM(out, BF16),
                pltpu.VMEM(out, F32),
                pltpu.SemaphoreType.DMA((10,)),
            ),
            (*moved, *layer),
            after,
            kept=((out, BF16), (out, F32)),
        )
        return send, keep

    def core_sum(self, chip, *others):
        send, keep = chip
        chip = keep + flip(behind(send, others), "c", 1, 2).astype(F32)
        return chip[0], *[chip[place].astype(BF16) for place in range(1, 4)]

    def line(self, parts):
        return [flip(part, "z", place, 4) for place, part in enumerate(parts[1:], 1)]

    def line_sum(self, parts, found, *others):
        total = behind(parts[0], others)
        for part in found:
            total = total + part.astype(F32)
        return total

    def owned(self, line):
        own = line.astype(BF16)
        other = flip(own, "y", 1, 2)
        first = lax.axis_index("y") == 0
        halves = [jnp.where(first, own, other), jnp.where(first, other, own)]
        return jnp.concatenate(halves, axis=1).astype(F32)


class Plain:
    axes = ("dp", "fsdp")
    shard_axes = ("fsdp",)

    sides = corners = ()

    def weights(self, low, x, back):
        full = lax.all_gather(low, "fsdp", axis=2, tiled=True)
        first, self.second = [Whole(array, low.shape[2]) for array in full]
        return first

    def second_weights(self, stats, gathered, *others):
        return self.second

    def turned_shapes(self, canvas, channels):
        return (((channels, canvas.rows), BF16),)

    def turned_scratch(self, canvas, channels):
        return ()

    def send(self, turned):
        return (turned,)

    def chip_sum(self, canvas, moved, layer, channels, after):
        (full,) = call(
            functools.partial(kernel_grad_whole, canvas),
            (*moved, layer[0]),
            (((TAPS, channels, channels), BF16),),
            (pltpu.VMEM((canvas.padded_rows, channels), F32),),
            after=after,
        )
        return (full,)

    def core_sum(self, chip, *others):
        return chip

    def line(self, parts):
        return ()

    def line_sum(self, parts, found, *others):
        return lax.psum_scatter(parts[0], "fsdp", scatter_dimension=1, tiled=True)

    def owned(self, line):
        return lax.psum(line, "dp").astype(F32)


def local(
    ways,
    sizes,
    field_five,
    field_seven,
    field_nine,
    mask_five,
    mask_seven,
    mask_nine,
    back_five,
    back_seven,
    back_nine,
    kernels,
    norm_params,
    kernel_first,
    kernel_second,
    norm_first,
    norm_second,
):
    copies, shards = sizes
    fields = (field_five, field_seven, field_nine)
    masks = (mask_five, mask_seven, mask_nine)
    backs = (back_five, back_seven, back_nine)
    channels = field_five.shape[3]
    width = kernels.shape[4]
    canvas = Canvas([(field.shape[0], field.shape[1]) for field in fields])
    rows = canvas.rows
    count = copies * shards

    def turned(kernel):
        return jnp.transpose(kernel, (0, 1, 2, 4, 3)).reshape(2, TAPS, width, channels)

    def exchange(spread):
        return lax.all_to_all(spread, ways.axes, 0, 0, tiled=True)

    kernels_turned = turned(kernels)
    low = kernels_turned.astype(BF16)

    buffer = pltpu.VMEM((rows, channels), F32)
    weighted = (
        pltpu.VMEM((canvas.padded_rows, channels), F32),
        pltpu.VMEM((TAPS, channels, channels), BF16),
        pltpu.SemaphoreType.DMA((3,)),
    )
    flat32 = ((rows, channels), F32)
    flat16 = ((rows, channels), BF16)
    two = ((count, 2, channels), F32)
    norm = ((4, channels), F32)
    sums = ((2, channels), F32)
    turned_shapes = ways.turned_shapes(canvas, channels)
    turned_scratch = ways.turned_scratch(canvas, channels)

    full = ((TAPS, channels, channels), BF16)

    bounds = (*range(0, rows - LANES, LANES), rows)

    bounds = (*range(0, rows - LANES, LANES), rows)

    def conv_call(body, source, inputs, outputs, after=()):
        return call(
            functools.partial(body, canvas, source),
            inputs,
            outputs,
            weighted,
            source.arrays,
            after,
        )

    x, mask, info = call(
        functools.partial(prepare, canvas),
        (*[jnp.transpose(field, (1, 2, 0, 3)) for field in fields], norm_params),
        (((canvas.sent_rows, channels), BF16), ((rows, LANES), F32), ((2, LANES), F32)),
        (buffer,),
        scalars=[jnp.transpose(mask, (1, 0, 2)) for mask in masks],
    )
    (back,) = call(
        functools.partial(prepare_back, canvas),
        [jnp.transpose(field, (1, 2, 0, 3)) for field in backs],
        (flat16,),
        (buffer,),
    )
    weight_one = ways.weights(low, x, back)
    sides = ways.sides
    hidden, stats = conv_call(
        forward_one,
        weight_one,
        (x, mask, info),
        (flat32, ((count, 2, channels + LANES), F32)),
        after=sides,
    )
    gathered = exchange(stats)
    side = ()
    weight_two = ways.second_weights(stats, gathered, *side)
    active, second, norm_one, params, counts, stats = conv_call(
        forward_two,
        weight_two,
        (hidden, gathered, mask),
        (flat16, flat32, norm, norm, ((count, channels), F32), two),
        after=side,
    )
    gathered = exchange(stats)
    actives = (active,)

    def side_call(sent, after, kept=()):
        return call(
            functools.partial(side_active, canvas, weight_one, len(sent)),
            (norm_one, params),
            (((len(sent), rows, channels), BF16),),
            (
                *weighted,
                pltpu.VMEM((rows, channels), F32),
                pltpu.VMEM((len(sent), canvas.sent_rows, channels), BF16),
                pltpu.SemaphoreType.DMA,
            ),
            (*weight_one.arrays, *sent),
            after,
            kept=kept,
        )

    if sides:
        found, full_one = side_call(sides, (stats,), (full,))
        weight_one = Whole(full_one, weight_one.width)
        actives += (found,)
    result, grad_sum, norm_two, stats = call(
        turn,
        (second, gathered, counts, params, mask, x, back),
        (flat16, flat32, norm, two),
        after=actives[1:],
    )
    gathered = exchange(stats)
    if sides:
        actives += tuple(side_call(ways.corners, (stats,)))
    sums_two, *turned_two, inner_two = call(
        functools.partial(norm_back, 2),
        (norm_two, gathered, params),
        (sums, *turned_shapes),
        turned_scratch,
        late=(grad_sum, second, mask),
        streams=(flat16,),
        bounds=bounds,
        after=actives[2:],
    )
    moved_two = ways.send(*turned_two)
    grad_hidden, stats = conv_call(
        backward_middle, weight_two, (inner_two, hidden, norm_one, params, mask), (flat32, two)
    )
    gathered = exchange(behind(stats, moved_two[1:]))
    chip_two = ways.chip_sum(canvas, moved_two, actives, channels, (grad_hidden,))
    layer_x = (x, *sides, *ways.corners)
    sums_one, *turned_one, inner_one = call(
        functools.partial(norm_back, 0),
        (norm_one, gathered, params),
        (sums, *turned_shapes),
        turned_scratch,
        late=(grad_hidden, hidden, mask),
        streams=(flat16,),
        bounds=bounds,
        after=chip_two,
    )
    moved_one = ways.send(*turned_one)
    core_two = ways.core_sum(chip_two, gathered)
    line_two = ways.line(core_two)
    chip_one = ways.chip_sum(canvas, moved_one, layer_x, channels, core_two[1:])
    core_one = ways.core_sum(chip_one, *line_two)
    shapes = [(side, side, images, channels) for images, side in canvas.shapes]
    finished = call(
        functools.partial(backward_input, canvas, weight_one),
        (inner_one, grad_sum, mask, result),
        [(shape, BF16) for shape in shapes] + [(shape, F32) for shape in shapes],
        (*weighted, buffer),
        weight_one.arrays,
        core_one,
    )
    owned_two = ways.owned(ways.line_sum(core_two, line_two, finished[0]))
    owned_one = ways.owned(ways.line_sum(core_one, ways.line(core_one), finished[0]))

    results = adamw(
        kernels_turned,
        jnp.stack([owned_one, owned_two]),
        turned(kernel_first),
        turned(kernel_second),
        KERNEL_RATE,
        KERNEL_DECAY,
    )
    kernel_results = [
        jnp.transpose(value.reshape(2, 3, 3, width, channels), (0, 1, 2, 4, 3))
        for value in results
    ]
    norm_full = jnp.concatenate([behind(sums_one, finished[:1]), sums_two], axis=0)
    place = lax.axis_index(ways.shard_axes) * width
    norm_grads = lax.dynamic_slice_in_dim(norm_full, place, width, 1)
    norm_results = adamw(norm_params, norm_grads, norm_first, norm_second, NORM_RATE, 0.0)
    return (
        *[jnp.transpose(array, (2, 0, 1, 3)) for array in finished],
        *kernel_results,
        *norm_results,
    )


def solution(mesh):
    sizes = (mesh.shape["dp"], mesh.shape["fsdp"])
    if sizes == (2, 16):
        ways = Grid()
        mesh = Mesh(mesh.devices.reshape(2, 4, 2, 2), ways.axes)
    else:
        ways = Plain()
    images = P(ways.axes, None, None, None)
    maps = P(ways.axes, None, None)
    weights = P(None, None, None, None, ways.shard_axes)
    norms = P(None, ways.shard_axes)
    in_specs = (
        (images,) * 3 + (maps,) * 3 + (images,) * 3 + (weights, norms, weights, weights, norms, norms)
    )
    out_specs = (images,) * 6 + (weights,) * 3 + (norms,) * 3
    body = functools.partial(local, ways, sizes)
    return jax.shard_map(body, mesh=mesh, in_specs=in_specs, out_specs=out_specs, check_vma=False)
```

profile of v0, /device:TPU:0, one launch (start us, length us, event | category | flops | bytes accessed | tf_op | source)
XLA Modules:
  0.0 197.3 jit_solution(3397117395206232365)
XLA Ops:
  0.6 1.4 bitcast_convert_fusion
  2.2 3.0 %collective-permute-start.1 = (bf16[1,9,32,512]{3,2,1,0:T(8,128)(2,1)S(1)}, bf16[1,9,32,512]{3,2,1,0:T(8,128)(2,1)S(1)}, u32[]{:S(2)}, u32[]{:S(2)}) collective-permute-start(bf16[1,9,32,512]{3,2,1,0:T(8,128)(2,1)S(1)} %bitcast.82), channel_id=1, source_target_pairs={{0,2},{2,0},{1,3},{3,1},{4,6},{6,4},{5,7},{7,5},{8,10},{10,8},{9,1... | collective-permute-start | bytes 884744 | tf_op jit(solution)/shard_map/ppermute | solution.py:588
  5.2 2.7 %collective-permute-start.3 = (bf16[1,9,32,256]{3,2,1,0:T(8,128)(2,1)S(1)}, bf16[1,9,32,256]{3,2,1,0:T(8,128)(2,1)S(1)}, u32[]{:S(2)}, u32[]{:S(2)}) collective-permute-start(bf16[1,9,32,256]{3,2,1,0:T(8,128)(2,1)S(1)} %get-tuple-element.147), channel_id=1, source_target_pairs={{0,8},{4,12},{8,0},{12,4},{1,9},{5,13},{9,1},{13,5},{2,10},{6,14},... | collective-permute-start | bytes 442376 | tf_op jit(solution)/shard_map/ppermute | solution.py:588
  7.9 2.6 %shard_map.238 = (bf16[560,512]{1,0:T(8,128)(2,1)}, f32[544,128]{1,0:T(8,128)S(1)}, f32[2,128]{1,0:T(2,128)S(1)}) custom-call(bf16[5,5,6,512]{3,2,1,0:T(8,128)(2,1)S(1)} %bitcast.72, bf16[7,7,2,512]{3,2,1,0:T(2,128)(2,1)S(1)} %bitcast.76, bf16[9,9,2,512]{3,2,1,0:T(2,128)(2,1)S(1)} %bitcast.75, f32[4,32]{1,0:T(4,128)S(1)} %copy-done.13, ...), custom_call_target="tpu_custom_call" | custom-call | tf_op jit(solution)/shard_map/pallas_call | solution.py:564
  11.1 1.5 collective-permute-start.6
  12.6 2.1 %collective-permute-done.3 = bf16[1,9,32,256]{3,2,1,0:T(8,128)(2,1)S(1)} collective-permute-done((bf16[1,9,32,256]{3,2,1,0:T(8,128)(2,1)S(1)}, bf16[1,9,32,256]{3,2,1,0:T(8,128)(2,1)S(1)}, u32[]{:S(2)}, u32[]{:S(2)}) %collective-permute-start.3) | collective-permute-done | bytes 147488 | tf_op jit(solution)/shard_map/ppermute | solution.py:588
  14.7 0.7 collective-permute-start.4
  15.5 1.2 shard_map.239.refs_6_
  16.7 6.0 %collective-permute-done.4 = bf16[2,9,32,256]{3,2,1,0:T(8,128)(2,1)S(1)} collective-permute-done((bf16[2,9,32,256]{3,2,1,0:T(8,128)(2,1)S(1)}, bf16[2,9,32,256]{3,2,1,0:T(8,128)(2,1)S(1)}, u32[]{:S(2)}, u32[]{:S(2)}) %collective-permute-start.4) | collective-permute-done | bytes 294944 | tf_op jit(solution)/shard_map/ppermute | solution.py:588
  22.7 2.2 %collective-permute-done.5.refs_17_.refs_16_.refs_5_ = bf16[560,512]{1,0:T(8,128)(2,1)S(1)} collective-permute-done((bf16[560,512]{1,0:T(8,128)(2,1)}, bf16[560,512]{1,0:T(8,128)(2,1)S(1)}, u32[]{:S(2)}, u32[]{:S(2)}) %collective-permute-start.5) | collective-permute-done | bytes 573472 | tf_op jit(solution)/shard_map/ppermute | solution.py:588
  25.2 1.5 collective-permute-start.10
  26.7 1.5 collective-permute-start.8
  28.2 2.2 %collective-permute-start.19 = (bf16[1,9,32,256]{3,2,1,0:T(8,128)(2,1)S(1)}, bf16[1,9,32,256]{3,2,1,0:T(8,128)(2,1)S(1)}, u32[]{:S(2)}, u32[]{:S(2)}) collective-permute-start(bf16[1,9,32,256]{3,2,1,0:T(8,128)(2,1)S(1)} %get-tuple-element.81), channel_id=1, source_target_pairs={{0,8},{4,12},{8,0},{12,4},{1,9},{5,13},{9,1},{13,5},{2,10},{6,14},... | collective-permute-start | bytes 442376 | tf_op jit(solution)/shard_map/ppermute | solution.py:588
  30.6 4.8 %collective-permute-done.10.refs_11_.refs_10_ = bf16[3,9,32,256]{3,2,1,0:T(8,128)(2,1)S(1)} collective-permute-done((bf16[3,9,32,256]{3,2,1,0:T(8,128)(2,1)S(1)}, bf16[3,9,32,256]{3,2,1,0:T(8,128)(2,1)S(1)}, u32[]{:S(2)}, u32[]{:S(2)}) %collective-permute-start.10) | collective-permute-done | bytes 442400 | tf_op jit(solution)/shard_map/ppermute | solution.py:588
  35.4 2.1 %collective-permute-start.17 = (bf16[1,9,32,512]{3,2,1,0:T(8,128)(2,1)S(1)}, bf16[1,9,32,512]{3,2,1,0:T(8,128)(2,1)S(1)}, u32[]{:S(2)}, u32[]{:S(2)}) collective-permute-start(bf16[1,9,32,512]{3,2,1,0:T(8,128)(2,1)S(1)} %bitcast.68), channel_id=1, source_target_pairs={{0,2},{2,0},{1,3},{3,1},{4,6},{6,4},{5,7},{7,5},{8,10},{10,8},{9,1... | collective-permute-start | bytes 884744 | tf_op jit(solution)/shard_map/ppermute | solution.py:588
  37.7 1.7 collective-permute-start.12
  39.6 1.6 collective-permute-start.20
  41.3 6.8 %collective-permute-done.12.refs_13_.refs_12_ = bf16[3,9,16,256]{3,2,1,0:T(8,128)(2,1)S(1)} collective-permute-done((bf16[3,9,16,256]{3,2,1,0:T(8,128)(2,1)S(1)}, bf16[3,9,16,256]{3,2,1,0:T(8,128)(2,1)S(1)}, u32[]{:S(2)}, u32[]{:S(2)}) %collective-permute-start.12) | collective-permute-done | bytes 221216 | tf_op jit(solution)/shard_map/ppermute | solution.py:588
  49.2 0.8 collective-permute-start.24
  50.0 0.8 collective-permute-done.14.refs_14_.refs_13_
  50.8 1.7 collective-permute-start.22
  54.0 6.6 %shard_map.240 = (f32[544,512]{1,0:T(8,128)}, f32[32,2,640]{2,1,0:T(2,128)}) custom-call(bf16[560,512]{1,0:T(8,128)(2,1)} %get-tuple-element.97.refs_0_.refs_5_.refs_4_, f32[544,128]{1,0:T(8,128)} %copy-done, f32[2,128]{1,0:T(2,128)S(1)} %get-tuple-element.73.refs_2_, bf16[1,9,32,512]{3,2,1,0:T(8,128)(2,1)} %bitcast.84, bf16[1,9,32,512]{3,2,1,0:T(8,128)(2,1)} %copy-done.34, ...), custom_call_target="tpu_custom_call" | custom-call | tf_op jit(solution)/shard_map/pallas_call | solution.py:564
  60.6 5.7 %all-to-all-start = ((f32[32,2,640]{2,1,0:T(2,128)}), f32[32,2,640]{2,1,0:T(2,128)S(1)}, u32[]{:S(2)}, u32[]{:S(2)}) async-start(f32[32,2,640]{2,1,0:T(2,128)} %get-tuple-element.79), calls=%async_computation | async-start | bytes 327680 | tf_op jit(solution)/shard_map/all_to_all | solution.py:810
  67.4 6.8 %collective-permute-done.26.refs_13_.refs_15_ = bf16[3,9,32,256]{3,2,1,0:T(8,128)(2,1)} collective-permute-done((bf16[3,9,32,256]{3,2,1,0:T(8,128)(2,1)S(1)}, bf16[3,9,32,256]{3,2,1,0:T(8,128)(2,1)}, u32[]{:S(2)}, u32[]{:S(2)}) %collective-permute-start.26) | collective-permute-done | bytes 442400 | tf_op jit(solution)/shard_map/ppermute | solution.py:592
  75.3 1.8 collective-permute-done.18.refs_6_.refs_8_
  77.1 2.0 %collective-permute-start.28 = (bf16[560,512]{1,0:T(8,128)(2,1)S(1)}, bf16[560,512]{1,0:T(8,128)(2,1)S(1)}, u32[]{:S(2)}, u32[]{:S(2)}) collective-permute-start(bf16[560,512]{1,0:T(8,128)(2,1)S(1)} %copy-done.17), channel_id=1, source_target_pairs={{0,18},{2,16},{16,2},{18,0},{1,19},{3,17},{17,3},{19,1},{4,22},{6,... | collective-permute-start | bytes 1720328 | tf_op jit(solution)/shard_map/ppermute | solution.py:592
  79.2 0.8 copy-done.31
  79.9 7.0 %shard_map.241 = (bf16[544,512]{1,0:T(8,128)(2,1)}, f32[544,512]{1,0:T(8,128)}, f32[4,512]{1,0:T(4,128)S(1)}, f32[4,512]{1,0:T(4,128)S(1)}, f32[32,512]{1,0:T(8,128)S(1)}, /*index=5*/f32[32,2,512]{2,1,0:T(2,128)}) custom-call(f32[544,512]{1,0:T(8,128)} %get-tuple-element.78.refs_0_.refs_1_.refs_4_, f32[32,2,640]{2,1,0:T(2,128)S(1)} %all-to-all-done.refs_1_, ...), custom_call_target="tpu_custom_call" | custom-call | tf_op jit(solution)/shard_map/pallas_call | solution.py:564
  86.9 4.3 %all-to-all-start.1 = ((f32[32,2,512]{2,1,0:T(2,128)}), f32[32,2,512]{2,1,0:T(2,128)S(1)}, u32[]{:S(2)}, u32[]{:S(2)}) async-start(f32[32,2,512]{2,1,0:T(2,128)} %get-tuple-element.89.refs_18_), calls=%async_computation.1 | async-start | bytes 262144 | tf_op jit(solution)/shard_map/all_to_all | solution.py:810
  91.2 9.5 %shard_map.242 = (bf16[2,544,512]{2,1,0:T(8,128)(2,1)}, bf16[9,512,512]{2,1,0:T(8,128)(2,1)}) custom-call(f32[4,512]{1,0:T(4,128)S(1)} %get-tuple-element.87.refs_0_.refs_2_, f32[4,512]{1,0:T(4,128)S(1)} %get-tuple-element.91.refs_1_.refs_3_.refs_2_, bf16[1,9,32,512]{3,2,1,0:T(8,128)(2,1)} %bitcast.85, bf16[1,9,32,512]{3,2,1,0:T(8,128)(2,1)} %copy-done.34, ...), custom_call_target="tpu_custom_call" | custom-call | tf_op jit(solution)/shard_map/pallas_call | solution.py:564
  100.8 3.6 %shard_map.243 = (bf16[544,512]{1,0:T(8,128)(2,1)}, f32[544,512]{1,0:T(8,128)}, f32[4,512]{1,0:T(4,128)S(1)}, f32[32,2,512]{2,1,0:T(2,128)}) custom-call(f32[544,512]{1,0:T(8,128)} %get-tuple-element.88.refs_0_.refs_4_, f32[32,2,512]{2,1,0:T(2,128)S(1)} %all-to-all-done.1.refs_1_, f32[32,512]{1,0:T(8,128)S(1)} %get-tuple-element.90.refs_2_, ...), custom_call_target="tpu_custom_call" | custom-call | tf_op jit(solution)/shard_map/pallas_call | solution.py:564
  104.4 5.7 %all-to-all-start.2 = ((f32[32,2,512]{2,1,0:T(2,128)}), f32[32,2,512]{2,1,0:T(2,128)S(1)}, u32[]{:S(2)}, u32[]{:S(2)}) async-start(f32[32,2,512]{2,1,0:T(2,128)} %get-tuple-element.94.refs_4_), calls=%async_computation.2 | async-start | bytes 262144 | tf_op jit(solution)/shard_map/all_to_all | solution.py:810
  110.1 0.8 copy-done.26
  110.9 5.6 %shard_map.244.refs_6_ = bf16[1,544,512]{2,1,0:T(8,128)(2,1)S(1)} custom-call(f32[4,512]{1,0:T(4,128)S(1)} %get-tuple-element.87.refs_0_.refs_2_, f32[4,512]{1,0:T(4,128)S(1)} %get-tuple-element.91.refs_1_.refs_3_.refs_2_, bf16[9,512,512]{2,1,0:T(8,128)(2,1)} %get-tuple-element.96.refs_2_.refs_4_, bf16[560,512]{1,0:T(8,128)(2,1)} %copy-done.26, ...), custom_call_target="tpu_custom_call" | custom-call | tf_op jit(solution)/shard_map/pallas_call | solution.py:564
  116.5 0.8 copy-done.4
  117.3 1.0 all-to-all-done.2.refs_1_
  118.3 2.6 %shard_map.245 = (f32[2,512]{1,0:T(2,128)S(1)}, bf16[2,64,640]{2,1,0:T(8,128)(2,1)S(1)}, bf16[2,64,640]{2,1,0:T(8,128)(2,1)S(1)}, bf16[2,64,640]{2,1,0:T(8,128)(...) custom-call(f32[4,512]{1,0:T(4,128)S(1)} %get-tuple-element.93.refs_0_, ...), custom_call_target="tpu_custom_call" | custom-call | tf_op jit(solution)/shard_map/pallas_call | solution.py:564
  120.9 0.9 collective-permute-start.29
  121.7 1.5 collective-permute-start.30
  123.2 1.2 collective-permute-start.31
  124.5 7.3 %shard_map.246 = (f32[544,512]{1,0:T(8,128)}, f32[32,2,512]{2,1,0:T(2,128)}) custom-call(bf16[544,512]{1,0:T(8,128)(2,1)} %get-tuple-element.98.refs_0_, f32[544,512]{1,0:T(8,128)} %get-tuple-element.78.refs_0_.refs_1_.refs_4_, f32[4,512]{1,0:T(4,128)S(1)} %get-tuple-element.87.refs_0_.refs_2_, f32[4,512]{1,0:T(4,128)S(1)} %get-tuple-element.91.refs_1_.refs_3_.refs_2_, ...), custom_call_target="tpu_custom_call" | custom-call | tf_op jit(solution)/shard_map/pallas_call | solution.py:564
  131.8 5.1 %all-to-all-start.3 = ((f32[32,2,512]{2,1,0:T(2,128)}), f32[32,2,512]{2,1,0:T(2,128)S(1)}, u32[]{:S(2)}, u32[]{:S(2)}) async-start(f32[32,2,512]{2,1,0:T(2,128)} %get-tuple-element.103), calls=%async_computation.3 | async-start | bytes 262144 | tf_op jit(solution)/shard_map/all_to_all | solution.py:810
  136.9 8.5 %shard_map.247 = (bf16[4,9,16,512]{3,2,1,0:T(8,128)(2,1)}, f32[4,9,16,512]{3,2,1,0:T(8,128)}) custom-call(bf16[2,64,640]{2,1,0:T(8,128)(2,1)S(1)} %get-tuple-element.105.refs_0_, bf16[2,64,640]{2,1,0:T(8,128)(2,1)S(1)} %collective-permute-done.29.refs_1_, bf16[2,64,640]{2,1,0:T(8,128)(2,1)S(1)} %collective-permute-done.30.refs_2_, ...), custom_call_target="tpu_custom_call" | custom-call | tf_op jit(solution)/shard_map/pallas_call | solution.py:564
  145.5 2.6 %shard_map.248 = (f32[2,512]{1,0:T(2,128)S(1)}, bf16[2,64,640]{2,1,0:T(8,128)(2,1)S(1)}, bf16[2,64,640]{2,1,0:T(8,128)(2,1)S(1)}, bf16[2,64,640]{2,1,0:T(8,128)(...) custom-call(f32[4,512]{1,0:T(4,128)S(1)} %get-tuple-element.87.refs_0_.refs_2_, ...), custom_call_target="tpu_custom_call" | custom-call | tf_op jit(solution)/shard_map/pallas_call | solution.py:564
  148.1 1.7 collective-permute-start.32
  149.9 1.5 collective-permute-start.33
  152.0 1.7 collective-permute-start.36
  153.7 2.4 %collective-permute-start.37 = (bf16[9,16,512]{2,1,0:T(8,128)(2,1)S(1)}, bf16[9,16,512]{2,1,0:T(8,128)(2,1)S(1)}, u32[]{:S(2)}, u32[]{:S(2)}) collective-permute-start(bf16[9,16,512]{2,1,0:T(8,128)(2,1)S(1)} %get-tuple-element.144.refs_9_), channel_id=1, source_target_pairs={{0,8},{4,12},{8,0},{12,4},{1,9},{5,13},{9,1},{13,5},{2,10},{6,14},... | collective-permute-start | bytes 442376 | tf_op jit(solution)/shard_map/ppermute | solution.py:588
  156.2 2.6 %collective-permute-start.38 = (bf16[9,16,512]{2,1,0:T(8,128)(2,1)S(1)}, bf16[9,16,512]{2,1,0:T(8,128)(2,1)S(1)}, u32[]{:S(2)}, u32[]{:S(2)}) collective-permute-start(bf16[9,16,512]{2,1,0:T(8,128)(2,1)S(1)} %get-tuple-element.143.refs_10_), channel_id=1, source_target_pairs={{0,12},{4,8},{8,4},{12,0},{1,13},{5,9},{9,5},{13,1},{2,14},{6,10},... | collective-permute-start | bytes 442376 | tf_op jit(solution)/shard_map/ppermute | solution.py:588
  158.7 0.8 collective-permute-done.33.refs_2_
  160.2 8.5 %shard_map.249 = (bf16[4,9,16,512]{3,2,1,0:T(8,128)(2,1)}, f32[4,9,16,512]{3,2,1,0:T(8,128)}) custom-call(bf16[2,64,640]{2,1,0:T(8,128)(2,1)S(1)} %get-tuple-element.111.refs_0_, bf16[2,64,640]{2,1,0:T(8,128)(2,1)S(1)} %collective-permute-done.32.refs_1_, bf16[2,64,640]{2,1,0:T(8,128)(2,1)S(1)} %collective-permute-done.33.refs_2_, ...), custom_call_target="tpu_custom_call" | custom-call | tf_op jit(solution)/shard_map/pallas_call | solution.py:564
  168.9 2.2 %collective-permute-done.39 = bf16[4,9,16,512]{3,2,1,0:T(8,128)(2,1)S(1)} collective-permute-done((bf16[4,9,16,512]{3,2,1,0:T(8,128)(2,1)}, bf16[4,9,16,512]{3,2,1,0:T(8,128)(2,1)S(1)}, u32[]{:S(2)}, u32[]{:S(2)}) %collective-permute-start.39) | collective-permute-done | bytes 589856 | tf_op jit(solution)/shard_map/ppermute | solution.py:588
  171.0 1.5 fusion.9
  172.6 0.7 slice_bitcast_fusion.1.refs_5_
  173.3 1.5 collective-permute-start.40
  174.8 2.4 %collective-permute-start.41 = (bf16[9,16,512]{2,1,0:T(8,128)(2,1)S(1)}, bf16[9,16,512]{2,1,0:T(8,128)(2,1)S(1)}, u32[]{:S(2)}, u32[]{:S(2)}) collective-permute-start(bf16[9,16,512]{2,1,0:T(8,128)(2,1)S(1)} %get-tuple-element.141.refs_7_), channel_id=1, source_target_pairs={{0,8},{4,12},{8,0},{12,4},{1,9},{5,13},{9,1},{13,5},{2,10},{6,14},... | collective-permute-start | bytes 442376 | tf_op jit(solution)/shard_map/ppermute | solution.py:588
  177.7 8.5 %shard_map.250 = (bf16[5,5,6,512]{3,2,1,0:T(8,128)(2,1)}, bf16[7,7,2,512]{3,2,1,0:T(2,128)(2,1)}, bf16[9,9,2,512]{3,2,1,0:T(2,128)(2,1)}, f32[5,5,6,512]{3,2,1,0...) custom-call(bf16[544,512]{1,0:T(8,128)(2,1)} %get-tuple-element.109.refs_0_, ...), custom_call_target="tpu_custom_call" | custom-call | tf_op jit(solution)/shard_map/pallas_call | solution.py:564
  186.3 1.5 collective-permute-start.44
  187.8 0.9 collective-permute-done.41
  188.8 1.5 collective-permute-start.43
  190.4 0.7 multiply_subtract_fusion
  191.0 2.0 collective-permute-done.44
  193.0 1.6 collective-permute-done.43
  194.7 2.7 %fusion.5 = (f32[2,3,3,512,32]{3,4,2,1,0:T(8,128)}, f32[2,3,3,512,32]{3,4,2,1,0:T(8,128)}, f32[2,3,3,512,32]{3,4,2,1,0:T(8,128)}) fusion(f32[2,3,3,512,32]{3,4,2,1,0:T(8,128)S(1)} %copy-done.37, bf16[1,3,3,16,512]{4,3,2,1,0:T(8,128)(2,1)S(1)} %bitcast.87, bf16[1,3,3,16,512]{4,3,2,1,0:T(8,128)(2,1)S(1)} %bitcast.86, ...), kind=kLoop, calls=%fused_computation.12 | loop fusion | flops 6488064 | bytes 7667712 | tf_op jit(solution)/shard_map/transpose | solution.py:962
  (153 shorter events, 8.6 us)
Async XLA Ops:
  2.1 13.4 %copy-start.6 = (bf16[6,5,5,512]{3,0,2,1:T(8,128)(2,1)S(1)}, bf16[6,5,5,512]{3,0,2,1:T(8,128)(2,1)}, u32[]{:S(2)}) copy-start(bf16[6,5,5,512]{3,0,2,1:T(8,128)(2,1)} %param.21) | copy-start | bytes 460804
  2.1 13.3 %copy-start.7 = (bf16[2,9,9,512]{3,0,2,1:T(2,128)(2,1)S(1)}, bf16[2,9,9,512]{3,0,2,1:T(2,128)(2,1)}, u32[]{:S(2)}) copy-start(bf16[2,9,9,512]{3,0,2,1:T(2,128)(2,1)} %param.23) | copy-start | bytes 497668
  2.2 26.0 %copy-start.24 = (bf16[1,3,3,32,512]{4,3,2,1,0:T(8,128)(2,1)}, bf16[1,3,3,32,512]{4,3,2,1,0:T(8,128)(2,1)S(1)}, u32[]{:S(2)}) copy-start(bf16[1,3,3,32,512]{4,3,2,1,0:T(8,128)(2,1)S(1)} %get-tuple-element.149) | copy-start | bytes 884740
  2.2 12.5 %collective-permute-start.1 = (bf16[1,9,32,512]{3,2,1,0:T(8,128)(2,1)S(1)}, bf16[1,9,32,512]{3,2,1,0:T(8,128)(2,1)S(1)}, u32[]{:S(2)}, u32[]{:S(2)}) collective-permute-start(bf16[1,9,32,512]{3,2,1,0:T(8,128)(2,1)S(1)} %bitcast.82), channel_id=1, source_target_pairs={{0,2},{2,0},{1,3},{3,1},{4,6},{6,4},{5,7},{7,5},{8,10},{10,8},{9,1... | collective-permute-start | bytes 884744 | tf_op jit(solution)/shard_map/ppermute | solution.py:588
  5.2 9.4 %collective-permute-start.3 = (bf16[1,9,32,256]{3,2,1,0:T(8,128)(2,1)S(1)}, bf16[1,9,32,256]{3,2,1,0:T(8,128)(2,1)S(1)}, u32[]{:S(2)}, u32[]{:S(2)}) collective-permute-start(bf16[1,9,32,256]{3,2,1,0:T(8,128)(2,1)S(1)} %get-tuple-element.147), channel_id=1, source_target_pairs={{0,8},{4,12},{8,0},{12,4},{1,9},{5,13},{9,1},{13,5},{2,10},{6,14},... | collective-permute-start | bytes 442376 | tf_op jit(solution)/shard_map/ppermute | solution.py:588
  10.5 14.4 %collective-permute-start.5 = (bf16[560,512]{1,0:T(8,128)(2,1)}, bf16[560,512]{1,0:T(8,128)(2,1)S(1)}, u32[]{:S(2)}, u32[]{:S(2)}) collective-permute-start(bf16[560,512]{1,0:T(8,128)(2,1)} %get-tuple-element.97.refs_0_.refs_5_.refs_4_), channel_id=1, source_target_pairs={{0,2},{2,0},{1,3},{3,1},{4,6},{6,4},{5,7},{7,5},{8,10},{10,8},{9,1... | collective-permute-start | bytes 1720328 | tf_op jit(solution)/shard_map/ppermute | solution.py:588
  11.1 14.1 %collective-permute-start.6 = (bf16[560,512]{1,0:T(8,128)(2,1)}, bf16[560,512]{1,0:T(8,128)(2,1)S(1)}, u32[]{:S(2)}, u32[]{:S(2)}) collective-permute-start(bf16[560,512]{1,0:T(8,128)(2,1)} %get-tuple-element.97.refs_0_.refs_5_.refs_4_), channel_id=1, source_target_pairs={{0,16},{16,0},{1,17},{17,1},{2,18},{18,2},{3,19},{19,3},{4,20},{20... | collective-permute-start | bytes 1720328 | tf_op jit(solution)/shard_map/ppermute | solution.py:588
  14.7 22.8 %copy-start.32 = (bf16[1,9,32,512]{3,2,1,0:T(8,128)(2,1)}, bf16[1,9,32,512]{3,2,1,0:T(8,128)(2,1)S(1)}, u32[]{:S(2)}) copy-start(bf16[1,9,32,512]{3,2,1,0:T(8,128)(2,1)S(1)} %collective-permute-done.1.refs_5_.refs_4_) | copy-start | bytes 884740
  14.7 7.9 %collective-permute-start.4 = (bf16[2,9,32,256]{3,2,1,0:T(8,128)(2,1)S(1)}, bf16[2,9,32,256]{3,2,1,0:T(8,128)(2,1)S(1)}, u32[]{:S(2)}, u32[]{:S(2)}) collective-permute-start(bf16[2,9,32,256]{3,2,1,0:T(8,128)(2,1)S(1)} %pad_maximum_fusion.2), channel_id=1, source_target_pairs={{0,4},{4,0},{8,12},{12,8},{1,5},{5,1},{9,13},{13,9},{2,6},{6,2},{1... | collective-permute-start | bytes 884744 | tf_op jit(solution)/shard_map/ppermute | solution.py:588
  22.7 26.5 %copy-start.20 = (bf16[3,9,32,256]{3,2,1,0:T(8,128)(2,1)}, bf16[3,9,32,256]{3,2,1,0:T(8,128)(2,1)S(1)}, u32[]{:S(2)}) copy-start(bf16[3,9,32,256]{3,2,1,0:T(8,128)(2,1)S(1)} %pad_maximum_fusion.refs_7_.refs_6_) | copy-start | bytes 1327108
  24.9 24.2 %copy-start.15 = (bf16[560,512]{1,0:T(8,128)(2,1)}, bf16[560,512]{1,0:T(8,128)(2,1)S(1)}, u32[]{:S(2)}) copy-start(bf16[560,512]{1,0:T(8,128)(2,1)S(1)} %collective-permute-done.5.refs_17_.refs_16_.refs_5_) | copy-start | bytes 1720324
  25.2 24.0 %copy-start.16 = (bf16[560,512]{1,0:T(8,128)(2,1)}, bf16[560,512]{1,0:T(8,128)(2,1)S(1)}, u32[]{:S(2)}) copy-start(bf16[560,512]{1,0:T(8,128)(2,1)S(1)} %collective-permute-done.6.refs_18_.refs_17_.refs_6_) | copy-start | bytes 1720324
  25.2 10.2 %collective-permute-start.10 = (bf16[3,9,32,256]{3,2,1,0:T(8,128)(2,1)S(1)}, bf16[3,9,32,256]{3,2,1,0:T(8,128)(2,1)S(1)}, u32[]{:S(2)}, u32[]{:S(2)}) collective-permute-start(bf16[3,9,32,256]{3,2,1,0:T(8,128)(2,1)S(1)} %pad_maximum_fusion.refs_7_.refs_6_), channel_id=1, source_target_pairs={{0,16},{16,0},{1,17},{17,1},{2,18},{18,2},{3,19},{19,3},{4,20},{20... | collective-permute-start | bytes 1327112 | tf_op jit(solution)/shard_map/ppermute | solution.py:588
  26.7 11.0 %collective-permute-start.8 = (bf16[3,9,32,256]{3,2,1,0:T(8,128)(2,1)S(1)}, bf16[3,9,32,256]{3,2,1,0:T(8,128)(2,1)S(1)}, u32[]{:S(2)}, u32[]{:S(2)}) collective-permute-start(bf16[3,9,32,256]{3,2,1,0:T(8,128)(2,1)S(1)} %pad_maximum_fusion.refs_7_.refs_6_), channel_id=1, source_target_pairs={{0,2},{2,0},{1,3},{3,1},{4,6},{6,4},{5,7},{7,5},{8,10},{10,8},{9,1... | collective-permute-start | bytes 1327112 | tf_op jit(solution)/shard_map/ppermute | solution.py:588
  28.2 11.4 %collective-permute-start = (bf16[1,9,32,512]{3,2,1,0:T(8,128)(2,1)S(1)}, bf16[1,9,32,512]{3,2,1,0:T(8,128)(2,1)S(1)}, u32[]{:S(2)}, u32[]{:S(2)}) collective-permute-start(bf16[1,9,32,512]{3,2,1,0:T(8,128)(2,1)S(1)} %bitcast.83), channel_id=1, source_target_pairs={{0,1},{1,0},{2,3},{3,2},{4,5},{5,4},{6,7},{7,6},{8,9},{9,8},{10,11... | collective-permute-start | bytes 884744 | tf_op jit(solution)/shard_map/ppermute | solution.py:588
  28.2 11.3 %collective-permute-start.19 = (bf16[1,9,32,256]{3,2,1,0:T(8,128)(2,1)S(1)}, bf16[1,9,32,256]{3,2,1,0:T(8,128)(2,1)S(1)}, u32[]{:S(2)}, u32[]{:S(2)}) collective-permute-start(bf16[1,9,32,256]{3,2,1,0:T(8,128)(2,1)S(1)} %get-tuple-element.81), channel_id=1, source_target_pairs={{0,8},{4,12},{8,0},{12,4},{1,9},{5,13},{9,1},{13,5},{2,10},{6,14},... | collective-permute-start | bytes 442376 | tf_op jit(solution)/shard_map/ppermute | solution.py:588
  30.4 10.9 %collective-permute-start.2 = (bf16[1,9,32,512]{3,2,1,0:T(8,128)(2,1)S(1)}, bf16[1,9,32,512]{3,2,1,0:T(8,128)(2,1)S(1)}, u32[]{:S(2)}, u32[]{:S(2)}) collective-permute-start(bf16[1,9,32,512]{3,2,1,0:T(8,128)(2,1)S(1)} %collective-permute-done.1.refs_5_.refs_4_), channel_id=1, source_target_pairs={{0,1},{1,0},{2,3},{3,2},{4,5},{5,4},{6,7},{7,6},{8,9},{9,8},{10,11... | collective-permute-start | bytes 884744 | tf_op jit(solution)/shard_map/ppermute | solution.py:588
  35.4 13.8 %copy-start.22 = (bf16[3,9,32,256]{3,2,1,0:T(8,128)(2,1)}, bf16[3,9,32,256]{3,2,1,0:T(8,128)(2,1)S(1)}, u32[]{:S(2)}) copy-start(bf16[3,9,32,256]{3,2,1,0:T(8,128)(2,1)S(1)} %collective-permute-done.10.refs_11_.refs_10_) | copy-start | bytes 1327108
  35.4 13.2 %collective-permute-start.17 = (bf16[1,9,32,512]{3,2,1,0:T(8,128)(2,1)S(1)}, bf16[1,9,32,512]{3,2,1,0:T(8,128)(2,1)S(1)}, u32[]{:S(2)}, u32[]{:S(2)}) collective-permute-start(bf16[1,9,32,512]{3,2,1,0:T(8,128)(2,1)S(1)} %bitcast.68), channel_id=1, source_target_pairs={{0,2},{2,0},{1,3},{3,1},{4,6},{6,4},{5,7},{7,5},{8,10},{10,8},{9,1... | collective-permute-start | bytes 884744 | tf_op jit(solution)/shard_map/ppermute | solution.py:588
  37.7 15.3 %copy-start.23 = (bf16[3,9,32,256]{3,2,1,0:T(8,128)(2,1)}, bf16[3,9,32,256]{3,2,1,0:T(8,128)(2,1)S(1)}, u32[]{:S(2)}) copy-start(bf16[3,9,32,256]{3,2,1,0:T(8,128)(2,1)S(1)} %collective-permute-done.8.refs_9_.refs_8_) | copy-start | bytes 1327108
  37.7 10.3 %collective-permute-start.12 = (bf16[3,9,16,256]{3,2,1,0:T(8,128)(2,1)S(1)}, bf16[3,9,16,256]{3,2,1,0:T(8,128)(2,1)S(1)}, u32[]{:S(2)}, u32[]{:S(2)}) collective-permute-start(bf16[3,9,16,256]{3,2,1,0:T(8,128)(2,1)S(1)} %slice.63), channel_id=1, source_target_pairs={{0,2},{2,0},{1,3},{3,1},{4,6},{6,4},{5,7},{7,5},{8,10},{10,8},{9,1... | collective-permute-start | bytes 663560 | tf_op jit(solution)/shard_map/ppermute | solution.py:588
  39.5 8.6 %collective-permute-start.13 = (bf16[3,9,16,256]{3,2,1,0:T(8,128)(2,1)S(1)}, bf16[3,9,16,256]{3,2,1,0:T(8,128)(2,1)S(1)}, u32[]{:S(2)}, u32[]{:S(2)}) collective-permute-start(bf16[3,9,16,256]{3,2,1,0:T(8,128)(2,1)S(1)} %slice.64), channel_id=1, source_target_pairs={{0,16},{16,0},{1,17},{17,1},{2,18},{18,2},{3,19},{19,3},{4,20},{20... | collective-permute-start | bytes 663560 | tf_op jit(solution)/shard_map/ppermute | solution.py:588
  39.6 13.4 %copy-start.34 = (bf16[1,9,32,512]{3,2,1,0:T(8,128)(2,1)}, bf16[1,9,32,512]{3,2,1,0:T(8,128)(2,1)S(1)}, u32[]{:S(2)}) copy-start(bf16[1,9,32,512]{3,2,1,0:T(8,128)(2,1)S(1)} %collective-permute-done.refs_4_.refs_3_) | copy-start | bytes 884740
  39.6 9.0 %collective-permute-start.20 = (bf16[2,9,32,256]{3,2,1,0:T(8,128)(2,1)S(1)}, bf16[2,9,32,256]{3,2,1,0:T(8,128)(2,1)S(1)}, u32[]{:S(2)}, u32[]{:S(2)}) collective-permute-start(bf16[2,9,32,256]{3,2,1,0:T(8,128)(2,1)S(1)} %pad_maximum_fusion.3), channel_id=1, source_target_pairs={{0,4},{4,0},{8,12},{12,8},{1,5},{5,1},{9,13},{13,9},{2,6},{6,2},{1... | collective-permute-start | bytes 884744 | tf_op jit(solution)/shard_map/ppermute | solution.py:588
  41.3 7.9 %collective-permute-start.7 = (bf16[3,9,32,256]{3,2,1,0:T(8,128)(2,1)S(1)}, bf16[3,9,32,256]{3,2,1,0:T(8,128)(2,1)S(1)}, u32[]{:S(2)}, u32[]{:S(2)}) collective-permute-start(bf16[3,9,32,256]{3,2,1,0:T(8,128)(2,1)S(1)} %pad_maximum_fusion.refs_7_.refs_6_), channel_id=1, source_target_pairs={{0,1},{1,0},{2,3},{3,2},{4,5},{5,4},{6,7},{7,6},{8,9},{9,8},{10,11... | collective-permute-start | bytes 1327112 | tf_op jit(solution)/shard_map/ppermute | solution.py:588
  48.1 5.0 %collective-permute-start.11 = (bf16[3,9,32,256]{3,2,1,0:T(8,128)(2,1)S(1)}, bf16[3,9,32,256]{3,2,1,0:T(8,128)(2,1)S(1)}, u32[]{:S(2)}, u32[]{:S(2)}) collective-permute-start(bf16[3,9,32,256]{3,2,1,0:T(8,128)(2,1)S(1)} %collective-permute-done.10.refs_11_.refs_10_), channel_id=1, source_target_pairs={{0,1},{1,0},{2,3},{3,2},{4,5},{5,4},{6,7},{7,6},{8,9},{9,8},{10,11... | collective-permute-start | bytes 1327112 | tf_op jit(solution)/shard_map/ppermute | solution.py:588
  48.1 5.0 %collective-permute-start.9 = (bf16[3,9,32,256]{3,2,1,0:T(8,128)(2,1)S(1)}, bf16[3,9,32,256]{3,2,1,0:T(8,128)(2,1)S(1)}, u32[]{:S(2)}, u32[]{:S(2)}) collective-permute-start(bf16[3,9,32,256]{3,2,1,0:T(8,128)(2,1)S(1)} %collective-permute-done.8.refs_9_.refs_8_), channel_id=1, source_target_pairs={{0,1},{1,0},{2,3},{3,2},{4,5},{5,4},{6,7},{7,6},{8,9},{9,8},{10,11... | collective-permute-start | bytes 1327112 | tf_op jit(solution)/shard_map/ppermute | solution.py:588
  48.6 26.7 %copy-start.33 = (bf16[1,9,32,512]{3,2,1,0:T(8,128)(2,1)}, bf16[1,9,32,512]{3,2,1,0:T(8,128)(2,1)S(1)}, u32[]{:S(2)}) copy-start(bf16[1,9,32,512]{3,2,1,0:T(8,128)(2,1)S(1)} %collective-permute-done.17.refs_5_.refs_7_) | copy-start | bytes 884740
  48.6 2.2 %collective-permute-start.14 = (bf16[3,9,16,256]{3,2,1,0:T(8,128)(2,1)S(1)}, bf16[3,9,16,256]{3,2,1,0:T(8,128)(2,1)S(1)}, u32[]{:S(2)}, u32[]{:S(2)}) collective-permute-start(bf16[3,9,16,256]{3,2,1,0:T(8,128)(2,1)S(1)} %collective-permute-done.12.refs_13_.refs_12_), channel_id=1, source_target_pairs={{0,1},{1,0},{2,3},{3,2},{4,5},{5,4},{6,7},{7,6},{8,9},{9,8},{10,11... | collective-permute-start | bytes 663560 | tf_op jit(solution)/shard_map/ppermute | solution.py:588
  48.7 3.9 %collective-permute-start.15 = (bf16[3,9,16,256]{3,2,1,0:T(8,128)(2,1)S(1)}, bf16[3,9,16,256]{3,2,1,0:T(8,128)(2,1)S(1)}, u32[]{:S(2)}, u32[]{:S(2)}) collective-permute-start(bf16[3,9,16,256]{3,2,1,0:T(8,128)(2,1)S(1)} %collective-permute-done.13.refs_15_.refs_14_), channel_id=1, source_target_pairs={{0,1},{1,0},{2,3},{3,2},{4,5},{5,4},{6,7},{7,6},{8,9},{9,8},{10,11... | collective-permute-start | bytes 663560 | tf_op jit(solution)/shard_map/ppermute | solution.py:588
  49.2 17.4 %copy-start.21 = (bf16[3,9,32,256]{3,2,1,0:T(8,128)(2,1)}, bf16[3,9,32,256]{3,2,1,0:T(8,128)(2,1)S(1)}, u32[]{:S(2)}) copy-start(bf16[3,9,32,256]{3,2,1,0:T(8,128)(2,1)S(1)} %pad_maximum_fusion.1.refs_7_.refs_9_) | copy-start | bytes 1327108
  49.2 17.6 %collective-permute-start.24 = (bf16[3,9,32,256]{3,2,1,0:T(8,128)(2,1)S(1)}, bf16[3,9,32,256]{3,2,1,0:T(8,128)(2,1)S(1)}, u32[]{:S(2)}, u32[]{:S(2)}) collective-permute-start(bf16[3,9,32,256]{3,2,1,0:T(8,128)(2,1)S(1)} %pad_maximum_fusion.1.refs_7_.refs_9_), channel_id=1, source_target_pairs={{0,16},{16,0},{1,17},{17,1},{2,18},{18,2},{3,19},{19,3},{4,20},{20... | collective-permute-start | bytes 1327112 | tf_op jit(solution)/shard_map/ppermute | solution.py:588
  50.8 16.3 %collective-permute-start.22 = (bf16[3,9,32,256]{3,2,1,0:T(8,128)(2,1)S(1)}, bf16[3,9,32,256]{3,2,1,0:T(8,128)(2,1)}, u32[]{:S(2)}, u32[]{:S(2)}) collective-permute-start(bf16[3,9,32,256]{3,2,1,0:T(8,128)(2,1)S(1)} %pad_maximum_fusion.1.refs_7_.refs_9_), channel_id=1, source_target_pairs={{0,2},{2,0},{1,3},{3,1},{4,6},{6,4},{5,7},{7,5},{8,10},{10,8},{9,1... | collective-permute-start | bytes 1327112 | tf_op jit(solution)/shard_map/ppermute | solution.py:588
  52.6 21.6 %collective-permute-start.26 = (bf16[3,9,32,256]{3,2,1,0:T(8,128)(2,1)S(1)}, bf16[3,9,32,256]{3,2,1,0:T(8,128)(2,1)}, u32[]{:S(2)}, u32[]{:S(2)}) collective-permute-start(bf16[3,9,32,256]{3,2,1,0:T(8,128)(2,1)S(1)} %pad_maximum_fusion.1.refs_7_.refs_9_), channel_id=1, source_target_pairs={{0,18},{2,16},{16,2},{18,0},{1,19},{3,17},{17,3},{19,1},{4,22},{6,... | collective-permute-start | bytes 1327112 | tf_op jit(solution)/shard_map/ppermute | solution.py:592
  54.0 23.2 %copy-start.17 = (bf16[560,512]{1,0:T(8,128)(2,1)S(1)}, bf16[560,512]{1,0:T(8,128)(2,1)}, u32[]{:S(2)}) copy-start(bf16[560,512]{1,0:T(8,128)(2,1)} %get-tuple-element.97.refs_0_.refs_5_.refs_4_) | copy-start | bytes 1720324
  54.0 26.0 %copy-start.1 = (f32[544,128]{1,0:T(8,128)S(1)}, f32[544,128]{1,0:T(8,128)}, u32[]{:S(2)}) copy-start(f32[544,128]{1,0:T(8,128)} %copy-done) | copy-start | bytes 835588
  60.6 14.3 %all-to-all-start = ((f32[32,2,640]{2,1,0:T(2,128)}), f32[32,2,640]{2,1,0:T(2,128)S(1)}, u32[]{:S(2)}, u32[]{:S(2)}) async-start(f32[32,2,640]{2,1,0:T(2,128)} %get-tuple-element.79), calls=%async_computation | async-start | bytes 327680 | tf_op jit(solution)/shard_map/all_to_all | solution.py:810
  66.3 9.0 %collective-permute-start.16 = (bf16[1,9,32,512]{3,2,1,0:T(8,128)(2,1)S(1)}, bf16[1,9,32,512]{3,2,1,0:T(8,128)(2,1)}, u32[]{:S(2)}, u32[]{:S(2)}) collective-permute-start(bf16[1,9,32,512]{3,2,1,0:T(8,128)(2,1)S(1)} %bitcast.69), channel_id=1, source_target_pairs={{0,1},{1,0},{2,3},{3,2},{4,5},{5,4},{6,7},{7,6},{8,9},{9,8},{10,11... | collective-permute-start | bytes 884744 | tf_op jit(solution)/shard_map/ppermute | solution.py:588
  66.6 12.5 %collective-permute-start.21 = (bf16[3,9,32,256]{3,2,1,0:T(8,128)(2,1)S(1)}, bf16[3,9,32,256]{3,2,1,0:T(8,128)(2,1)}, u32[]{:S(2)}, u32[]{:S(2)}) collective-permute-start(bf16[3,9,32,256]{3,2,1,0:T(8,128)(2,1)S(1)} %pad_maximum_fusion.1.refs_7_.refs_9_), channel_id=1, source_target_pairs={{0,1},{1,0},{2,3},{3,2},{4,5},{5,4},{6,7},{7,6},{8,9},{9,8},{10,11... | collective-permute-start | bytes 1327112 | tf_op jit(solution)/shard_map/ppermute | solution.py:588
  66.8 12.3 %collective-permute-start.25 = (bf16[3,9,32,256]{3,2,1,0:T(8,128)(2,1)S(1)}, bf16[3,9,32,256]{3,2,1,0:T(8,128)(2,1)}, u32[]{:S(2)}, u32[]{:S(2)}) collective-permute-start(bf16[3,9,32,256]{3,2,1,0:T(8,128)(2,1)S(1)} %collective-permute-done.24.refs_11_.refs_13_), channel_id=1, source_target_pairs={{0,1},{1,0},{2,3},{3,2},{4,5},{5,4},{6,7},{7,6},{8,9},{9,8},{10,11... | collective-permute-start | bytes 1327112 | tf_op jit(solution)/shard_map/ppermute | solution.py:588
  67.1 12.0 %collective-permute-start.23 = (bf16[3,9,32,256]{3,2,1,0:T(8,128)(2,1)}, bf16[3,9,32,256]{3,2,1,0:T(8,128)(2,1)}, u32[]{:S(2)}, u32[]{:S(2)}) collective-permute-start(bf16[3,9,32,256]{3,2,1,0:T(8,128)(2,1)} %collective-permute-done.22.refs_9_.refs_11_), channel_id=1, source_target_pairs={{0,1},{1,0},{2,3},{3,2},{4,5},{5,4},{6,7},{7,6},{8,9},{9,8},{10,11... | collective-permute-start | bytes 1327112 | tf_op jit(solution)/shard_map/ppermute | solution.py:588
  74.8 4.3 %collective-permute-start.27 = (bf16[3,9,32,256]{3,2,1,0:T(8,128)(2,1)}, bf16[3,9,32,256]{3,2,1,0:T(8,128)(2,1)S(1)}, u32[]{:S(2)}, u32[]{:S(2)}) collective-permute-start(bf16[3,9,32,256]{3,2,1,0:T(8,128)(2,1)} %collective-permute-done.26.refs_13_.refs_15_), channel_id=1, source_target_pairs={{0,1},{1,0},{2,3},{3,2},{4,5},{5,4},{6,7},{7,6},{8,9},{9,8},{10,11... | collective-permute-start | bytes 1327112 | tf_op jit(solution)/shard_map/ppermute | solution.py:588
  75.3 1.8 collective-permute-start.18
  77.1 33.0 %collective-permute-start.28 = (bf16[560,512]{1,0:T(8,128)(2,1)S(1)}, bf16[560,512]{1,0:T(8,128)(2,1)S(1)}, u32[]{:S(2)}, u32[]{:S(2)}) collective-permute-start(bf16[560,512]{1,0:T(8,128)(2,1)S(1)} %copy-done.17), channel_id=1, source_target_pairs={{0,18},{2,16},{16,2},{18,0},{1,19},{3,17},{17,3},{19,1},{4,22},{6,... | collective-permute-start | bytes 1720328 | tf_op jit(solution)/shard_map/ppermute | solution.py:592
  86.9 13.8 %all-to-all-start.1 = ((f32[32,2,512]{2,1,0:T(2,128)}), f32[32,2,512]{2,1,0:T(2,128)S(1)}, u32[]{:S(2)}, u32[]{:S(2)}) async-start(f32[32,2,512]{2,1,0:T(2,128)} %get-tuple-element.89.refs_18_), calls=%async_computation.1 | async-start | bytes 262144 | tf_op jit(solution)/shard_map/all_to_all | solution.py:810
  104.4 13.9 %all-to-all-start.2 = ((f32[32,2,512]{2,1,0:T(2,128)}), f32[32,2,512]{2,1,0:T(2,128)S(1)}, u32[]{:S(2)}, u32[]{:S(2)}) async-start(f32[32,2,512]{2,1,0:T(2,128)} %get-tuple-element.94.refs_4_), calls=%async_computation.2 | async-start | bytes 262144 | tf_op jit(solution)/shard_map/all_to_all | solution.py:810
  120.9 10.9 %collective-permute-start.29 = (bf16[2,64,640]{2,1,0:T(8,128)(2,1)S(1)}, bf16[2,64,640]{2,1,0:T(8,128)(2,1)S(1)}, u32[]{:S(2)}, u32[]{:S(2)}) collective-permute-start(bf16[2,64,640]{2,1,0:T(8,128)(2,1)S(1)} %get-tuple-element.100), channel_id=1, source_target_pairs={{0,2},{2,0},{1,3},{3,1},{4,6},{6,4},{5,7},{7,5},{8,10},{10,8},{9,1... | collective-permute-start | bytes 491528 | tf_op jit(solution)/shard_map/ppermute | solution.py:588
  121.7 10.0 %collective-permute-start.30 = (bf16[2,64,640]{2,1,0:T(8,128)(2,1)S(1)}, bf16[2,64,640]{2,1,0:T(8,128)(2,1)S(1)}, u32[]{:S(2)}, u32[]{:S(2)}) collective-permute-start(bf16[2,64,640]{2,1,0:T(8,128)(2,1)S(1)} %get-tuple-element.101), channel_id=1, source_target_pairs={{0,16},{16,0},{1,17},{17,1},{2,18},{18,2},{3,19},{19,3},{4,20},{20... | collective-permute-start | bytes 491528 | tf_op jit(solution)/shard_map/ppermute | solution.py:588
  123.2 8.6 %collective-permute-start.31 = (bf16[2,64,640]{2,1,0:T(8,128)(2,1)S(1)}, bf16[2,64,640]{2,1,0:T(8,128)(2,1)S(1)}, u32[]{:S(2)}, u32[]{:S(2)}) collective-permute-start(bf16[2,64,640]{2,1,0:T(8,128)(2,1)S(1)} %get-tuple-element.102), channel_id=1, source_target_pairs={{0,18},{2,16},{16,2},{18,0},{1,19},{3,17},{17,3},{19,1},{4,22},{6,... | collective-permute-start | bytes 491528 | tf_op jit(solution)/shard_map/ppermute | solution.py:592
  131.8 13.6 %all-to-all-start.3 = ((f32[32,2,512]{2,1,0:T(2,128)}), f32[32,2,512]{2,1,0:T(2,128)S(1)}, u32[]{:S(2)}, u32[]{:S(2)}) async-start(f32[32,2,512]{2,1,0:T(2,128)} %get-tuple-element.103), calls=%async_computation.3 | async-start | bytes 262144 | tf_op jit(solution)/shard_map/all_to_all | solution.py:810
  145.4 6.3 %collective-permute-start.35 = (bf16[4,9,16,512]{3,2,1,0:T(8,128)(2,1)}, bf16[4,9,16,512]{3,2,1,0:T(8,128)(2,1)S(1)}, u32[]{:S(2)}, u32[]{:S(2)}) collective-permute-start(bf16[4,9,16,512]{3,2,1,0:T(8,128)(2,1)} %get-tuple-element.115.refs_6_), channel_id=1, source_target_pairs={{0,1},{1,0},{2,3},{3,2},{4,5},{5,4},{6,7},{7,6},{8,9},{9,8},{10,11... | collective-permute-start | bytes 1769480 | tf_op jit(solution)/shard_map/ppermute | solution.py:588
  148.1 8.0 %collective-permute-start.32 = (bf16[2,64,640]{2,1,0:T(8,128)(2,1)S(1)}, bf16[2,64,640]{2,1,0:T(8,128)(2,1)S(1)}, u32[]{:S(2)}, u32[]{:S(2)}) collective-permute-start(bf16[2,64,640]{2,1,0:T(8,128)(2,1)S(1)} %get-tuple-element.112), channel_id=1, source_target_pairs={{0,2},{2,0},{1,3},{3,1},{4,6},{6,4},{5,7},{7,5},{8,10},{10,8},{9,1... | collective-permute-start | bytes 491528 | tf_op jit(solution)/shard_map/ppermute | solution.py:588
  149.9 9.7 %collective-permute-start.33 = (bf16[2,64,640]{2,1,0:T(8,128)(2,1)S(1)}, bf16[2,64,640]{2,1,0:T(8,128)(2,1)S(1)}, u32[]{:S(2)}, u32[]{:S(2)}) collective-permute-start(bf16[2,64,640]{2,1,0:T(8,128)(2,1)S(1)} %get-tuple-element.113), channel_id=1, source_target_pairs={{0,16},{16,0},{1,17},{17,1},{2,18},{18,2},{3,19},{19,3},{4,20},{20... | collective-permute-start | bytes 491528 | tf_op jit(solution)/shard_map/ppermute | solution.py:588
  151.3 8.2 %collective-permute-start.34 = (bf16[2,64,640]{2,1,0:T(8,128)(2,1)S(1)}, bf16[2,64,640]{2,1,0:T(8,128)(2,1)S(1)}, u32[]{:S(2)}, u32[]{:S(2)}) collective-permute-start(bf16[2,64,640]{2,1,0:T(8,128)(2,1)S(1)} %get-tuple-element.114), channel_id=1, source_target_pairs={{0,18},{2,16},{16,2},{18,0},{1,19},{3,17},{17,3},{19,1},{4,22},{6,... | collective-permute-start | bytes 491528 | tf_op jit(solution)/shard_map/ppermute | solution.py:592
  152.0 16.7 %collective-permute-start.36 = (bf16[9,16,512]{2,1,0:T(8,128)(2,1)S(1)}, bf16[9,16,512]{2,1,0:T(8,128)(2,1)S(1)}, u32[]{:S(2)}, u32[]{:S(2)}) collective-permute-start(bf16[9,16,512]{2,1,0:T(8,128)(2,1)S(1)} %get-tuple-element.145.refs_8_), channel_id=1, source_target_pairs={{0,4},{4,0},{8,12},{12,8},{1,5},{5,1},{9,13},{13,9},{2,6},{6,2},{1... | collective-permute-start | bytes 442376 | tf_op jit(solution)/shard_map/ppermute | solution.py:588
  153.7 15.0 %collective-permute-start.37 = (bf16[9,16,512]{2,1,0:T(8,128)(2,1)S(1)}, bf16[9,16,512]{2,1,0:T(8,128)(2,1)S(1)}, u32[]{:S(2)}, u32[]{:S(2)}) collective-permute-start(bf16[9,16,512]{2,1,0:T(8,128)(2,1)S(1)} %get-tuple-element.144.refs_9_), channel_id=1, source_target_pairs={{0,8},{4,12},{8,0},{12,4},{1,9},{5,13},{9,1},{13,5},{2,10},{6,14},... | collective-permute-start | bytes 442376 | tf_op jit(solution)/shard_map/ppermute | solution.py:588
  156.2 12.6 %collective-permute-start.38 = (bf16[9,16,512]{2,1,0:T(8,128)(2,1)S(1)}, bf16[9,16,512]{2,1,0:T(8,128)(2,1)S(1)}, u32[]{:S(2)}, u32[]{:S(2)}) collective-permute-start(bf16[9,16,512]{2,1,0:T(8,128)(2,1)S(1)} %get-tuple-element.143.refs_10_), channel_id=1, source_target_pairs={{0,12},{4,8},{8,4},{12,0},{1,13},{5,9},{9,5},{13,1},{2,14},{6,10},... | collective-permute-start | bytes 442376 | tf_op jit(solution)/shard_map/ppermute | solution.py:588
  168.7 2.3 %collective-permute-start.39 = (bf16[4,9,16,512]{3,2,1,0:T(8,128)(2,1)}, bf16[4,9,16,512]{3,2,1,0:T(8,128)(2,1)S(1)}, u32[]{:S(2)}, u32[]{:S(2)}) collective-permute-start(bf16[4,9,16,512]{3,2,1,0:T(8,128)(2,1)} %get-tuple-element.118), channel_id=1, source_target_pairs={{0,1},{1,0},{2,3},{3,2},{4,5},{5,4},{6,7},{7,6},{8,9},{9,8},{10,11... | collective-permute-start | bytes 1769480 | tf_op jit(solution)/shard_map/ppermute | solution.py:588
  173.3 14.5 %collective-permute-start.40 = (bf16[9,16,512]{2,1,0:T(8,128)(2,1)S(1)}, bf16[9,16,512]{2,1,0:T(8,128)(2,1)S(1)}, u32[]{:S(2)}, u32[]{:S(2)}) collective-permute-start(bf16[9,16,512]{2,1,0:T(8,128)(2,1)S(1)} %get-tuple-element.142.refs_6_), channel_id=1, source_target_pairs={{0,4},{4,0},{8,12},{12,8},{1,5},{5,1},{9,13},{13,9},{2,6},{6,2},{1... | collective-permute-start | bytes 442376 | tf_op jit(solution)/shard_map/ppermute | solution.py:588
  174.8 13.9 %collective-permute-start.41 = (bf16[9,16,512]{2,1,0:T(8,128)(2,1)S(1)}, bf16[9,16,512]{2,1,0:T(8,128)(2,1)S(1)}, u32[]{:S(2)}, u32[]{:S(2)}) collective-permute-start(bf16[9,16,512]{2,1,0:T(8,128)(2,1)S(1)} %get-tuple-element.141.refs_7_), channel_id=1, source_target_pairs={{0,8},{4,12},{8,0},{12,4},{1,9},{5,13},{9,1},{13,5},{2,10},{6,14},... | collective-permute-start | bytes 442376 | tf_op jit(solution)/shard_map/ppermute | solution.py:588
  177.2 11.5 %collective-permute-start.42 = (bf16[9,16,512]{2,1,0:T(8,128)(2,1)S(1)}, bf16[9,16,512]{2,1,0:T(8,128)(2,1)S(1)}, u32[]{:S(2)}, u32[]{:S(2)}) collective-permute-start(bf16[9,16,512]{2,1,0:T(8,128)(2,1)S(1)} %get-tuple-element.140.refs_8_), channel_id=1, source_target_pairs={{0,12},{4,8},{8,4},{12,0},{1,13},{5,9},{9,5},{13,1},{2,14},{6,10},... | collective-permute-start | bytes 442376 | tf_op jit(solution)/shard_map/ppermute | solution.py:588
  177.7 16.9 %copy-start.38 = (f32[2,3,3,512,32]{3,4,2,1,0:T(8,128)S(1)}, f32[2,3,3,512,32]{3,4,2,1,0:T(8,128)}, u32[]{:S(2)}) copy-start(f32[2,3,3,512,32]{3,4,2,1,0:T(8,128)} %param.26) | copy-start | bytes 3538948
  186.3 6.7 %collective-permute-start.44 = (bf16[9,16,512]{2,1,0:T(8,128)(2,1)S(1)}, bf16[9,16,512]{2,1,0:T(8,128)(2,1)S(1)}, u32[]{:S(2)}, u32[]{:S(2)}) collective-permute-start(bf16[9,16,512]{2,1,0:T(8,128)(2,1)S(1)} %add_convert_fusion), channel_id=1, source_target_pairs={{0,16},{16,0},{1,17},{17,1},{2,18},{18,2},{3,19},{19,3},{4,20},{20... | collective-permute-start | bytes 442376 | tf_op jit(solution)/shard_map/ppermute | solution.py:588
  188.8 5.8 %collective-permute-start.43 = (bf16[9,16,512]{2,1,0:T(8,128)(2,1)S(1)}, bf16[9,16,512]{2,1,0:T(8,128)(2,1)S(1)}, u32[]{:S(2)}, u32[]{:S(2)}) collective-permute-start(bf16[9,16,512]{2,1,0:T(8,128)(2,1)S(1)} %add_convert_fusion.1), channel_id=1, source_target_pairs={{0,16},{16,0},{1,17},{17,1},{2,18},{18,2},{3,19},{19,3},{4,20},{20... | collective-permute-start | bytes 442376 | tf_op jit(solution)/shard_map/ppermute | solution.py:588
  (28 other events, 155.7 us)
where the time goes:
time: 198 us; the launch traced here: 197 us
  Pallas kernels  74 us (37%)
  starting transfers between devices  69.4 us (35%)
  waiting for transfers between devices  40.7 us (21%)
  other arithmetic  6.8 us (3%)
  local copies, waits for them, and re-layouts  5.03 us (3%)
    pallas_call x13, Pallas kernels, call(): pl.pallas_call(kernel, out_shape=[jax.ShapeDtypeStruct(shape, dtype) for...  74 us
    ppermute x41, starting transfers between devices, flip(): lax.ppermute(value, axis, [(place, place ^ bit) for place in range(size)])  44.6 us
    ppermute x41, waiting for transfers between devices, flip(): lax.ppermute(value, axis, [(place, place ^ bit) for place in range(size)])  32.2 us
    all_to_all x4, starting transfers between devices, exchange(): return lax.all_to_all(spread, ways.axes, 0, 0, tiled=True)  20.8 us
    ppermute x4, waiting for transfers between devices, diagonal(): lax.ppermute(value, ('y', 'x'), [(place, place ^ 3) for place in range(4)])  6.84 us
    unnamed x86, local copies, waits for them, and re-layouts  4.12 us
    ppermute x4, starting transfers between devices, diagonal(): lax.ppermute(value, ('y', 'x'), [(place, place ^ 3) for place in range(4)])  4.06 us
  transfers between devices with their start and end apart: 49, of which 17 were waited for; matrix products, arithmetic and copies ran while one was open for 1% of the time, Pallas kernels for 36%

commit v1 on v0

--- a/solution.py
+++ b/solution.py
@@ -446,8 +446,6 @@
     def half_sum(core, wait):
         for index in range(4):
             slot = index % 2
-            if wait:
-                pl.when(core == 1)(turns[index].wait)
             turned = turned_ref[index, c ^ core].astype(F32)
             for tap in range(TAPS):
                 shift = canvas.shift(tap) % canvas.lanes
@@ -466,6 +464,9 @@
 
     send = pltpu.make_async_copy(send_ref, send_hbm, sems.at[8])
     keep = pltpu.make_async_copy(keep_ref, keep_hbm, sems.at[9])
+
+    for turn in turns:
+        turn.wait()
 
     def both(step, carry):
         half_sum(1 - step, True)
@@ -708,14 +709,16 @@
 
     def core_sum(self, chip, *others):
         send, keep = chip
-        chip = keep + flip(behind(send, others), "c", 1, 2).astype(F32)
-        return chip[0], *[chip[place].astype(BF16) for place in range(1, 4)]
+        other = flip(behind(send, others), "c", 1, 2)
+        parts = [(keep[place] + other[place].astype(F32)).astype(BF16) for place in range(1, 4)]
+        return (keep[0], other[0]), *parts
 
     def line(self, parts):
         return [flip(part, "z", place, 4) for place, part in enumerate(parts[1:], 1)]
 
     def line_sum(self, parts, found, *others):
-        total = behind(parts[0], others)
+        keep, other = lax.optimization_barrier((*parts[0], *others))[:2]
+        total = keep + other.astype(F32)
         for part in found:
             total = total + part.astype(F32)
         return total
@@ -945,7 +948,7 @@
         [(shape, BF16) for shape in shapes] + [(shape, F32) for shape in shapes],
         (*weighted, buffer),
         weight_one.arrays,
-        core_one,
+        core_one[1:],
     )
     owned_two = ways.owned(ways.line_sum(core_two, line_two, finished[0]))
     owned_one = ways.owned(ways.line_sum(core_one, ways.line(core_one), finished[0]))

time: 198 us -> 195 us (0.985)
  Pallas kernels: 74 us -> 71.8 us
    pallas_call x13, Pallas kernels: 74 us -> 71.8 us  [call(): pl.pallas_call(kernel, out_shape=[jax.ShapeDtypeStruct(shape, dtype) for...]
    ppermute x41, starting transfers between devices: 44.6 us -> 42.4 us  [flip(): lax.ppermute(value, axis, [(place, place ^ bit) for place in range(size)])]
  transfers between devices with their start and end apart: 49 -> 49, of which waited for: 17 -> 19; matrix products, arithmetic and copies ran while one was open for 1% -> 1% of each run, Pallas kernels for 36% -> 36%
where the time goes in v1:
time: 195 us; the launch traced here: 194 us
  Pallas kernels  71.8 us (37%)
  starting transfers between devices  68.3 us (35%)
  waiting for transfers between devices  41.9 us (21%)
  other arithmetic  6.77 us (3%)
  local copies, waits for them, and re-layouts  4.22 us (2%)
    pallas_call x13, Pallas kernels, call(): pl.pallas_call(kernel, out_shape=[jax.ShapeDtypeStruct(shape, dtype) for...  71.8 us
    ppermute x41, starting transfers between devices, flip(): lax.ppermute(value, axis, [(place, place ^ bit) for place in range(size)])  42.4 us
    ppermute x41, waiting for transfers between devices, flip(): lax.ppermute(value, axis, [(place, place ^ bit) for place in range(size)])  32.5 us
    all_to_all x4, starting transfers between devices, exchange(): return lax.all_to_all(spread, ways.axes, 0, 0, tiled=True)  20.7 us
    ppermute x4, waiting for transfers between devices, diagonal(): lax.ppermute(value, ('y', 'x'), [(place, place ^ 3) for place in range(4)])  6.82 us
    ppermute x4, starting transfers between devices, diagonal(): lax.ppermute(value, ('y', 'x'), [(place, place ^ 3) for place in range(4)])  5.16 us
    unnamed x86, local copies, waits for them, and re-layouts  4.11 us
  transfers between devices with their start and end apart: 49, of which 19 were waited for; matrix products, arithmetic and copies ran while one was open for 1% of the time, Pallas kernels for 36%

profile of v1, /device:TPU:0, one launch (start us, length us, event | category | flops | bytes accessed | tf_op | source)
XLA Modules:
  0.0 194.4 jit_solution(3015950724367772139)
XLA Ops:
  0.6 1.4 bitcast_convert_fusion
  2.2 3.0 %collective-permute-start.1 = (bf16[1,9,32,512]{3,2,1,0:T(8,128)(2,1)S(1)}, bf16[1,9,32,512]{3,2,1,0:T(8,128)(2,1)S(1)}, u32[]{:S(2)}, u32[]{:S(2)}) collective-permute-start(bf16[1,9,32,512]{3,2,1,0:T(8,128)(2,1)S(1)} %bitcast.86), channel_id=1, source_target_pairs={{0,2},{2,0},{1,3},{3,1},{4,6},{6,4},{5,7},{7,5},{8,10},{10,8},{9,1... | collective-permute-start | bytes 884744 | tf_op jit(solution)/shard_map/ppermute | solution.py:589
  5.2 2.7 %collective-permute-start.3 = (bf16[1,9,32,256]{3,2,1,0:T(8,128)(2,1)S(1)}, bf16[1,9,32,256]{3,2,1,0:T(8,128)(2,1)S(1)}, u32[]{:S(2)}, u32[]{:S(2)}) collective-permute-start(bf16[1,9,32,256]{3,2,1,0:T(8,128)(2,1)S(1)} %get-tuple-element.149), channel_id=1, source_target_pairs={{0,8},{4,12},{8,0},{12,4},{1,9},{5,13},{9,1},{13,5},{2,10},{6,14},... | collective-permute-start | bytes 442376 | tf_op jit(solution)/shard_map/ppermute | solution.py:589
  7.9 2.6 %shard_map.238 = (bf16[560,512]{1,0:T(8,128)(2,1)}, f32[544,128]{1,0:T(8,128)S(1)}, f32[2,128]{1,0:T(2,128)S(1)}) custom-call(bf16[5,5,6,512]{3,2,1,0:T(8,128)(2,1)S(1)} %bitcast.76, bf16[7,7,2,512]{3,2,1,0:T(2,128)(2,1)S(1)} %bitcast.80, bf16[9,9,2,512]{3,2,1,0:T(2,128)(2,1)S(1)} %bitcast.79, f32[4,32]{1,0:T(4,128)S(1)} %copy-done.13, ...), custom_call_target="tpu_custom_call" | custom-call | tf_op jit(solution)/shard_map/pallas_call | solution.py:565
  11.1 1.5 collective-permute-start.6
  12.6 2.1 %collective-permute-done.3 = bf16[1,9,32,256]{3,2,1,0:T(8,128)(2,1)S(1)} collective-permute-done((bf16[1,9,32,256]{3,2,1,0:T(8,128)(2,1)S(1)}, bf16[1,9,32,256]{3,2,1,0:T(8,128)(2,1)S(1)}, u32[]{:S(2)}, u32[]{:S(2)}) %collective-permute-start.3) | collective-permute-done | bytes 147488 | tf_op jit(solution)/shard_map/ppermute | solution.py:589
  14.7 0.7 collective-permute-start.4
  15.4 1.2 shard_map.239.refs_6_
  16.6 6.0 %collective-permute-done.4 = bf16[2,9,32,256]{3,2,1,0:T(8,128)(2,1)S(1)} collective-permute-done((bf16[2,9,32,256]{3,2,1,0:T(8,128)(2,1)S(1)}, bf16[2,9,32,256]{3,2,1,0:T(8,128)(2,1)S(1)}, u32[]{:S(2)}, u32[]{:S(2)}) %collective-permute-start.4) | collective-permute-done | bytes 294944 | tf_op jit(solution)/shard_map/ppermute | solution.py:589
  22.7 2.2 %collective-permute-done.5.refs_17_.refs_16_.refs_5_ = bf16[560,512]{1,0:T(8,128)(2,1)S(1)} collective-permute-done((bf16[560,512]{1,0:T(8,128)(2,1)}, bf16[560,512]{1,0:T(8,128)(2,1)S(1)}, u32[]{:S(2)}, u32[]{:S(2)}) %collective-permute-start.5) | collective-permute-done | bytes 573472 | tf_op jit(solution)/shard_map/ppermute | solution.py:589
  25.2 1.5 collective-permute-start.10
  26.7 1.5 collective-permute-start.8
  28.2 2.2 %collective-permute-start.19 = (bf16[1,9,32,256]{3,2,1,0:T(8,128)(2,1)S(1)}, bf16[1,9,32,256]{3,2,1,0:T(8,128)(2,1)S(1)}, u32[]{:S(2)}, u32[]{:S(2)}) collective-permute-start(bf16[1,9,32,256]{3,2,1,0:T(8,128)(2,1)S(1)} %get-tuple-element.83), channel_id=1, source_target_pairs={{0,8},{4,12},{8,0},{12,4},{1,9},{5,13},{9,1},{13,5},{2,10},{6,14},... | collective-permute-start | bytes 442376 | tf_op jit(solution)/shard_map/ppermute | solution.py:589
  30.6 4.8 %collective-permute-done.10.refs_11_.refs_10_ = bf16[3,9,32,256]{3,2,1,0:T(8,128)(2,1)S(1)} collective-permute-done((bf16[3,9,32,256]{3,2,1,0:T(8,128)(2,1)S(1)}, bf16[3,9,32,256]{3,2,1,0:T(8,128)(2,1)S(1)}, u32[]{:S(2)}, u32[]{:S(2)}) %collective-permute-start.10) | collective-permute-done | bytes 442400 | tf_op jit(solution)/shard_map/ppermute | solution.py:589
  35.4 2.1 %collective-permute-start.17 = (bf16[1,9,32,512]{3,2,1,0:T(8,128)(2,1)S(1)}, bf16[1,9,32,512]{3,2,1,0:T(8,128)(2,1)S(1)}, u32[]{:S(2)}, u32[]{:S(2)}) collective-permute-start(bf16[1,9,32,512]{3,2,1,0:T(8,128)(2,1)S(1)} %bitcast.72), channel_id=1, source_target_pairs={{0,2},{2,0},{1,3},{3,1},{4,6},{6,4},{5,7},{7,5},{8,10},{10,8},{9,1... | collective-permute-start | bytes 884744 | tf_op jit(solution)/shard_map/ppermute | solution.py:589
  37.7 1.7 collective-permute-start.12
  39.6 1.6 collective-permute-start.20
  41.3 6.8 %collective-permute-done.12.refs_13_.refs_12_ = bf16[3,9,16,256]{3,2,1,0:T(8,128)(2,1)S(1)} collective-permute-done((bf16[3,9,16,256]{3,2,1,0:T(8,128)(2,1)S(1)}, bf16[3,9,16,256]{3,2,1,0:T(8,128)(2,1)S(1)}, u32[]{:S(2)}, u32[]{:S(2)}) %collective-permute-start.12) | collective-permute-done | bytes 221216 | tf_op jit(solution)/shard_map/ppermute | solution.py:589
  49.2 0.8 collective-permute-start.24
  50.0 0.8 collective-permute-done.14.refs_14_.refs_13_
  50.8 1.7 collective-permute-start.22
  54.0 6.6 %shard_map.240 = (f32[544,512]{1,0:T(8,128)}, f32[32,2,640]{2,1,0:T(2,128)}) custom-call(bf16[560,512]{1,0:T(8,128)(2,1)} %get-tuple-element.99.refs_0_.refs_5_.refs_4_, f32[544,128]{1,0:T(8,128)} %copy-done, f32[2,128]{1,0:T(2,128)S(1)} %get-tuple-element.75.refs_2_, bf16[1,9,32,512]{3,2,1,0:T(8,128)(2,1)} %bitcast.88, bf16[1,9,32,512]{3,2,1,0:T(8,128)(2,1)} %copy-done.34, ...), custom_call_target="tpu_custom_call" | custom-call | tf_op jit(solution)/shard_map/pallas_call | solution.py:565
  60.6 5.7 %all-to-all-start = ((f32[32,2,640]{2,1,0:T(2,128)}), f32[32,2,640]{2,1,0:T(2,128)S(1)}, u32[]{:S(2)}, u32[]{:S(2)}) async-start(f32[32,2,640]{2,1,0:T(2,128)} %get-tuple-element.81), calls=%async_computation | async-start | bytes 327680 | tf_op jit(solution)/shard_map/all_to_all | solution.py:813
  67.4 6.8 %collective-permute-done.26.refs_13_.refs_15_ = bf16[3,9,32,256]{3,2,1,0:T(8,128)(2,1)} collective-permute-done((bf16[3,9,32,256]{3,2,1,0:T(8,128)(2,1)S(1)}, bf16[3,9,32,256]{3,2,1,0:T(8,128)(2,1)}, u32[]{:S(2)}, u32[]{:S(2)}) %collective-permute-start.26) | collective-permute-done | bytes 442400 | tf_op jit(solution)/shard_map/ppermute | solution.py:593
  75.4 1.8 collective-permute-done.18.refs_6_.refs_8_
  77.1 2.0 %collective-permute-start.28 = (bf16[560,512]{1,0:T(8,128)(2,1)S(1)}, bf16[560,512]{1,0:T(8,128)(2,1)S(1)}, u32[]{:S(2)}, u32[]{:S(2)}) collective-permute-start(bf16[560,512]{1,0:T(8,128)(2,1)S(1)} %copy-done.17), channel_id=1, source_target_pairs={{0,18},{2,16},{16,2},{18,0},{1,19},{3,17},{17,3},{19,1},{4,22},{6,... | collective-permute-start | bytes 1720328 | tf_op jit(solution)/shard_map/ppermute | solution.py:593
  79.2 0.8 copy-done.30
  79.9 7.0 %shard_map.241 = (bf16[544,512]{1,0:T(8,128)(2,1)}, f32[544,512]{1,0:T(8,128)}, f32[4,512]{1,0:T(4,128)S(1)}, f32[4,512]{1,0:T(4,128)S(1)}, f32[32,512]{1,0:T(8,128)S(1)}, /*index=5*/f32[32,2,512]{2,1,0:T(2,128)}) custom-call(f32[544,512]{1,0:T(8,128)} %get-tuple-element.80.refs_0_.refs_1_.refs_4_, f32[32,2,640]{2,1,0:T(2,128)S(1)} %all-to-all-done.refs_1_, ...), custom_call_target="tpu_custom_call" | custom-call | tf_op jit(solution)/shard_map/pallas_call | solution.py:565
  86.9 4.3 %all-to-all-start.1 = ((f32[32,2,512]{2,1,0:T(2,128)}), f32[32,2,512]{2,1,0:T(2,128)S(1)}, u32[]{:S(2)}, u32[]{:S(2)}) async-start(f32[32,2,512]{2,1,0:T(2,128)} %get-tuple-element.91.refs_18_), calls=%async_computation.1 | async-start | bytes 262144 | tf_op jit(solution)/shard_map/all_to_all | solution.py:813
  91.3 9.5 %shard_map.242 = (bf16[2,544,512]{2,1,0:T(8,128)(2,1)}, bf16[9,512,512]{2,1,0:T(8,128)(2,1)}) custom-call(f32[4,512]{1,0:T(4,128)S(1)} %get-tuple-element.89.refs_0_.refs_2_, f32[4,512]{1,0:T(4,128)S(1)} %get-tuple-element.93.refs_1_.refs_3_.refs_2_, bf16[1,9,32,512]{3,2,1,0:T(8,128)(2,1)} %bitcast.89, bf16[1,9,32,512]{3,2,1,0:T(8,128)(2,1)} %copy-done.34, ...), custom_call_target="tpu_custom_call" | custom-call | tf_op jit(solution)/shard_map/pallas_call | solution.py:565
  100.8 3.6 %shard_map.243 = (bf16[544,512]{1,0:T(8,128)(2,1)}, f32[544,512]{1,0:T(8,128)}, f32[4,512]{1,0:T(4,128)S(1)}, f32[32,2,512]{2,1,0:T(2,128)}) custom-call(f32[544,512]{1,0:T(8,128)} %get-tuple-element.90.refs_0_.refs_4_, f32[32,2,512]{2,1,0:T(2,128)S(1)} %all-to-all-done.1.refs_1_, f32[32,512]{1,0:T(8,128)S(1)} %get-tuple-element.92.refs_2_, ...), custom_call_target="tpu_custom_call" | custom-call | tf_op jit(solution)/shard_map/pallas_call | solution.py:565
  104.4 5.7 %all-to-all-start.2 = ((f32[32,2,512]{2,1,0:T(2,128)}), f32[32,2,512]{2,1,0:T(2,128)S(1)}, u32[]{:S(2)}, u32[]{:S(2)}) async-start(f32[32,2,512]{2,1,0:T(2,128)} %get-tuple-element.96.refs_4_), calls=%async_computation.2 | async-start | bytes 262144 | tf_op jit(solution)/shard_map/all_to_all | solution.py:813
  110.1 0.8 copy-done.25
  110.9 5.6 %shard_map.244.refs_6_ = bf16[1,544,512]{2,1,0:T(8,128)(2,1)S(1)} custom-call(f32[4,512]{1,0:T(4,128)S(1)} %get-tuple-element.89.refs_0_.refs_2_, f32[4,512]{1,0:T(4,128)S(1)} %get-tuple-element.93.refs_1_.refs_3_.refs_2_, bf16[9,512,512]{2,1,0:T(8,128)(2,1)} %get-tuple-element.98.refs_2_.refs_4_, bf16[560,512]{1,0:T(8,128)(2,1)} %copy-done.25, ...), custom_call_target="tpu_custom_call" | custom-call | tf_op jit(solution)/shard_map/pallas_call | solution.py:565
  116.5 0.8 copy-done.4
  117.3 1.0 all-to-all-done.2.refs_1_
  118.3 2.6 %shard_map.245 = (f32[2,512]{1,0:T(2,128)S(1)}, bf16[2,64,640]{2,1,0:T(8,128)(2,1)S(1)}, bf16[2,64,640]{2,1,0:T(8,128)(2,1)S(1)}, bf16[2,64,640]{2,1,0:T(8,128)(...) custom-call(f32[4,512]{1,0:T(4,128)S(1)} %get-tuple-element.95.refs_0_, ...), custom_call_target="tpu_custom_call" | custom-call | tf_op jit(solution)/shard_map/pallas_call | solution.py:565
  120.9 0.8 collective-permute-start.29
  121.8 1.5 collective-permute-start.30
  123.2 1.2 collective-permute-start.31
  124.5 7.3 %shard_map.246 = (f32[544,512]{1,0:T(8,128)}, f32[32,2,512]{2,1,0:T(2,128)}) custom-call(bf16[544,512]{1,0:T(8,128)(2,1)} %get-tuple-element.100.refs_0_, f32[544,512]{1,0:T(8,128)} %get-tuple-element.80.refs_0_.refs_1_.refs_4_, f32[4,512]{1,0:T(4,128)S(1)} %get-tuple-element.89.refs_0_.refs_2_, f32[4,512]{1,0:T(4,128)S(1)} %get-tuple-element.93.refs_1_.refs_3_.refs_2_, ...), custom_call_target="tpu_custom_call" | custom-call | tf_op jit(solution)/shard_map/pallas_call | solution.py:565
  131.8 5.1 %all-to-all-start.3 = ((f32[32,2,512]{2,1,0:T(2,128)}), f32[32,2,512]{2,1,0:T(2,128)S(1)}, u32[]{:S(2)}, u32[]{:S(2)}) async-start(f32[32,2,512]{2,1,0:T(2,128)} %get-tuple-element.105), calls=%async_computation.3 | async-start | bytes 262144 | tf_op jit(solution)/shard_map/all_to_all | solution.py:813
  136.9 7.0 %shard_map.247 = (bf16[4,9,16,512]{3,2,1,0:T(8,128)(2,1)}, f32[4,9,16,512]{3,2,1,0:T(8,128)}) custom-call(bf16[2,64,640]{2,1,0:T(8,128)(2,1)S(1)} %get-tuple-element.107.refs_0_, bf16[2,64,640]{2,1,0:T(8,128)(2,1)S(1)} %collective-permute-done.29.refs_1_, bf16[2,64,640]{2,1,0:T(8,128)(2,1)S(1)} %collective-permute-done.30.refs_2_, ...), custom_call_target="tpu_custom_call" | custom-call | tf_op jit(solution)/shard_map/pallas_call | solution.py:565
  143.9 1.0 all-to-all-done.3.refs_1_
  145.2 2.6 %shard_map.248 = (f32[2,512]{1,0:T(2,128)S(1)}, bf16[2,64,640]{2,1,0:T(8,128)(2,1)S(1)}, bf16[2,64,640]{2,1,0:T(8,128)(2,1)S(1)}, bf16[2,64,640]{2,1,0:T(8,128)(...) custom-call(f32[4,512]{1,0:T(4,128)S(1)} %get-tuple-element.89.refs_0_.refs_2_, ...), custom_call_target="tpu_custom_call" | custom-call | tf_op jit(solution)/shard_map/pallas_call | solution.py:565
  148.4 1.5 collective-permute-start.33
  149.9 1.4 collective-permute-start.34
  152.2 2.4 %collective-permute-start.37 = (bf16[9,16,512]{2,1,0:T(8,128)(2,1)S(1)}, bf16[9,16,512]{2,1,0:T(8,128)(2,1)S(1)}, u32[]{:S(2)}, u32[]{:S(2)}) collective-permute-start(bf16[9,16,512]{2,1,0:T(8,128)(2,1)S(1)} %get-tuple-element.144.refs_9_), channel_id=1, source_target_pairs={{0,8},{4,12},{8,0},{12,4},{1,9},{5,13},{9,1},{13,5},{2,10},{6,14},... | collective-permute-start | bytes 442376 | tf_op jit(solution)/shard_map/ppermute | solution.py:589
  154.9 2.4 %collective-permute-start.38 = (bf16[9,16,512]{2,1,0:T(8,128)(2,1)S(1)}, bf16[9,16,512]{2,1,0:T(8,128)(2,1)S(1)}, u32[]{:S(2)}, u32[]{:S(2)}) collective-permute-start(bf16[9,16,512]{2,1,0:T(8,128)(2,1)S(1)} %get-tuple-element.143.refs_10_), channel_id=1, source_target_pairs={{0,12},{4,8},{8,4},{12,0},{1,13},{5,9},{9,5},{13,1},{2,14},{6,10},... | collective-permute-start | bytes 442376 | tf_op jit(solution)/shard_map/ppermute | solution.py:589
  157.3 0.8 collective-permute-done.33.refs_2_
  158.1 0.7 copy-done.40
  158.8 7.8 %shard_map.249 = (bf16[4,9,16,512]{3,2,1,0:T(8,128)(2,1)}, f32[4,9,16,512]{3,2,1,0:T(8,128)}) custom-call(bf16[2,64,640]{2,1,0:T(8,128)(2,1)S(1)} %get-tuple-element.113.refs_0_, bf16[2,64,640]{2,1,0:T(8,128)(2,1)S(1)} %collective-permute-done.32.refs_1_, bf16[2,64,640]{2,1,0:T(8,128)(2,1)S(1)} %collective-permute-done.33.refs_2_, ...), custom_call_target="tpu_custom_call" | custom-call | tf_op jit(solution)/shard_map/pallas_call | solution.py:565
  166.7 2.2 %collective-permute-done.39 = bf16[4,9,16,512]{3,2,1,0:T(8,128)(2,1)S(1)} collective-permute-done((bf16[4,9,16,512]{3,2,1,0:T(8,128)(2,1)}, bf16[4,9,16,512]{3,2,1,0:T(8,128)(2,1)S(1)}, u32[]{:S(2)}, u32[]{:S(2)}) %collective-permute-start.39) | collective-permute-done | bytes 589856 | tf_op jit(solution)/shard_map/ppermute | solution.py:589
  168.9 1.4 fusion.11
  170.3 1.6 collective-permute-start.40
  171.9 2.4 %collective-permute-start.41 = (bf16[9,16,512]{2,1,0:T(8,128)(2,1)S(1)}, bf16[9,16,512]{2,1,0:T(8,128)(2,1)S(1)}, u32[]{:S(2)}, u32[]{:S(2)}) collective-permute-start(bf16[9,16,512]{2,1,0:T(8,128)(2,1)S(1)} %get-tuple-element.141.refs_6_), channel_id=1, source_target_pairs={{0,8},{4,12},{8,0},{12,4},{1,9},{5,13},{9,1},{13,5},{2,10},{6,14},... | collective-permute-start | bytes 442376 | tf_op jit(solution)/shard_map/ppermute | solution.py:589
  174.8 8.4 %shard_map.250 = (bf16[5,5,6,512]{3,2,1,0:T(8,128)(2,1)}, bf16[7,7,2,512]{3,2,1,0:T(2,128)(2,1)}, bf16[9,9,2,512]{3,2,1,0:T(2,128)(2,1)}, f32[5,5,6,512]{3,2,1,0...) custom-call(bf16[544,512]{1,0:T(8,128)(2,1)} %get-tuple-element.111.refs_0_, ...), custom_call_target="tpu_custom_call" | custom-call | tf_op jit(solution)/shard_map/pallas_call | solution.py:565
  183.4 1.5 collective-permute-start.44
  184.9 0.9 collective-permute-done.41
  186.0 1.5 collective-permute-start.43
  187.5 0.7 multiply_subtract_fusion
  188.2 1.9 collective-permute-done.44
  190.1 1.6 collective-permute-done.43
  191.8 2.7 %fusion.5 = (f32[2,3,3,512,32]{3,4,2,1,0:T(8,128)}, f32[2,3,3,512,32]{3,4,2,1,0:T(8,128)}, f32[2,3,3,512,32]{3,4,2,1,0:T(8,128)}) fusion(f32[2,3,3,512,32]{3,4,2,1,0:T(8,128)S(1)} %copy-done.37, bf16[1,3,3,16,512]{4,3,2,1,0:T(8,128)(2,1)S(1)} %bitcast.91, bf16[1,3,3,16,512]{4,3,2,1,0:T(8,128)(2,1)S(1)} %bitcast.90, ...), kind=kLoop, calls=%fused_computation.10 | loop fusion | flops 6488064 | bytes 7667712 | tf_op jit(solution)/shard_map/transpose | solution.py:965
  (151 shorter events, 9.3 us)
Async XLA Ops:
  2.1 13.4 %copy-start.6 = (bf16[6,5,5,512]{3,0,2,1:T(8,128)(2,1)S(1)}, bf16[6,5,5,512]{3,0,2,1:T(8,128)(2,1)}, u32[]{:S(2)}) copy-start(bf16[6,5,5,512]{3,0,2,1:T(8,128)(2,1)} %param.21) | copy-start | bytes 460804
  2.1 13.3 %copy-start.7 = (bf16[2,9,9,512]{3,0,2,1:T(2,128)(2,1)S(1)}, bf16[2,9,9,512]{3,0,2,1:T(2,128)(2,1)}, u32[]{:S(2)}) copy-start(bf16[2,9,9,512]{3,0,2,1:T(2,128)(2,1)} %param.23) | copy-start | bytes 497668
  2.1 13.3 %copy-start.10 = (bf16[2,7,7,512]{3,0,2,1:T(2,128)(2,1)S(1)}, bf16[2,7,7,512]{3,0,2,1:T(2,128)(2,1)}, u32[]{:S(2)}) copy-start(bf16[2,7,7,512]{3,0,2,1:T(2,128)(2,1)} %param.22) | copy-start | bytes 301060
  2.2 26.0 %copy-start.24 = (bf16[1,3,3,32,512]{4,3,2,1,0:T(8,128)(2,1)}, bf16[1,3,3,32,512]{4,3,2,1,0:T(8,128)(2,1)S(1)}, u32[]{:S(2)}) copy-start(bf16[1,3,3,32,512]{4,3,2,1,0:T(8,128)(2,1)S(1)} %get-tuple-element.151) | copy-start | bytes 884740
  2.2 12.5 %collective-permute-start.1 = (bf16[1,9,32,512]{3,2,1,0:T(8,128)(2,1)S(1)}, bf16[1,9,32,512]{3,2,1,0:T(8,128)(2,1)S(1)}, u32[]{:S(2)}, u32[]{:S(2)}) collective-permute-start(bf16[1,9,32,512]{3,2,1,0:T(8,128)(2,1)S(1)} %bitcast.86), channel_id=1, source_target_pairs={{0,2},{2,0},{1,3},{3,1},{4,6},{6,4},{5,7},{7,5},{8,10},{10,8},{9,1... | collective-permute-start | bytes 884744 | tf_op jit(solution)/shard_map/ppermute | solution.py:589
  5.2 9.4 %collective-permute-start.3 = (bf16[1,9,32,256]{3,2,1,0:T(8,128)(2,1)S(1)}, bf16[1,9,32,256]{3,2,1,0:T(8,128)(2,1)S(1)}, u32[]{:S(2)}, u32[]{:S(2)}) collective-permute-start(bf16[1,9,32,256]{3,2,1,0:T(8,128)(2,1)S(1)} %get-tuple-element.149), channel_id=1, source_target_pairs={{0,8},{4,12},{8,0},{12,4},{1,9},{5,13},{9,1},{13,5},{2,10},{6,14},... | collective-permute-start | bytes 442376 | tf_op jit(solution)/shard_map/ppermute | solution.py:589
  10.5 14.4 %collective-permute-start.5 = (bf16[560,512]{1,0:T(8,128)(2,1)}, bf16[560,512]{1,0:T(8,128)(2,1)S(1)}, u32[]{:S(2)}, u32[]{:S(2)}) collective-permute-start(bf16[560,512]{1,0:T(8,128)(2,1)} %get-tuple-element.99.refs_0_.refs_5_.refs_4_), channel_id=1, source_target_pairs={{0,2},{2,0},{1,3},{3,1},{4,6},{6,4},{5,7},{7,5},{8,10},{10,8},{9,1... | collective-permute-start | bytes 1720328 | tf_op jit(solution)/shard_map/ppermute | solution.py:589
  11.1 14.1 %collective-permute-start.6 = (bf16[560,512]{1,0:T(8,128)(2,1)}, bf16[560,512]{1,0:T(8,128)(2,1)S(1)}, u32[]{:S(2)}, u32[]{:S(2)}) collective-permute-start(bf16[560,512]{1,0:T(8,128)(2,1)} %get-tuple-element.99.refs_0_.refs_5_.refs_4_), channel_id=1, source_target_pairs={{0,16},{16,0},{1,17},{17,1},{2,18},{18,2},{3,19},{19,3},{4,20},{20... | collective-permute-start | bytes 1720328 | tf_op jit(solution)/shard_map/ppermute | solution.py:589
  14.7 22.8 %copy-start.31 = (bf16[1,9,32,512]{3,2,1,0:T(8,128)(2,1)}, bf16[1,9,32,512]{3,2,1,0:T(8,128)(2,1)S(1)}, u32[]{:S(2)}) copy-start(bf16[1,9,32,512]{3,2,1,0:T(8,128)(2,1)S(1)} %collective-permute-done.1.refs_5_.refs_4_) | copy-start | bytes 884740
  14.7 7.9 %collective-permute-start.4 = (bf16[2,9,32,256]{3,2,1,0:T(8,128)(2,1)S(1)}, bf16[2,9,32,256]{3,2,1,0:T(8,128)(2,1)S(1)}, u32[]{:S(2)}, u32[]{:S(2)}) collective-permute-start(bf16[2,9,32,256]{3,2,1,0:T(8,128)(2,1)S(1)} %pad_maximum_fusion.2), channel_id=1, source_target_pairs={{0,4},{4,0},{8,12},{12,8},{1,5},{5,1},{9,13},{13,9},{2,6},{6,2},{1... | collective-permute-start | bytes 884744 | tf_op jit(solution)/shard_map/ppermute | solution.py:589
  22.7 26.5 %copy-start.20 = (bf16[3,9,32,256]{3,2,1,0:T(8,128)(2,1)}, bf16[3,9,32,256]{3,2,1,0:T(8,128)(2,1)S(1)}, u32[]{:S(2)}) copy-start(bf16[3,9,32,256]{3,2,1,0:T(8,128)(2,1)S(1)} %pad_maximum_fusion.refs_7_.refs_6_) | copy-start | bytes 1327108
  24.9 24.3 %copy-start.15 = (bf16[560,512]{1,0:T(8,128)(2,1)}, bf16[560,512]{1,0:T(8,128)(2,1)S(1)}, u32[]{:S(2)}) copy-start(bf16[560,512]{1,0:T(8,128)(2,1)S(1)} %collective-permute-done.5.refs_17_.refs_16_.refs_5_) | copy-start | bytes 1720324
  25.2 24.0 %copy-start.16 = (bf16[560,512]{1,0:T(8,128)(2,1)}, bf16[560,512]{1,0:T(8,128)(2,1)S(1)}, u32[]{:S(2)}) copy-start(bf16[560,512]{1,0:T(8,128)(2,1)S(1)} %collective-permute-done.6.refs_18_.refs_17_.refs_6_) | copy-start | bytes 1720324
  25.2 10.2 %collective-permute-start.10 = (bf16[3,9,32,256]{3,2,1,0:T(8,128)(2,1)S(1)}, bf16[3,9,32,256]{3,2,1,0:T(8,128)(2,1)S(1)}, u32[]{:S(2)}, u32[]{:S(2)}) collective-permute-start(bf16[3,9,32,256]{3,2,1,0:T(8,128)(2,1)S(1)} %pad_maximum_fusion.refs_7_.refs_6_), channel_id=1, source_target_pairs={{0,16},{16,0},{1,17},{17,1},{2,18},{18,2},{3,19},{19,3},{4,20},{20... | collective-permute-start | bytes 1327112 | tf_op jit(solution)/shard_map/ppermute | solution.py:589
  26.7 11.0 %collective-permute-start.8 = (bf16[3,9,32,256]{3,2,1,0:T(8,128)(2,1)S(1)}, bf16[3,9,32,256]{3,2,1,0:T(8,128)(2,1)S(1)}, u32[]{:S(2)}, u32[]{:S(2)}) collective-permute-start(bf16[3,9,32,256]{3,2,1,0:T(8,128)(2,1)S(1)} %pad_maximum_fusion.refs_7_.refs_6_), channel_id=1, source_target_pairs={{0,2},{2,0},{1,3},{3,1},{4,6},{6,4},{5,7},{7,5},{8,10},{10,8},{9,1... | collective-permute-start | bytes 1327112 | tf_op jit(solution)/shard_map/ppermute | solution.py:589
  28.2 11.4 %collective-permute-start = (bf16[1,9,32,512]{3,2,1,0:T(8,128)(2,1)S(1)}, bf16[1,9,32,512]{3,2,1,0:T(8,128)(2,1)S(1)}, u32[]{:S(2)}, u32[]{:S(2)}) collective-permute-start(bf16[1,9,32,512]{3,2,1,0:T(8,128)(2,1)S(1)} %bitcast.87), channel_id=1, source_target_pairs={{0,1},{1,0},{2,3},{3,2},{4,5},{5,4},{6,7},{7,6},{8,9},{9,8},{10,11... | collective-permute-start | bytes 884744 | tf_op jit(solution)/shard_map/ppermute | solution.py:589
  28.2 11.3 %collective-permute-start.19 = (bf16[1,9,32,256]{3,2,1,0:T(8,128)(2,1)S(1)}, bf16[1,9,32,256]{3,2,1,0:T(8,128)(2,1)S(1)}, u32[]{:S(2)}, u32[]{:S(2)}) collective-permute-start(bf16[1,9,32,256]{3,2,1,0:T(8,128)(2,1)S(1)} %get-tuple-element.83), channel_id=1, source_target_pairs={{0,8},{4,12},{8,0},{12,4},{1,9},{5,13},{9,1},{13,5},{2,10},{6,14},... | collective-permute-start | bytes 442376 | tf_op jit(solution)/shard_map/ppermute | solution.py:589
  30.4 10.9 %collective-permute-start.2 = (bf16[1,9,32,512]{3,2,1,0:T(8,128)(2,1)S(1)}, bf16[1,9,32,512]{3,2,1,0:T(8,128)(2,1)S(1)}, u32[]{:S(2)}, u32[]{:S(2)}) collective-permute-start(bf16[1,9,32,512]{3,2,1,0:T(8,128)(2,1)S(1)} %collective-permute-done.1.refs_5_.refs_4_), channel_id=1, source_target_pairs={{0,1},{1,0},{2,3},{3,2},{4,5},{5,4},{6,7},{7,6},{8,9},{9,8},{10,11... | collective-permute-start | bytes 884744 | tf_op jit(solution)/shard_map/ppermute | solution.py:589
  35.4 13.8 %copy-start.22 = (bf16[3,9,32,256]{3,2,1,0:T(8,128)(2,1)}, bf16[3,9,32,256]{3,2,1,0:T(8,128)(2,1)S(1)}, u32[]{:S(2)}) copy-start(bf16[3,9,32,256]{3,2,1,0:T(8,128)(2,1)S(1)} %collective-permute-done.10.refs_11_.refs_10_) | copy-start | bytes 1327108
  35.4 13.2 %collective-permute-start.17 = (bf16[1,9,32,512]{3,2,1,0:T(8,128)(2,1)S(1)}, bf16[1,9,32,512]{3,2,1,0:T(8,128)(2,1)S(1)}, u32[]{:S(2)}, u32[]{:S(2)}) collective-permute-start(bf16[1,9,32,512]{3,2,1,0:T(8,128)(2,1)S(1)} %bitcast.72), channel_id=1, source_target_pairs={{0,2},{2,0},{1,3},{3,1},{4,6},{6,4},{5,7},{7,5},{8,10},{10,8},{9,1... | collective-permute-start | bytes 884744 | tf_op jit(solution)/shard_map/ppermute | solution.py:589
  37.7 15.4 %copy-start.23 = (bf16[3,9,32,256]{3,2,1,0:T(8,128)(2,1)}, bf16[3,9,32,256]{3,2,1,0:T(8,128)(2,1)S(1)}, u32[]{:S(2)}) copy-start(bf16[3,9,32,256]{3,2,1,0:T(8,128)(2,1)S(1)} %collective-permute-done.8.refs_9_.refs_8_) | copy-start | bytes 1327108
  37.7 10.3 %collective-permute-start.12 = (bf16[3,9,16,256]{3,2,1,0:T(8,128)(2,1)S(1)}, bf16[3,9,16,256]{3,2,1,0:T(8,128)(2,1)S(1)}, u32[]{:S(2)}, u32[]{:S(2)}) collective-permute-start(bf16[3,9,16,256]{3,2,1,0:T(8,128)(2,1)S(1)} %slice.89), channel_id=1, source_target_pairs={{0,2},{2,0},{1,3},{3,1},{4,6},{6,4},{5,7},{7,5},{8,10},{10,8},{9,1... | collective-permute-start | bytes 663560 | tf_op jit(solution)/shard_map/ppermute | solution.py:589
  39.5 8.6 %collective-permute-start.13 = (bf16[3,9,16,256]{3,2,1,0:T(8,128)(2,1)S(1)}, bf16[3,9,16,256]{3,2,1,0:T(8,128)(2,1)S(1)}, u32[]{:S(2)}, u32[]{:S(2)}) collective-permute-start(bf16[3,9,16,256]{3,2,1,0:T(8,128)(2,1)S(1)} %slice.90), channel_id=1, source_target_pairs={{0,16},{16,0},{1,17},{17,1},{2,18},{18,2},{3,19},{19,3},{4,20},{20... | collective-permute-start | bytes 663560 | tf_op jit(solution)/shard_map/ppermute | solution.py:589
  39.6 13.5 %copy-start.34 = (bf16[1,9,32,512]{3,2,1,0:T(8,128)(2,1)}, bf16[1,9,32,512]{3,2,1,0:T(8,128)(2,1)S(1)}, u32[]{:S(2)}) copy-start(bf16[1,9,32,512]{3,2,1,0:T(8,128)(2,1)S(1)} %collective-permute-done.refs_4_.refs_3_) | copy-start | bytes 884740
  39.6 9.0 %collective-permute-start.20 = (bf16[2,9,32,256]{3,2,1,0:T(8,128)(2,1)S(1)}, bf16[2,9,32,256]{3,2,1,0:T(8,128)(2,1)S(1)}, u32[]{:S(2)}, u32[]{:S(2)}) collective-permute-start(bf16[2,9,32,256]{3,2,1,0:T(8,128)(2,1)S(1)} %pad_maximum_fusion.3), channel_id=1, source_target_pairs={{0,4},{4,0},{8,12},{12,8},{1,5},{5,1},{9,13},{13,9},{2,6},{6,2},{1... | collective-permute-start | bytes 884744 | tf_op jit(solution)/shard_map/ppermute | solution.py:589
  41.3 7.9 %collective-permute-start.7 = (bf16[3,9,32,256]{3,2,1,0:T(8,128)(2,1)S(1)}, bf16[3,9,32,256]{3,2,1,0:T(8,128)(2,1)S(1)}, u32[]{:S(2)}, u32[]{:S(2)}) collective-permute-start(bf16[3,9,32,256]{3,2,1,0:T(8,128)(2,1)S(1)} %pad_maximum_fusion.refs_7_.refs_6_), channel_id=1, source_target_pairs={{0,1},{1,0},{2,3},{3,2},{4,5},{5,4},{6,7},{7,6},{8,9},{9,8},{10,11... | collective-permute-start | bytes 1327112 | tf_op jit(solution)/shard_map/ppermute | solution.py:589
  48.1 5.0 %collective-permute-start.11 = (bf16[3,9,32,256]{3,2,1,0:T(8,128)(2,1)S(1)}, bf16[3,9,32,256]{3,2,1,0:T(8,128)(2,1)S(1)}, u32[]{:S(2)}, u32[]{:S(2)}) collective-permute-start(bf16[3,9,32,256]{3,2,1,0:T(8,128)(2,1)S(1)} %collective-permute-done.10.refs_11_.refs_10_), channel_id=1, source_target_pairs={{0,1},{1,0},{2,3},{3,2},{4,5},{5,4},{6,7},{7,6},{8,9},{9,8},{10,11... | collective-permute-start | bytes 1327112 | tf_op jit(solution)/shard_map/ppermute | solution.py:589
  48.1 5.0 %collective-permute-start.9 = (bf16[3,9,32,256]{3,2,1,0:T(8,128)(2,1)S(1)}, bf16[3,9,32,256]{3,2,1,0:T(8,128)(2,1)S(1)}, u32[]{:S(2)}, u32[]{:S(2)}) collective-permute-start(bf16[3,9,32,256]{3,2,1,0:T(8,128)(2,1)S(1)} %collective-permute-done.8.refs_9_.refs_8_), channel_id=1, source_target_pairs={{0,1},{1,0},{2,3},{3,2},{4,5},{5,4},{6,7},{7,6},{8,9},{9,8},{10,11... | collective-permute-start | bytes 1327112 | tf_op jit(solution)/shard_map/ppermute | solution.py:589
  48.6 2.2 %collective-permute-start.14 = (bf16[3,9,16,256]{3,2,1,0:T(8,128)(2,1)S(1)}, bf16[3,9,16,256]{3,2,1,0:T(8,128)(2,1)S(1)}, u32[]{:S(2)}, u32[]{:S(2)}) collective-permute-start(bf16[3,9,16,256]{3,2,1,0:T(8,128)(2,1)S(1)} %collective-permute-done.12.refs_13_.refs_12_), channel_id=1, source_target_pairs={{0,1},{1,0},{2,3},{3,2},{4,5},{5,4},{6,7},{7,6},{8,9},{9,8},{10,11... | collective-permute-start | bytes 663560 | tf_op jit(solution)/shard_map/ppermute | solution.py:589
  48.7 3.9 %collective-permute-start.15 = (bf16[3,9,16,256]{3,2,1,0:T(8,128)(2,1)S(1)}, bf16[3,9,16,256]{3,2,1,0:T(8,128)(2,1)S(1)}, u32[]{:S(2)}, u32[]{:S(2)}) collective-permute-start(bf16[3,9,16,256]{3,2,1,0:T(8,128)(2,1)S(1)} %collective-permute-done.13.refs_15_.refs_14_), channel_id=1, source_target_pairs={{0,1},{1,0},{2,3},{3,2},{4,5},{5,4},{6,7},{7,6},{8,9},{9,8},{10,11... | collective-permute-start | bytes 663560 | tf_op jit(solution)/shard_map/ppermute | solution.py:589
  49.2 17.4 %copy-start.21 = (bf16[3,9,32,256]{3,2,1,0:T(8,128)(2,1)}, bf16[3,9,32,256]{3,2,1,0:T(8,128)(2,1)S(1)}, u32[]{:S(2)}) copy-start(bf16[3,9,32,256]{3,2,1,0:T(8,128)(2,1)S(1)} %pad_maximum_fusion.1.refs_7_.refs_9_) | copy-start | bytes 1327108
  49.2 17.6 %collective-permute-start.24 = (bf16[3,9,32,256]{3,2,1,0:T(8,128)(2,1)S(1)}, bf16[3,9,32,256]{3,2,1,0:T(8,128)(2,1)S(1)}, u32[]{:S(2)}, u32[]{:S(2)}) collective-permute-start(bf16[3,9,32,256]{3,2,1,0:T(8,128)(2,1)S(1)} %pad_maximum_fusion.1.refs_7_.refs_9_), channel_id=1, source_target_pairs={{0,16},{16,0},{1,17},{17,1},{2,18},{18,2},{3,19},{19,3},{4,20},{20... | collective-permute-start | bytes 1327112 | tf_op jit(solution)/shard_map/ppermute | solution.py:589
  50.8 16.3 %collective-permute-start.22 = (bf16[3,9,32,256]{3,2,1,0:T(8,128)(2,1)S(1)}, bf16[3,9,32,256]{3,2,1,0:T(8,128)(2,1)}, u32[]{:S(2)}, u32[]{:S(2)}) collective-permute-start(bf16[3,9,32,256]{3,2,1,0:T(8,128)(2,1)S(1)} %pad_maximum_fusion.1.refs_7_.refs_9_), channel_id=1, source_target_pairs={{0,2},{2,0},{1,3},{3,1},{4,6},{6,4},{5,7},{7,5},{8,10},{10,8},{9,1... | collective-permute-start | bytes 1327112 | tf_op jit(solution)/shard_map/ppermute | solution.py:589
  52.6 21.6 %collective-permute-start.26 = (bf16[3,9,32,256]{3,2,1,0:T(8,128)(2,1)S(1)}, bf16[3,9,32,256]{3,2,1,0:T(8,128)(2,1)}, u32[]{:S(2)}, u32[]{:S(2)}) collective-permute-start(bf16[3,9,32,256]{3,2,1,0:T(8,128)(2,1)S(1)} %pad_maximum_fusion.1.refs_7_.refs_9_), channel_id=1, source_target_pairs={{0,18},{2,16},{16,2},{18,0},{1,19},{3,17},{17,3},{19,1},{4,22},{6,... | collective-permute-start | bytes 1327112 | tf_op jit(solution)/shard_map/ppermute | solution.py:593
  54.0 21.3 %copy-start.33 = (bf16[1,9,32,512]{3,2,1,0:T(8,128)(2,1)S(1)}, bf16[1,9,32,512]{3,2,1,0:T(8,128)(2,1)}, u32[]{:S(2)}) copy-start(bf16[1,9,32,512]{3,2,1,0:T(8,128)(2,1)} %copy-done.32) | copy-start | bytes 884740
  54.0 23.2 %copy-start.17 = (bf16[560,512]{1,0:T(8,128)(2,1)S(1)}, bf16[560,512]{1,0:T(8,128)(2,1)}, u32[]{:S(2)}) copy-start(bf16[560,512]{1,0:T(8,128)(2,1)} %get-tuple-element.99.refs_0_.refs_5_.refs_4_) | copy-start | bytes 1720324
  54.0 26.0 %copy-start.1 = (f32[544,128]{1,0:T(8,128)S(1)}, f32[544,128]{1,0:T(8,128)}, u32[]{:S(2)}) copy-start(f32[544,128]{1,0:T(8,128)} %copy-done) | copy-start | bytes 835588
  60.6 14.2 %all-to-all-start = ((f32[32,2,640]{2,1,0:T(2,128)}), f32[32,2,640]{2,1,0:T(2,128)S(1)}, u32[]{:S(2)}, u32[]{:S(2)}) async-start(f32[32,2,640]{2,1,0:T(2,128)} %get-tuple-element.81), calls=%async_computation | async-start | bytes 327680 | tf_op jit(solution)/shard_map/all_to_all | solution.py:813
  66.3 9.0 %collective-permute-start.16 = (bf16[1,9,32,512]{3,2,1,0:T(8,128)(2,1)S(1)}, bf16[1,9,32,512]{3,2,1,0:T(8,128)(2,1)}, u32[]{:S(2)}, u32[]{:S(2)}) collective-permute-start(bf16[1,9,32,512]{3,2,1,0:T(8,128)(2,1)S(1)} %bitcast.73), channel_id=1, source_target_pairs={{0,1},{1,0},{2,3},{3,2},{4,5},{5,4},{6,7},{7,6},{8,9},{9,8},{10,11... | collective-permute-start | bytes 884744 | tf_op jit(solution)/shard_map/ppermute | solution.py:589
  66.6 12.5 %collective-permute-start.21 = (bf16[3,9,32,256]{3,2,1,0:T(8,128)(2,1)S(1)}, bf16[3,9,32,256]{3,2,1,0:T(8,128)(2,1)}, u32[]{:S(2)}, u32[]{:S(2)}) collective-permute-start(bf16[3,9,32,256]{3,2,1,0:T(8,128)(2,1)S(1)} %pad_maximum_fusion.1.refs_7_.refs_9_), channel_id=1, source_target_pairs={{0,1},{1,0},{2,3},{3,2},{4,5},{5,4},{6,7},{7,6},{8,9},{9,8},{10,11... | collective-permute-start | bytes 1327112 | tf_op jit(solution)/shard_map/ppermute | solution.py:589
  66.9 12.3 %collective-permute-start.25 = (bf16[3,9,32,256]{3,2,1,0:T(8,128)(2,1)S(1)}, bf16[3,9,32,256]{3,2,1,0:T(8,128)(2,1)}, u32[]{:S(2)}, u32[]{:S(2)}) collective-permute-start(bf16[3,9,32,256]{3,2,1,0:T(8,128)(2,1)S(1)} %collective-permute-done.24.refs_11_.refs_13_), channel_id=1, source_target_pairs={{0,1},{1,0},{2,3},{3,2},{4,5},{5,4},{6,7},{7,6},{8,9},{9,8},{10,11... | collective-permute-start | bytes 1327112 | tf_op jit(solution)/shard_map/ppermute | solution.py:589
  67.1 12.0 %collective-permute-start.23 = (bf16[3,9,32,256]{3,2,1,0:T(8,128)(2,1)}, bf16[3,9,32,256]{3,2,1,0:T(8,128)(2,1)}, u32[]{:S(2)}, u32[]{:S(2)}) collective-permute-start(bf16[3,9,32,256]{3,2,1,0:T(8,128)(2,1)} %collective-permute-done.22.refs_9_.refs_11_), channel_id=1, source_target_pairs={{0,1},{1,0},{2,3},{3,2},{4,5},{5,4},{6,7},{7,6},{8,9},{9,8},{10,11... | collective-permute-start | bytes 1327112 | tf_op jit(solution)/shard_map/ppermute | solution.py:589
  74.8 4.3 %collective-permute-start.27 = (bf16[3,9,32,256]{3,2,1,0:T(8,128)(2,1)}, bf16[3,9,32,256]{3,2,1,0:T(8,128)(2,1)S(1)}, u32[]{:S(2)}, u32[]{:S(2)}) collective-permute-start(bf16[3,9,32,256]{3,2,1,0:T(8,128)(2,1)} %collective-permute-done.26.refs_13_.refs_15_), channel_id=1, source_target_pairs={{0,1},{1,0},{2,3},{3,2},{4,5},{5,4},{6,7},{7,6},{8,9},{9,8},{10,11... | collective-permute-start | bytes 1327112 | tf_op jit(solution)/shard_map/ppermute | solution.py:589
  75.3 1.8 collective-permute-start.18
  77.1 33.0 %collective-permute-start.28 = (bf16[560,512]{1,0:T(8,128)(2,1)S(1)}, bf16[560,512]{1,0:T(8,128)(2,1)S(1)}, u32[]{:S(2)}, u32[]{:S(2)}) collective-permute-start(bf16[560,512]{1,0:T(8,128)(2,1)S(1)} %copy-done.17), channel_id=1, source_target_pairs={{0,18},{2,16},{16,2},{18,0},{1,19},{3,17},{17,3},{19,1},{4,22},{6,... | collective-permute-start | bytes 1720328 | tf_op jit(solution)/shard_map/ppermute | solution.py:593
  86.9 13.8 %all-to-all-start.1 = ((f32[32,2,512]{2,1,0:T(2,128)}), f32[32,2,512]{2,1,0:T(2,128)S(1)}, u32[]{:S(2)}, u32[]{:S(2)}) async-start(f32[32,2,512]{2,1,0:T(2,128)} %get-tuple-element.91.refs_18_), calls=%async_computation.1 | async-start | bytes 262144 | tf_op jit(solution)/shard_map/all_to_all | solution.py:813
  104.4 13.9 %all-to-all-start.2 = ((f32[32,2,512]{2,1,0:T(2,128)}), f32[32,2,512]{2,1,0:T(2,128)S(1)}, u32[]{:S(2)}, u32[]{:S(2)}) async-start(f32[32,2,512]{2,1,0:T(2,128)} %get-tuple-element.96.refs_4_), calls=%async_computation.2 | async-start | bytes 262144 | tf_op jit(solution)/shard_map/all_to_all | solution.py:813
  120.9 10.9 %collective-permute-start.29 = (bf16[2,64,640]{2,1,0:T(8,128)(2,1)S(1)}, bf16[2,64,640]{2,1,0:T(8,128)(2,1)S(1)}, u32[]{:S(2)}, u32[]{:S(2)}) collective-permute-start(bf16[2,64,640]{2,1,0:T(8,128)(2,1)S(1)} %get-tuple-element.102), channel_id=1, source_target_pairs={{0,2},{2,0},{1,3},{3,1},{4,6},{6,4},{5,7},{7,5},{8,10},{10,8},{9,1... | collective-permute-start | bytes 491528 | tf_op jit(solution)/shard_map/ppermute | solution.py:589
  121.8 10.0 %collective-permute-start.30 = (bf16[2,64,640]{2,1,0:T(8,128)(2,1)S(1)}, bf16[2,64,640]{2,1,0:T(8,128)(2,1)S(1)}, u32[]{:S(2)}, u32[]{:S(2)}) collective-permute-start(bf16[2,64,640]{2,1,0:T(8,128)(2,1)S(1)} %get-tuple-element.103), channel_id=1, source_target_pairs={{0,16},{16,0},{1,17},{17,1},{2,18},{18,2},{3,19},{19,3},{4,20},{20... | collective-permute-start | bytes 491528 | tf_op jit(solution)/shard_map/ppermute | solution.py:589
  123.2 8.6 %collective-permute-start.31 = (bf16[2,64,640]{2,1,0:T(8,128)(2,1)S(1)}, bf16[2,64,640]{2,1,0:T(8,128)(2,1)S(1)}, u32[]{:S(2)}, u32[]{:S(2)}) collective-permute-start(bf16[2,64,640]{2,1,0:T(8,128)(2,1)S(1)} %get-tuple-element.104), channel_id=1, source_target_pairs={{0,18},{2,16},{16,2},{18,0},{1,19},{3,17},{17,3},{19,1},{4,22},{6,... | collective-permute-start | bytes 491528 | tf_op jit(solution)/shard_map/ppermute | solution.py:593
  131.8 13.1 %all-to-all-start.3 = ((f32[32,2,512]{2,1,0:T(2,128)}), f32[32,2,512]{2,1,0:T(2,128)S(1)}, u32[]{:S(2)}, u32[]{:S(2)}) async-start(f32[32,2,512]{2,1,0:T(2,128)} %get-tuple-element.105), calls=%async_computation.3 | async-start | bytes 262144 | tf_op jit(solution)/shard_map/all_to_all | solution.py:813
  144.9 6.5 %collective-permute-start.35 = (bf16[4,9,16,512]{3,2,1,0:T(8,128)(2,1)}, bf16[4,9,16,512]{3,2,1,0:T(8,128)(2,1)S(1)}, u32[]{:S(2)}, u32[]{:S(2)}) collective-permute-start(bf16[4,9,16,512]{3,2,1,0:T(8,128)(2,1)} %get-tuple-element.117.refs_6_), channel_id=1, source_target_pairs={{0,1},{1,0},{2,3},{3,2},{4,5},{5,4},{6,7},{7,6},{8,9},{9,8},{10,11... | collective-permute-start | bytes 1769480 | tf_op jit(solution)/shard_map/ppermute | solution.py:589
  147.8 7.1 %collective-permute-start.32 = (bf16[2,64,640]{2,1,0:T(8,128)(2,1)S(1)}, bf16[2,64,640]{2,1,0:T(8,128)(2,1)S(1)}, u32[]{:S(2)}, u32[]{:S(2)}) collective-permute-start(bf16[2,64,640]{2,1,0:T(8,128)(2,1)S(1)} %get-tuple-element.114), channel_id=1, source_target_pairs={{0,2},{2,0},{1,3},{3,1},{4,6},{6,4},{5,7},{7,5},{8,10},{10,8},{9,1... | collective-permute-start | bytes 491528 | tf_op jit(solution)/shard_map/ppermute | solution.py:589
  148.4 9.7 %collective-permute-start.33 = (bf16[2,64,640]{2,1,0:T(8,128)(2,1)S(1)}, bf16[2,64,640]{2,1,0:T(8,128)(2,1)S(1)}, u32[]{:S(2)}, u32[]{:S(2)}) collective-permute-start(bf16[2,64,640]{2,1,0:T(8,128)(2,1)S(1)} %get-tuple-element.115), channel_id=1, source_target_pairs={{0,16},{16,0},{1,17},{17,1},{2,18},{18,2},{3,19},{19,3},{4,20},{20... | collective-permute-start | bytes 491528 | tf_op jit(solution)/shard_map/ppermute | solution.py:589
  149.9 8.2 %collective-permute-start.34 = (bf16[2,64,640]{2,1,0:T(8,128)(2,1)S(1)}, bf16[2,64,640]{2,1,0:T(8,128)(2,1)S(1)}, u32[]{:S(2)}, u32[]{:S(2)}) collective-permute-start(bf16[2,64,640]{2,1,0:T(8,128)(2,1)S(1)} %get-tuple-element.116), channel_id=1, source_target_pairs={{0,18},{2,16},{16,2},{18,0},{1,19},{3,17},{17,3},{19,1},{4,22},{6,... | collective-permute-start | bytes 491528 | tf_op jit(solution)/shard_map/ppermute | solution.py:593
  151.6 15.0 %collective-permute-start.36 = (bf16[9,16,512]{2,1,0:T(8,128)(2,1)S(1)}, bf16[9,16,512]{2,1,0:T(8,128)(2,1)S(1)}, u32[]{:S(2)}, u32[]{:S(2)}) collective-permute-start(bf16[9,16,512]{2,1,0:T(8,128)(2,1)S(1)} %get-tuple-element.145.refs_8_), channel_id=1, source_target_pairs={{0,4},{4,0},{8,12},{12,8},{1,5},{5,1},{9,13},{13,9},{2,6},{6,2},{1... | collective-permute-start | bytes 442376 | tf_op jit(solution)/shard_map/ppermute | solution.py:589
  152.2 14.4 %collective-permute-start.37 = (bf16[9,16,512]{2,1,0:T(8,128)(2,1)S(1)}, bf16[9,16,512]{2,1,0:T(8,128)(2,1)S(1)}, u32[]{:S(2)}, u32[]{:S(2)}) collective-permute-start(bf16[9,16,512]{2,1,0:T(8,128)(2,1)S(1)} %get-tuple-element.144.refs_9_), channel_id=1, source_target_pairs={{0,8},{4,12},{8,0},{12,4},{1,9},{5,13},{9,1},{13,5},{2,10},{6,14},... | collective-permute-start | bytes 442376 | tf_op jit(solution)/shard_map/ppermute | solution.py:589
  154.9 11.7 %collective-permute-start.38 = (bf16[9,16,512]{2,1,0:T(8,128)(2,1)S(1)}, bf16[9,16,512]{2,1,0:T(8,128)(2,1)S(1)}, u32[]{:S(2)}, u32[]{:S(2)}) collective-permute-start(bf16[9,16,512]{2,1,0:T(8,128)(2,1)S(1)} %get-tuple-element.143.refs_10_), channel_id=1, source_target_pairs={{0,12},{4,8},{8,4},{12,0},{1,13},{5,9},{9,5},{13,1},{2,14},{6,10},... | collective-permute-start | bytes 442376 | tf_op jit(solution)/shard_map/ppermute | solution.py:589
  166.6 2.3 %collective-permute-start.39 = (bf16[4,9,16,512]{3,2,1,0:T(8,128)(2,1)}, bf16[4,9,16,512]{3,2,1,0:T(8,128)(2,1)S(1)}, u32[]{:S(2)}, u32[]{:S(2)}) collective-permute-start(bf16[4,9,16,512]{3,2,1,0:T(8,128)(2,1)} %get-tuple-element.120), channel_id=1, source_target_pairs={{0,1},{1,0},{2,3},{3,2},{4,5},{5,4},{6,7},{7,6},{8,9},{9,8},{10,11... | collective-permute-start | bytes 1769480 | tf_op jit(solution)/shard_map/ppermute | solution.py:589
  170.3 14.6 %collective-permute-start.40 = (bf16[9,16,512]{2,1,0:T(8,128)(2,1)S(1)}, bf16[9,16,512]{2,1,0:T(8,128)(2,1)S(1)}, u32[]{:S(2)}, u32[]{:S(2)}) collective-permute-start(bf16[9,16,512]{2,1,0:T(8,128)(2,1)S(1)} %get-tuple-element.142.refs_5_), channel_id=1, source_target_pairs={{0,4},{4,0},{8,12},{12,8},{1,5},{5,1},{9,13},{13,9},{2,6},{6,2},{1... | collective-permute-start | bytes 442376 | tf_op jit(solution)/shard_map/ppermute | solution.py:589
  171.9 14.0 %collective-permute-start.41 = (bf16[9,16,512]{2,1,0:T(8,128)(2,1)S(1)}, bf16[9,16,512]{2,1,0:T(8,128)(2,1)S(1)}, u32[]{:S(2)}, u32[]{:S(2)}) collective-permute-start(bf16[9,16,512]{2,1,0:T(8,128)(2,1)S(1)} %get-tuple-element.141.refs_6_), channel_id=1, source_target_pairs={{0,8},{4,12},{8,0},{12,4},{1,9},{5,13},{9,1},{13,5},{2,10},{6,14},... | collective-permute-start | bytes 442376 | tf_op jit(solution)/shard_map/ppermute | solution.py:589
  174.3 11.6 %collective-permute-start.42 = (bf16[9,16,512]{2,1,0:T(8,128)(2,1)S(1)}, bf16[9,16,512]{2,1,0:T(8,128)(2,1)S(1)}, u32[]{:S(2)}, u32[]{:S(2)}) collective-permute-start(bf16[9,16,512]{2,1,0:T(8,128)(2,1)S(1)} %get-tuple-element.140.refs_7_), channel_id=1, source_target_pairs={{0,12},{4,8},{8,4},{12,0},{1,13},{5,9},{9,5},{13,1},{2,14},{6,10},... | collective-permute-start | bytes 442376 | tf_op jit(solution)/shard_map/ppermute | solution.py:589
  183.4 6.7 %collective-permute-start.44 = (bf16[9,16,512]{2,1,0:T(8,128)(2,1)S(1)}, bf16[9,16,512]{2,1,0:T(8,128)(2,1)S(1)}, u32[]{:S(2)}, u32[]{:S(2)}) collective-permute-start(bf16[9,16,512]{2,1,0:T(8,128)(2,1)S(1)} %add_convert_fusion), channel_id=1, source_target_pairs={{0,16},{16,0},{1,17},{17,1},{2,18},{18,2},{3,19},{19,3},{4,20},{20... | collective-permute-start | bytes 442376 | tf_op jit(solution)/shard_map/ppermute | solution.py:589
  186.0 5.7 %collective-permute-start.43 = (bf16[9,16,512]{2,1,0:T(8,128)(2,1)S(1)}, bf16[9,16,512]{2,1,0:T(8,128)(2,1)S(1)}, u32[]{:S(2)}, u32[]{:S(2)}) collective-permute-start(bf16[9,16,512]{2,1,0:T(8,128)(2,1)S(1)} %add_convert_fusion.1), channel_id=1, source_target_pairs={{0,16},{16,0},{1,17},{17,1},{2,18},{18,2},{3,19},{19,3},{4,20},{20... | collective-permute-start | bytes 442376 | tf_op jit(solution)/shard_map/ppermute | solution.py:589
  (28 other events, 145.4 us)

commit v2 on v1

--- a/solution.py
+++ b/solution.py
@@ -267,17 +267,59 @@
     return value * sigmoid(value) * valid
 
 
-def side_active(canvas, source, count, *refs):
-    norm_ref, param_ref, *refs = refs
+def side_hidden(canvas, source, count, *refs):
     weights, refs = refs[: len(source.arrays)], refs[len(source.arrays) :]
     sent_hbm, refs = refs[:count], refs[count:]
-    active_ref, *full, buffer, weight, sems, hidden, sent, sent_sem = refs
+    hidden_ref, full, buffer, weight, sems, sent, sent_sem = refs
     copies = [
         pltpu.make_async_copy(hbm, sent.at[index], sent_sem) for index, hbm in enumerate(sent_hbm)
     ]
     for copy in copies:
         copy.start()
-    fetch = Fetch(source, weights, weight, sems, *full)
+    fetch = Fetch(source, weights, weight, sems, full)
+    for copy in copies:
+        copy.wait()
+
+    def image(index, carry):
+        pixels = sent[index, 0 : canvas.rows, :].astype(F32)
+        convolve(canvas, pixels, fetch, buffer, hidden_ref.at[index], 1, when=index == 0)
+        return carry
+
+    lax.fori_loop(0, count, image, 0)
+    fetch.finish()
+
+
+def side_activate(canvas, hidden_ref, norm_ref, param_ref, *refs):
+    *sent_hbm, active_ref, lines, sent_sem = refs
+    copies = []
+    for index, hbm in enumerate(sent_hbm):
+        tail = hbm.at[pl.ds(canvas.rows, 16)]
+        copies.append(pltpu.make_async_copy(tail, lines.at[index], sent_sem))
+    for copy in copies:
+        copy.start()
+    for copy in copies:
+        copy.wait()
+
+    def image(index, carry):
+        valid = sent_mask(canvas, lines[index].astype(F32))
+        active = activate(hidden_ref[index], norm_ref, param_ref, valid)
+        active_ref[index] = active.astype(BF16)
+        return carry
+
+    lax.fori_loop(0, len(sent_hbm), image, 0)
+
+
+def side_active(canvas, source, count, *refs):
+    norm_ref, param_ref, *refs = refs
+    weights, refs = refs[: len(source.arrays)], refs[len(source.arrays) :]
+    sent_hbm, refs = refs[:count], refs[count:]
+    active_ref, buffer, weight, sems, hidden, sent, sent_sem = refs
+    copies = [
+        pltpu.make_async_copy(hbm, sent.at[index], sent_sem) for index, hbm in enumerate(sent_hbm)
+    ]
+    for copy in copies:
+        copy.start()
+    fetch = Fetch(source, weights, weight, sems)
     for copy in copies:
         copy.wait()
 
@@ -290,8 +332,6 @@
         return carry
 
     lax.fori_loop(0, count, image, 0)
-    if full:
-        fetch.finish()
 
 
 def forward_one(canvas, source, x_ref, mask_ref, info_ref, *refs):
@@ -698,19 +738,19 @@
                 pltpu.VMEM((2, TAPS * part, canvas.rows), BF16),
                 pltpu.VMEM((TAPS * part, channels), F32),
                 pltpu.VMEM(out, BF16),
-                pltpu.VMEM(out, F32),
+                pltpu.VMEM(out, BF16),
                 pltpu.SemaphoreType.DMA((10,)),
             ),
             (*moved, *layer),
             after,
-            kept=((out, BF16), (out, F32)),
+            kept=((out, BF16), (out, BF16)),
         )
         return send, keep
 
     def core_sum(self, chip, *others):
         send, keep = chip
         other = flip(behind(send, others), "c", 1, 2)
-        parts = [(keep[place] + other[place].astype(F32)).astype(BF16) for place in range(1, 4)]
+        parts = [(keep[place].astype(F32) + other[place].astype(F32)).astype(BF16) for place in range(1, 4)]
         return (keep[0], other[0]), *parts
 
     def line(self, parts):
@@ -718,7 +758,7 @@
 
     def line_sum(self, parts, found, *others):
         keep, other = lax.optimization_barrier((*parts[0], *others))[:2]
-        total = keep + other.astype(F32)
+        total = keep.astype(F32) + other.astype(F32)
         for part in found:
             total = total + part.astype(F32)
         return total
@@ -869,6 +909,18 @@
     )
     gathered = exchange(stats)
     side = ()
+    if sides:
+        sent_images = pltpu.VMEM((len(sides), canvas.sent_rows, channels), BF16)
+        *side, full_one = call(
+            functools.partial(side_hidden, canvas, weight_one, len(sides)),
+            (),
+            (((len(sides), rows, channels), F32),),
+            (*weighted, sent_images, pltpu.SemaphoreType.DMA),
+            (*weight_one.arrays, *sides),
+            (stats,),
+            kept=(full,),
+        )
+        weight_one = Whole(full_one, weight_one.width)
     weight_two = ways.second_weights(stats, gathered, *side)
     active, second, norm_one, params, counts, stats = conv_call(
         forward_two,
@@ -880,7 +932,7 @@
     gathered = exchange(stats)
     actives = (active,)
 
-    def side_call(sent, after, kept=()):
+    def side_call(sent, after):
         return call(
             functools.partial(side_active, canvas, weight_one, len(sent)),
             (norm_one, params),
@@ -893,12 +945,17 @@
             ),
             (*weight_one.arrays, *sent),
             after,
-            kept=kept,
         )
 
     if sides:
-        found, full_one = side_call(sides, (stats,), (full,))
-        weight_one = Whole(full_one, weight_one.width)
+        (found,) = call(
+            functools.partial(side_activate, canvas),
+            (*side, norm_one, params),
+            (((len(sides), rows, channels), BF16),),
+            (pltpu.VMEM((len(sides), 16, channels), BF16), pltpu.SemaphoreType.DMA),
+            sides,
+            (stats,),
+        )
         actives += (found,)
     result, grad_sum, norm_two, stats = call(
         turn,

time: 195 us -> 192 us (0.985)
  starting transfers between devices: 68.3 us -> 64.2 us
  Pallas kernels: 71.8 us -> 75.6 us
  waiting for transfers between devices: 41.9 us -> 39.3 us
    ppermute x4, waiting for transfers between devices: 6.82 us -> 0.82 us  [diagonal(): lax.ppermute(value, ('y', 'x'), [(place, place ^ 3) for place in range(4)])]
    all_to_all x4, waiting for transfers between devices: 2.59 us -> 6.5 us  [exchange(): return lax.all_to_all(spread, ways.axes, 0, 0, tiled=True)]
    all_to_all x4, starting transfers between devices: 20.7 us -> 16.9 us  [exchange(): return lax.all_to_all(spread, ways.axes, 0, 0, tiled=True)]
    pallas_call x13 -> x14, Pallas kernels: 71.8 us -> 75.6 us  [call(): pl.pallas_call(kernel, out_shape=[jax.ShapeDtypeStruct(shape, dtype) for...]
    unnamed x86 -> x90, local copies, waits for them, and re-layouts: 4.11 us -> 4.01 us
  transfers between devices with their start and end apart: 49 -> 49, of which waited for: 19 -> 18; matrix products, arithmetic and copies ran while one was open for 1% -> 1% of each run, Pallas kernels for 36% -> 38%
where the time goes in v2:
time: 192 us; the launch traced here: 191 us
  Pallas kernels  75.6 us (39%)
  starting transfers between devices  64.2 us (33%)
  waiting for transfers between devices  39.3 us (20%)
  other arithmetic  5.4 us (3%)
  local copies, waits for them, and re-layouts  5.13 us (3%)
    pallas_call x14, Pallas kernels, call(): pl.pallas_call(kernel, out_shape=[jax.ShapeDtypeStruct(shape, dtype) for...  75.6 us
    ppermute x41, starting transfers between devices, flip(): lax.ppermute(value, axis, [(place, place ^ bit) for place in range(size)])  40.7 us
    ppermute x41, waiting for transfers between devices, flip(): lax.ppermute(value, axis, [(place, place ^ bit) for place in range(size)])  32 us
    all_to_all x4, starting transfers between devices, exchange(): return lax.all_to_all(spread, ways.axes, 0, 0, tiled=True)  16.9 us
    ppermute x4, starting transfers between devices, diagonal(): lax.ppermute(value, ('y', 'x'), [(place, place ^ 3) for place in range(4)])  6.6 us
    all_to_all x4, waiting for transfers between devices, exchange(): return lax.all_to_all(spread, ways.axes, 0, 0, tiled=True)  6.5 us
    unnamed x90, local copies, waits for them, and re-layouts  4.01 us
  transfers between devices with their start and end apart: 49, of which 18 were waited for; matrix products, arithmetic and copies ran while one was open for 1% of the time, Pallas kernels for 38%

profile of v2, /device:TPU:0, one launch (start us, length us, event | category | flops | bytes accessed | tf_op | source)
XLA Modules:
  0.0 191.0 jit_solution(16597536468750855412)
XLA Ops:
  0.6 1.4 bitcast_convert_fusion
  2.2 3.0 %collective-permute-start.1 = (bf16[1,9,32,512]{3,2,1,0:T(8,128)(2,1)S(1)}, bf16[1,9,32,512]{3,2,1,0:T(8,128)(2,1)S(1)}, u32[]{:S(2)}, u32[]{:S(2)}) collective-permute-start(bf16[1,9,32,512]{3,2,1,0:T(8,128)(2,1)S(1)} %bitcast.86), channel_id=1, source_target_pairs={{0,2},{2,0},{1,3},{3,1},{4,6},{6,4},{5,7},{7,5},{8,10},{10,8},{9,1... | collective-permute-start | bytes 884744 | tf_op jit(solution)/shard_map/ppermute | solution.py:629
  5.2 2.7 %collective-permute-start.3 = (bf16[1,9,32,256]{3,2,1,0:T(8,128)(2,1)S(1)}, bf16[1,9,32,256]{3,2,1,0:T(8,128)(2,1)S(1)}, u32[]{:S(2)}, u32[]{:S(2)}) collective-permute-start(bf16[1,9,32,256]{3,2,1,0:T(8,128)(2,1)S(1)} %get-tuple-element.147), channel_id=1, source_target_pairs={{0,8},{4,12},{8,0},{12,4},{1,9},{5,13},{9,1},{13,5},{2,10},{6,14},... | collective-permute-start | bytes 442376 | tf_op jit(solution)/shard_map/ppermute | solution.py:629
  7.9 2.7 %shard_map.238 = (bf16[560,512]{1,0:T(8,128)(2,1)}, f32[544,128]{1,0:T(8,128)S(1)}, f32[2,128]{1,0:T(2,128)S(1)}) custom-call(bf16[5,5,6,512]{3,2,1,0:T(8,128)(2,1)S(1)} %bitcast.76, bf16[7,7,2,512]{3,2,1,0:T(2,128)(2,1)S(1)} %bitcast.80, bf16[9,9,2,512]{3,2,1,0:T(2,128)(2,1)S(1)} %bitcast.79, f32[4,32]{1,0:T(4,128)S(1)} %copy-done.15, ...), custom_call_target="tpu_custom_call" | custom-call | tf_op jit(solution)/shard_map/pallas_call | solution.py:605
  11.1 1.5 collective-permute-start.6
  12.7 2.0 %collective-permute-done.3 = bf16[1,9,32,256]{3,2,1,0:T(8,128)(2,1)S(1)} collective-permute-done((bf16[1,9,32,256]{3,2,1,0:T(8,128)(2,1)S(1)}, bf16[1,9,32,256]{3,2,1,0:T(8,128)(2,1)S(1)}, u32[]{:S(2)}, u32[]{:S(2)}) %collective-permute-start.3) | collective-permute-done | bytes 147488 | tf_op jit(solution)/shard_map/ppermute | solution.py:629
  14.7 0.7 collective-permute-start.4
  15.4 1.2 shard_map.239.refs_6_
  16.6 6.0 %collective-permute-done.4 = bf16[2,9,32,256]{3,2,1,0:T(8,128)(2,1)S(1)} collective-permute-done((bf16[2,9,32,256]{3,2,1,0:T(8,128)(2,1)S(1)}, bf16[2,9,32,256]{3,2,1,0:T(8,128)(2,1)S(1)}, u32[]{:S(2)}, u32[]{:S(2)}) %collective-permute-start.4) | collective-permute-done | bytes 294944 | tf_op jit(solution)/shard_map/ppermute | solution.py:629
  22.7 2.3 %collective-permute-done.5.refs_17_.refs_14_.refs_3_.refs_5_ = bf16[560,512]{1,0:T(8,128)(2,1)S(1)} collective-permute-done((bf16[560,512]{1,0:T(8,128)(2,1)}, bf16[560,512]{1,0:T(8,128)(2,1)S(1)}, u32[]{:S(2)}, u32[]{:S(2)}) %collective-permute-start.5) | collective-permute-done | bytes 573472 | tf_op jit(solution)/shard_map/ppermute | solution.py:629
  25.2 1.5 collective-permute-start.10
  26.8 1.5 collective-permute-start.8
  28.2 2.2 %collective-permute-start.19 = (bf16[1,9,32,256]{3,2,1,0:T(8,128)(2,1)S(1)}, bf16[1,9,32,256]{3,2,1,0:T(8,128)(2,1)S(1)}, u32[]{:S(2)}, u32[]{:S(2)}) collective-permute-start(bf16[1,9,32,256]{3,2,1,0:T(8,128)(2,1)S(1)} %get-tuple-element.83), channel_id=1, source_target_pairs={{0,8},{4,12},{8,0},{12,4},{1,9},{5,13},{9,1},{13,5},{2,10},{6,14},... | collective-permute-start | bytes 442376 | tf_op jit(solution)/shard_map/ppermute | solution.py:629
  30.6 4.8 %collective-permute-done.10.refs_11_.refs_8_ = bf16[3,9,32,256]{3,2,1,0:T(8,128)(2,1)S(1)} collective-permute-done((bf16[3,9,32,256]{3,2,1,0:T(8,128)(2,1)S(1)}, bf16[3,9,32,256]{3,2,1,0:T(8,128)(2,1)S(1)}, u32[]{:S(2)}, u32[]{:S(2)}) %collective-permute-start.10) | collective-permute-done | bytes 442400 | tf_op jit(solution)/shard_map/ppermute | solution.py:629
  35.5 2.0 %collective-permute-start.17 = (bf16[1,9,32,512]{3,2,1,0:T(8,128)(2,1)S(1)}, bf16[1,9,32,512]{3,2,1,0:T(8,128)(2,1)S(1)}, u32[]{:S(2)}, u32[]{:S(2)}) collective-permute-start(bf16[1,9,32,512]{3,2,1,0:T(8,128)(2,1)S(1)} %bitcast.72), channel_id=1, source_target_pairs={{0,2},{2,0},{1,3},{3,1},{4,6},{6,4},{5,7},{7,5},{8,10},{10,8},{9,1... | collective-permute-start | bytes 884744 | tf_op jit(solution)/shard_map/ppermute | solution.py:629
  37.8 1.7 collective-permute-start.12
  39.7 1.6 collective-permute-start.20
  41.4 6.6 %collective-permute-done.12.refs_13_.refs_10_ = bf16[3,9,16,256]{3,2,1,0:T(8,128)(2,1)S(1)} collective-permute-done((bf16[3,9,16,256]{3,2,1,0:T(8,128)(2,1)S(1)}, bf16[3,9,16,256]{3,2,1,0:T(8,128)(2,1)S(1)}, u32[]{:S(2)}, u32[]{:S(2)}) %collective-permute-start.12) | collective-permute-done | bytes 221216 | tf_op jit(solution)/shard_map/ppermute | solution.py:629
  49.1 0.7 collective-permute-start.24
  49.8 0.9 collective-permute-done.14.refs_14_.refs_11_
  50.7 1.7 collective-permute-start.22
  53.7 6.5 %shard_map.240 = (f32[544,512]{1,0:T(8,128)}, f32[32,2,640]{2,1,0:T(2,128)}) custom-call(bf16[560,512]{1,0:T(8,128)(2,1)} %get-tuple-element.99.refs_0_.refs_5_.refs_4_, f32[544,128]{1,0:T(8,128)} %copy-done, f32[2,128]{1,0:T(2,128)S(1)} %get-tuple-element.75.refs_2_, bf16[1,9,32,512]{3,2,1,0:T(8,128)(2,1)} %bitcast.88, bf16[1,9,32,512]{3,2,1,0:T(8,128)(2,1)} %copy-done.35, ...), custom_call_target="tpu_custom_call" | custom-call | tf_op jit(solution)/shard_map/pallas_call | solution.py:605
  60.3 6.1 %all-to-all-start = ((f32[32,2,640]{2,1,0:T(2,128)}), f32[32,2,640]{2,1,0:T(2,128)S(1)}, u32[]{:S(2)}, u32[]{:S(2)}) async-start(f32[32,2,640]{2,1,0:T(2,128)} %get-tuple-element.81.refs_16_), calls=%async_computation | async-start | bytes 327680 | tf_op jit(solution)/shard_map/all_to_all | solution.py:853
  66.9 9.2 %shard_map.241 = (f32[2,544,512]{2,1,0:T(8,128)}, bf16[9,512,512]{2,1,0:T(8,128)(2,1)}) custom-call(bf16[1,9,32,512]{3,2,1,0:T(8,128)(2,1)} %bitcast.89, bf16[1,9,32,512]{3,2,1,0:T(8,128)(2,1)} %copy-done.35, bf16[1,9,32,512]{3,2,1,0:T(8,128)(2,1)} %copy-done.34, bf16[1,9,32,512]{3,2,1,0:T(8,128)(2,1)} %copy-done.36, bf16[3,9,32,256]{3,2,1,0:T(8,128)(2,1)} %copy-done.20, ...), custom_call_target="tpu_custom_call" | custom-call | tf_op jit(solution)/shard_map/pallas_call | solution.py:605
  77.3 2.7 %collective-permute-done.18.refs_6_.refs_8_ = bf16[1,9,32,512]{3,2,1,0:T(8,128)(2,1)S(1)} collective-permute-done((bf16[1,9,32,512]{3,2,1,0:T(8,128)(2,1)}, bf16[1,9,32,512]{3,2,1,0:T(8,128)(2,1)S(1)}, u32[]{:S(2)}, u32[]{:S(2)}) %collective-permute-start.18) | collective-permute-done | bytes 294944 | tf_op jit(solution)/shard_map/ppermute | solution.py:629
  80.0 2.5 %collective-permute-start.28 = (bf16[560,512]{1,0:T(8,128)(2,1)S(1)}, bf16[560,512]{1,0:T(8,128)(2,1)}, u32[]{:S(2)}, u32[]{:S(2)}) collective-permute-start(bf16[560,512]{1,0:T(8,128)(2,1)S(1)} %copy-done.18), channel_id=1, source_target_pairs={{0,18},{2,16},{16,2},{18,0},{1,19},{3,17},{17,3},{19,1},{4,22},{6,... | collective-permute-start | bytes 1720328 | tf_op jit(solution)/shard_map/ppermute | solution.py:633
  82.5 0.7 copy-done.31
  83.2 0.8 copy-done.32
  84.0 7.0 %shard_map.242 = (bf16[544,512]{1,0:T(8,128)(2,1)}, f32[544,512]{1,0:T(8,128)}, f32[4,512]{1,0:T(4,128)S(1)}, f32[4,512]{1,0:T(4,128)S(1)}, f32[32,512]{1,0:T(8,128)S(1)}, /*index=5*/f32[32,2,512]{2,1,0:T(2,128)}) custom-call(f32[544,512]{1,0:T(8,128)} %get-tuple-element.80.refs_0_.refs_1_.refs_4_, f32[32,2,640]{2,1,0:T(2,128)S(1)} %all-to-all-done.refs_1_, ...), custom_call_target="tpu_custom_call" | custom-call | tf_op jit(solution)/shard_map/pallas_call | solution.py:605
  91.0 3.7 %all-to-all-start.1 = ((f32[32,2,512]{2,1,0:T(2,128)}), f32[32,2,512]{2,1,0:T(2,128)S(1)}, u32[]{:S(2)}, u32[]{:S(2)}) async-start(f32[32,2,512]{2,1,0:T(2,128)} %get-tuple-element.92.refs_5_), calls=%async_computation.1 | async-start | bytes 262144 | tf_op jit(solution)/shard_map/all_to_all | solution.py:853
  94.8 4.4 %shard_map.243.refs_7_.refs_5_ = bf16[2,544,512]{2,1,0:T(8,128)(2,1)} custom-call(f32[2,544,512]{2,1,0:T(8,128)} %get-tuple-element.88.refs_15_.refs_0_, f32[4,512]{1,0:T(4,128)S(1)} %get-tuple-element.90.refs_1_.refs_0_.refs_2_, f32[4,512]{1,0:T(4,128)S(1)} %get-tuple-element.94.refs_2_.refs_3_.refs_1_, bf16[560,512]{1,0:T(8,128)(2,1)S(1)} %copy-done.5, ...), custom_call_target="tpu_custom_call" | custom-call | tf_op jit(solution)/shard_map/pallas_call | solution.py:605
  99.2 3.8 %all-to-all-done.1.refs_1_ = f32[32,2,512]{2,1,0:T(2,128)S(1)} async-done(((f32[32,2,512]{2,1,0:T(2,128)}), f32[32,2,512]{2,1,0:T(2,128)S(1)}, u32[]{:S(2)}, u32[]{:S(2)}) %all-to-all-start.1) | async-done | bytes 131104 | tf_op jit(solution)/shard_map/all_to_all | solution.py:853
  103.0 3.6 %shard_map.244 = (bf16[544,512]{1,0:T(8,128)(2,1)}, f32[544,512]{1,0:T(8,128)}, f32[4,512]{1,0:T(4,128)S(1)}, f32[32,2,512]{2,1,0:T(2,128)}) custom-call(f32[544,512]{1,0:T(8,128)} %get-tuple-element.91.refs_0_.refs_4_, f32[32,2,512]{2,1,0:T(2,128)S(1)} %all-to-all-done.1.refs_1_, f32[32,512]{1,0:T(8,128)S(1)} %get-tuple-element.93.refs_2_, ...), custom_call_target="tpu_custom_call" | custom-call | tf_op jit(solution)/shard_map/pallas_call | solution.py:605
  106.6 2.8 %all-to-all-start.2 = ((f32[32,2,512]{2,1,0:T(2,128)}), f32[32,2,512]{2,1,0:T(2,128)S(1)}, u32[]{:S(2)}, u32[]{:S(2)}) async-start(f32[32,2,512]{2,1,0:T(2,128)} %get-tuple-element.96.refs_4_), calls=%async_computation.2 | async-start | bytes 262144 | tf_op jit(solution)/shard_map/all_to_all | solution.py:853
  109.5 5.6 %shard_map.245.refs_6_ = bf16[1,544,512]{2,1,0:T(8,128)(2,1)S(1)} custom-call(f32[4,512]{1,0:T(4,128)S(1)} %get-tuple-element.90.refs_1_.refs_0_.refs_2_, f32[4,512]{1,0:T(4,128)S(1)} %get-tuple-element.94.refs_2_.refs_3_.refs_1_, bf16[9,512,512]{2,1,0:T(8,128)(2,1)} %get-tuple-element.98.refs_2_.refs_4_, ...), custom_call_target="tpu_custom_call" | custom-call | tf_op jit(solution)/shard_map/pallas_call | solution.py:605
  115.0 0.8 copy-done.6
  115.8 1.6 all-to-all-done.2.refs_1_
  117.5 2.6 %shard_map.246 = (f32[2,512]{1,0:T(2,128)S(1)}, bf16[2,64,640]{2,1,0:T(8,128)(2,1)S(1)}, bf16[2,64,640]{2,1,0:T(8,128)(2,1)S(1)}, bf16[2,64,640]{2,1,0:T(8,128)(...) custom-call(f32[4,512]{1,0:T(4,128)S(1)} %get-tuple-element.95.refs_0_, ...), custom_call_target="tpu_custom_call" | custom-call | tf_op jit(solution)/shard_map/pallas_call | solution.py:605
  120.6 0.8 collective-permute-start.30
  121.4 2.2 %collective-permute-start.31 = (bf16[2,64,640]{2,1,0:T(8,128)(2,1)S(1)}, bf16[2,64,640]{2,1,0:T(8,128)(2,1)S(1)}, u32[]{:S(2)}, u32[]{:S(2)}) collective-permute-start(bf16[2,64,640]{2,1,0:T(8,128)(2,1)S(1)} %get-tuple-element.104), channel_id=1, source_target_pairs={{0,18},{2,16},{16,2},{18,0},{1,19},{3,17},{17,3},{19,1},{4,22},{6,... | collective-permute-start | bytes 491528 | tf_op jit(solution)/shard_map/ppermute | solution.py:633
  123.6 7.3 %shard_map.247 = (f32[544,512]{1,0:T(8,128)}, f32[32,2,512]{2,1,0:T(2,128)}) custom-call(bf16[544,512]{1,0:T(8,128)(2,1)} %get-tuple-element.100.refs_0_, f32[544,512]{1,0:T(8,128)} %get-tuple-element.80.refs_0_.refs_1_.refs_4_, f32[4,512]{1,0:T(4,128)S(1)} %get-tuple-element.90.refs_1_.refs_0_.refs_2_, ...), custom_call_target="tpu_custom_call" | custom-call | tf_op jit(solution)/shard_map/pallas_call | solution.py:605
  130.9 4.3 %all-to-all-start.3 = ((f32[32,2,512]{2,1,0:T(2,128)}), f32[32,2,512]{2,1,0:T(2,128)S(1)}, u32[]{:S(2)}, u32[]{:S(2)}) async-start(f32[32,2,512]{2,1,0:T(2,128)} %get-tuple-element.105), calls=%async_computation.3 | async-start | bytes 262144 | tf_op jit(solution)/shard_map/all_to_all | solution.py:853
  135.2 6.9 %shard_map.248 = (bf16[4,9,16,512]{3,2,1,0:T(8,128)(2,1)}, bf16[4,9,16,512]{3,2,1,0:T(8,128)(2,1)}) custom-call(bf16[2,64,640]{2,1,0:T(8,128)(2,1)S(1)} %get-tuple-element.107.refs_0_, bf16[2,64,640]{2,1,0:T(8,128)(2,1)S(1)} %collective-permute-done.29.refs_1_, bf16[2,64,640]{2,1,0:T(8,128)(2,1)S(1)} %collective-permute-done.30.refs_2_, ...), custom_call_target="tpu_custom_call" | custom-call | tf_op jit(solution)/shard_map/pallas_call | solution.py:605
  142.1 1.1 all-to-all-done.3.refs_1_
  143.4 2.6 %shard_map.249 = (f32[2,512]{1,0:T(2,128)S(1)}, bf16[2,64,640]{2,1,0:T(8,128)(2,1)S(1)}, bf16[2,64,640]{2,1,0:T(8,128)(2,1)S(1)}, bf16[2,64,640]{2,1,0:T(8,128)(...) custom-call(f32[4,512]{1,0:T(4,128)S(1)} %get-tuple-element.90.refs_1_.refs_0_.refs_2_, ...), custom_call_target="tpu_custom_call" | custom-call | tf_op jit(solution)/shard_map/pallas_call | solution.py:605
  146.5 1.5 collective-permute-start.33
  148.0 1.6 collective-permute-start.34
  150.2 2.4 %collective-permute-start.37 = (bf16[9,16,512]{2,1,0:T(8,128)(2,1)S(1)}, bf16[9,16,512]{2,1,0:T(8,128)(2,1)S(1)}, u32[]{:S(2)}, u32[]{:S(2)}) collective-permute-start(bf16[9,16,512]{2,1,0:T(8,128)(2,1)S(1)} %get-tuple-element.144.refs_9_), channel_id=1, source_target_pairs={{0,8},{4,12},{8,0},{12,4},{1,9},{5,13},{9,1},{13,5},{2,10},{6,14},... | collective-permute-start | bytes 442376 | tf_op jit(solution)/shard_map/ppermute | solution.py:629
  153.1 2.3 %collective-permute-start.38 = (bf16[9,16,512]{2,1,0:T(8,128)(2,1)S(1)}, bf16[9,16,512]{2,1,0:T(8,128)(2,1)S(1)}, u32[]{:S(2)}, u32[]{:S(2)}) collective-permute-start(bf16[9,16,512]{2,1,0:T(8,128)(2,1)S(1)} %get-tuple-element.143.refs_10_), channel_id=1, source_target_pairs={{0,12},{4,8},{8,4},{12,0},{1,13},{5,9},{9,5},{13,1},{2,14},{6,10},... | collective-permute-start | bytes 442376 | tf_op jit(solution)/shard_map/ppermute | solution.py:629
  155.4 0.8 collective-permute-done.34.refs_3_
  156.2 0.7 copy-done.42
  156.9 7.6 %shard_map.250 = (bf16[4,9,16,512]{3,2,1,0:T(8,128)(2,1)}, bf16[4,9,16,512]{3,2,1,0:T(8,128)(2,1)}) custom-call(bf16[2,64,640]{2,1,0:T(8,128)(2,1)S(1)} %get-tuple-element.113.refs_0_, bf16[2,64,640]{2,1,0:T(8,128)(2,1)S(1)} %collective-permute-done.32.refs_1_, bf16[2,64,640]{2,1,0:T(8,128)(2,1)S(1)} %collective-permute-done.33.refs_2_, ...), custom_call_target="tpu_custom_call" | custom-call | tf_op jit(solution)/shard_map/pallas_call | solution.py:605
  164.6 1.0 slice_bitcast_fusion.3
  165.6 1.2 collective-permute-done.39
  166.9 1.7 collective-permute-start.40
  168.6 2.3 %collective-permute-start.41 = (bf16[9,16,512]{2,1,0:T(8,128)(2,1)S(1)}, bf16[9,16,512]{2,1,0:T(8,128)(2,1)S(1)}, u32[]{:S(2)}, u32[]{:S(2)}) collective-permute-start(bf16[9,16,512]{2,1,0:T(8,128)(2,1)S(1)} %get-tuple-element.141.refs_6_), channel_id=1, source_target_pairs={{0,8},{4,12},{8,0},{12,4},{1,9},{5,13},{9,1},{13,5},{2,10},{6,14},... | collective-permute-start | bytes 442376 | tf_op jit(solution)/shard_map/ppermute | solution.py:629
  171.4 8.4 %shard_map.251 = (bf16[5,5,6,512]{3,2,1,0:T(8,128)(2,1)}, bf16[7,7,2,512]{3,2,1,0:T(2,128)(2,1)}, bf16[9,9,2,512]{3,2,1,0:T(2,128)(2,1)}, f32[5,5,6,512]{3,2,1,0...) custom-call(bf16[544,512]{1,0:T(8,128)(2,1)} %get-tuple-element.111.refs_0_, ...), custom_call_target="tpu_custom_call" | custom-call | tf_op jit(solution)/shard_map/pallas_call | solution.py:605
  180.0 1.5 collective-permute-start.44
  181.6 1.0 collective-permute-done.41
  182.7 1.5 collective-permute-start.43
  184.3 0.7 multiply_subtract_fusion
  184.9 1.8 collective-permute-done.44
  186.7 1.6 collective-permute-done.43
  188.4 2.7 %fusion.5 = (f32[2,3,3,512,32]{3,4,2,1,0:T(8,128)}, f32[2,3,3,512,32]{3,4,2,1,0:T(8,128)}, f32[2,3,3,512,32]{3,4,2,1,0:T(8,128)}) fusion(f32[2,3,3,512,32]{3,4,2,1,0:T(8,128)S(1)} %copy-done.38, bf16[1,3,3,16,512]{4,3,2,1,0:T(8,128)(2,1)S(1)} %bitcast.91, bf16[1,3,3,16,512]{4,3,2,1,0:T(8,128)(2,1)S(1)} %bitcast.90, ...), kind=kLoop, calls=%fused_computation.10 | loop fusion | flops 6488064 | bytes 7667712 | tf_op jit(solution)/shard_map/transpose | solution.py:1022
  (158 shorter events, 9.3 us)
Async XLA Ops:
  2.1 13.4 %copy-start.8 = (bf16[6,5,5,512]{3,0,2,1:T(8,128)(2,1)S(1)}, bf16[6,5,5,512]{3,0,2,1:T(8,128)(2,1)}, u32[]{:S(2)}) copy-start(bf16[6,5,5,512]{3,0,2,1:T(8,128)(2,1)} %param.21) | copy-start | bytes 460804
  2.1 13.3 %copy-start.9 = (bf16[2,9,9,512]{3,0,2,1:T(2,128)(2,1)S(1)}, bf16[2,9,9,512]{3,0,2,1:T(2,128)(2,1)}, u32[]{:S(2)}) copy-start(bf16[2,9,9,512]{3,0,2,1:T(2,128)(2,1)} %param.23) | copy-start | bytes 497668
  2.1 13.3 %copy-start.12 = (bf16[2,7,7,512]{3,0,2,1:T(2,128)(2,1)S(1)}, bf16[2,7,7,512]{3,0,2,1:T(2,128)(2,1)}, u32[]{:S(2)}) copy-start(bf16[2,7,7,512]{3,0,2,1:T(2,128)(2,1)} %param.22) | copy-start | bytes 301060
  2.2 26.1 %copy-start.24 = (bf16[1,3,3,32,512]{4,3,2,1,0:T(8,128)(2,1)}, bf16[1,3,3,32,512]{4,3,2,1,0:T(8,128)(2,1)S(1)}, u32[]{:S(2)}) copy-start(bf16[1,3,3,32,512]{4,3,2,1,0:T(8,128)(2,1)S(1)} %get-tuple-element.149) | copy-start | bytes 884740
  2.2 12.5 %collective-permute-start.1 = (bf16[1,9,32,512]{3,2,1,0:T(8,128)(2,1)S(1)}, bf16[1,9,32,512]{3,2,1,0:T(8,128)(2,1)S(1)}, u32[]{:S(2)}, u32[]{:S(2)}) collective-permute-start(bf16[1,9,32,512]{3,2,1,0:T(8,128)(2,1)S(1)} %bitcast.86), channel_id=1, source_target_pairs={{0,2},{2,0},{1,3},{3,1},{4,6},{6,4},{5,7},{7,5},{8,10},{10,8},{9,1... | collective-permute-start | bytes 884744 | tf_op jit(solution)/shard_map/ppermute | solution.py:629
  5.2 9.4 %collective-permute-start.3 = (bf16[1,9,32,256]{3,2,1,0:T(8,128)(2,1)S(1)}, bf16[1,9,32,256]{3,2,1,0:T(8,128)(2,1)S(1)}, u32[]{:S(2)}, u32[]{:S(2)}) collective-permute-start(bf16[1,9,32,256]{3,2,1,0:T(8,128)(2,1)S(1)} %get-tuple-element.147), channel_id=1, source_target_pairs={{0,8},{4,12},{8,0},{12,4},{1,9},{5,13},{9,1},{13,5},{2,10},{6,14},... | collective-permute-start | bytes 442376 | tf_op jit(solution)/shard_map/ppermute | solution.py:629
  10.6 12.1 %copy-start = (f32[544,128]{1,0:T(8,128)}, f32[544,128]{1,0:T(8,128)S(1)}, u32[]{:S(2)}) copy-start(f32[544,128]{1,0:T(8,128)S(1)} %get-tuple-element.74.refs_1_.refs_2_.refs_4_.refs_5_) | copy-start | bytes 835588
  10.6 14.4 %collective-permute-start.5 = (bf16[560,512]{1,0:T(8,128)(2,1)}, bf16[560,512]{1,0:T(8,128)(2,1)S(1)}, u32[]{:S(2)}, u32[]{:S(2)}) collective-permute-start(bf16[560,512]{1,0:T(8,128)(2,1)} %get-tuple-element.99.refs_0_.refs_5_.refs_4_), channel_id=1, source_target_pairs={{0,2},{2,0},{1,3},{3,1},{4,6},{6,4},{5,7},{7,5},{8,10},{10,8},{9,1... | collective-permute-start | bytes 1720328 | tf_op jit(solution)/shard_map/ppermute | solution.py:629
  11.1 14.1 %collective-permute-start.6 = (bf16[560,512]{1,0:T(8,128)(2,1)}, bf16[560,512]{1,0:T(8,128)(2,1)S(1)}, u32[]{:S(2)}, u32[]{:S(2)}) collective-permute-start(bf16[560,512]{1,0:T(8,128)(2,1)} %get-tuple-element.99.refs_0_.refs_5_.refs_4_), channel_id=1, source_target_pairs={{0,16},{16,0},{1,17},{17,1},{2,18},{18,2},{3,19},{19,3},{4,20},{20... | collective-permute-start | bytes 1720328 | tf_op jit(solution)/shard_map/ppermute | solution.py:629
  14.7 7.9 %collective-permute-start.4 = (bf16[2,9,32,256]{3,2,1,0:T(8,128)(2,1)S(1)}, bf16[2,9,32,256]{3,2,1,0:T(8,128)(2,1)S(1)}, u32[]{:S(2)}, u32[]{:S(2)}) collective-permute-start(bf16[2,9,32,256]{3,2,1,0:T(8,128)(2,1)S(1)} %pad_maximum_fusion.2), channel_id=1, source_target_pairs={{0,4},{4,0},{8,12},{12,8},{1,5},{5,1},{9,13},{13,9},{2,6},{6,2},{1... | collective-permute-start | bytes 884744 | tf_op jit(solution)/shard_map/ppermute | solution.py:629
  22.7 26.4 %copy-start.20 = (bf16[3,9,32,256]{3,2,1,0:T(8,128)(2,1)}, bf16[3,9,32,256]{3,2,1,0:T(8,128)(2,1)S(1)}, u32[]{:S(2)}) copy-start(bf16[3,9,32,256]{3,2,1,0:T(8,128)(2,1)S(1)} %pad_maximum_fusion.refs_7_.refs_4_) | copy-start | bytes 1327108
  25.0 24.1 %copy-start.4 = (bf16[560,512]{1,0:T(8,128)(2,1)}, bf16[560,512]{1,0:T(8,128)(2,1)S(1)}, u32[]{:S(2)}) copy-start(bf16[560,512]{1,0:T(8,128)(2,1)S(1)} %collective-permute-done.5.refs_17_.refs_14_.refs_3_.refs_5_) | copy-start | bytes 1720324
  25.2 23.9 %copy-start.17 = (bf16[560,512]{1,0:T(8,128)(2,1)}, bf16[560,512]{1,0:T(8,128)(2,1)S(1)}, u32[]{:S(2)}) copy-start(bf16[560,512]{1,0:T(8,128)(2,1)S(1)} %collective-permute-done.6.refs_18_.refs_15_.refs_4_.refs_6_) | copy-start | bytes 1720324
  25.2 10.2 %collective-permute-start.10 = (bf16[3,9,32,256]{3,2,1,0:T(8,128)(2,1)S(1)}, bf16[3,9,32,256]{3,2,1,0:T(8,128)(2,1)S(1)}, u32[]{:S(2)}, u32[]{:S(2)}) collective-permute-start(bf16[3,9,32,256]{3,2,1,0:T(8,128)(2,1)S(1)} %pad_maximum_fusion.refs_7_.refs_4_), channel_id=1, source_target_pairs={{0,16},{16,0},{1,17},{17,1},{2,18},{18,2},{3,19},{19,3},{4,20},{20... | collective-permute-start | bytes 1327112 | tf_op jit(solution)/shard_map/ppermute | solution.py:629
  26.8 11.0 %collective-permute-start.8 = (bf16[3,9,32,256]{3,2,1,0:T(8,128)(2,1)S(1)}, bf16[3,9,32,256]{3,2,1,0:T(8,128)(2,1)S(1)}, u32[]{:S(2)}, u32[]{:S(2)}) collective-permute-start(bf16[3,9,32,256]{3,2,1,0:T(8,128)(2,1)S(1)} %pad_maximum_fusion.refs_7_.refs_4_), channel_id=1, source_target_pairs={{0,2},{2,0},{1,3},{3,1},{4,6},{6,4},{5,7},{7,5},{8,10},{10,8},{9,1... | collective-permute-start | bytes 1327112 | tf_op jit(solution)/shard_map/ppermute | solution.py:629
  28.2 11.4 %collective-permute-start = (bf16[1,9,32,512]{3,2,1,0:T(8,128)(2,1)S(1)}, bf16[1,9,32,512]{3,2,1,0:T(8,128)(2,1)S(1)}, u32[]{:S(2)}, u32[]{:S(2)}) collective-permute-start(bf16[1,9,32,512]{3,2,1,0:T(8,128)(2,1)S(1)} %bitcast.87), channel_id=1, source_target_pairs={{0,1},{1,0},{2,3},{3,2},{4,5},{5,4},{6,7},{7,6},{8,9},{9,8},{10,11... | collective-permute-start | bytes 884744 | tf_op jit(solution)/shard_map/ppermute | solution.py:629
  28.2 11.3 %collective-permute-start.19 = (bf16[1,9,32,256]{3,2,1,0:T(8,128)(2,1)S(1)}, bf16[1,9,32,256]{3,2,1,0:T(8,128)(2,1)S(1)}, u32[]{:S(2)}, u32[]{:S(2)}) collective-permute-start(bf16[1,9,32,256]{3,2,1,0:T(8,128)(2,1)S(1)} %get-tuple-element.83), channel_id=1, source_target_pairs={{0,8},{4,12},{8,0},{12,4},{1,9},{5,13},{9,1},{13,5},{2,10},{6,14},... | collective-permute-start | bytes 442376 | tf_op jit(solution)/shard_map/ppermute | solution.py:629
  30.4 10.9 %collective-permute-start.2 = (bf16[1,9,32,512]{3,2,1,0:T(8,128)(2,1)}, bf16[1,9,32,512]{3,2,1,0:T(8,128)(2,1)S(1)}, u32[]{:S(2)}, u32[]{:S(2)}) collective-permute-start(bf16[1,9,32,512]{3,2,1,0:T(8,128)(2,1)} %copy-done.34), channel_id=1, source_target_pairs={{0,1},{1,0},{2,3},{3,2},{4,5},{5,4},{6,7},{7,6},{8,9},{9,8},{10,11... | collective-permute-start | bytes 884744 | tf_op jit(solution)/shard_map/ppermute | solution.py:629
  35.5 13.6 %copy-start.22 = (bf16[3,9,32,256]{3,2,1,0:T(8,128)(2,1)}, bf16[3,9,32,256]{3,2,1,0:T(8,128)(2,1)S(1)}, u32[]{:S(2)}) copy-start(bf16[3,9,32,256]{3,2,1,0:T(8,128)(2,1)S(1)} %collective-permute-done.10.refs_11_.refs_8_) | copy-start | bytes 1327108
  35.5 13.0 %collective-permute-start.17 = (bf16[1,9,32,512]{3,2,1,0:T(8,128)(2,1)S(1)}, bf16[1,9,32,512]{3,2,1,0:T(8,128)(2,1)S(1)}, u32[]{:S(2)}, u32[]{:S(2)}) collective-permute-start(bf16[1,9,32,512]{3,2,1,0:T(8,128)(2,1)S(1)} %bitcast.72), channel_id=1, source_target_pairs={{0,2},{2,0},{1,3},{3,1},{4,6},{6,4},{5,7},{7,5},{8,10},{10,8},{9,1... | collective-permute-start | bytes 884744 | tf_op jit(solution)/shard_map/ppermute | solution.py:629
  37.8 15.1 %copy-start.23 = (bf16[3,9,32,256]{3,2,1,0:T(8,128)(2,1)}, bf16[3,9,32,256]{3,2,1,0:T(8,128)(2,1)S(1)}, u32[]{:S(2)}) copy-start(bf16[3,9,32,256]{3,2,1,0:T(8,128)(2,1)S(1)} %collective-permute-done.8.refs_9_.refs_6_) | copy-start | bytes 1327108
  37.8 10.2 %collective-permute-start.12 = (bf16[3,9,16,256]{3,2,1,0:T(8,128)(2,1)S(1)}, bf16[3,9,16,256]{3,2,1,0:T(8,128)(2,1)S(1)}, u32[]{:S(2)}, u32[]{:S(2)}) collective-permute-start(bf16[3,9,16,256]{3,2,1,0:T(8,128)(2,1)S(1)} %slice.89), channel_id=1, source_target_pairs={{0,2},{2,0},{1,3},{3,1},{4,6},{6,4},{5,7},{7,5},{8,10},{10,8},{9,1... | collective-permute-start | bytes 663560 | tf_op jit(solution)/shard_map/ppermute | solution.py:629
  39.6 8.4 %collective-permute-start.13 = (bf16[3,9,16,256]{3,2,1,0:T(8,128)(2,1)S(1)}, bf16[3,9,16,256]{3,2,1,0:T(8,128)(2,1)S(1)}, u32[]{:S(2)}, u32[]{:S(2)}) collective-permute-start(bf16[3,9,16,256]{3,2,1,0:T(8,128)(2,1)S(1)} %slice.90), channel_id=1, source_target_pairs={{0,16},{16,0},{1,17},{17,1},{2,18},{18,2},{3,19},{19,3},{4,20},{20... | collective-permute-start | bytes 663560 | tf_op jit(solution)/shard_map/ppermute | solution.py:629
  39.7 13.2 %copy-start.35 = (bf16[1,9,32,512]{3,2,1,0:T(8,128)(2,1)}, bf16[1,9,32,512]{3,2,1,0:T(8,128)(2,1)S(1)}, u32[]{:S(2)}) copy-start(bf16[1,9,32,512]{3,2,1,0:T(8,128)(2,1)S(1)} %collective-permute-done.refs_4_.refs_1_) | copy-start | bytes 884740
  39.7 8.9 %collective-permute-start.20 = (bf16[2,9,32,256]{3,2,1,0:T(8,128)(2,1)S(1)}, bf16[2,9,32,256]{3,2,1,0:T(8,128)(2,1)S(1)}, u32[]{:S(2)}, u32[]{:S(2)}) collective-permute-start(bf16[2,9,32,256]{3,2,1,0:T(8,128)(2,1)S(1)} %pad_maximum_fusion.3), channel_id=1, source_target_pairs={{0,4},{4,0},{8,12},{12,8},{1,5},{5,1},{9,13},{13,9},{2,6},{6,2},{1... | collective-permute-start | bytes 884744 | tf_op jit(solution)/shard_map/ppermute | solution.py:629
  41.4 7.8 %collective-permute-start.7 = (bf16[3,9,32,256]{3,2,1,0:T(8,128)(2,1)S(1)}, bf16[3,9,32,256]{3,2,1,0:T(8,128)(2,1)S(1)}, u32[]{:S(2)}, u32[]{:S(2)}) collective-permute-start(bf16[3,9,32,256]{3,2,1,0:T(8,128)(2,1)S(1)} %pad_maximum_fusion.refs_7_.refs_4_), channel_id=1, source_target_pairs={{0,1},{1,0},{2,3},{3,2},{4,5},{5,4},{6,7},{7,6},{8,9},{9,8},{10,11... | collective-permute-start | bytes 1327112 | tf_op jit(solution)/shard_map/ppermute | solution.py:629
  48.0 4.8 %collective-permute-start.11 = (bf16[3,9,32,256]{3,2,1,0:T(8,128)(2,1)S(1)}, bf16[3,9,32,256]{3,2,1,0:T(8,128)(2,1)S(1)}, u32[]{:S(2)}, u32[]{:S(2)}) collective-permute-start(bf16[3,9,32,256]{3,2,1,0:T(8,128)(2,1)S(1)} %collective-permute-done.10.refs_11_.refs_8_), channel_id=1, source_target_pairs={{0,1},{1,0},{2,3},{3,2},{4,5},{5,4},{6,7},{7,6},{8,9},{9,8},{10,11... | collective-permute-start | bytes 1327112 | tf_op jit(solution)/shard_map/ppermute | solution.py:629
  48.0 4.8 %collective-permute-start.9 = (bf16[3,9,32,256]{3,2,1,0:T(8,128)(2,1)S(1)}, bf16[3,9,32,256]{3,2,1,0:T(8,128)(2,1)S(1)}, u32[]{:S(2)}, u32[]{:S(2)}) collective-permute-start(bf16[3,9,32,256]{3,2,1,0:T(8,128)(2,1)S(1)} %collective-permute-done.8.refs_9_.refs_6_), channel_id=1, source_target_pairs={{0,1},{1,0},{2,3},{3,2},{4,5},{5,4},{6,7},{7,6},{8,9},{9,8},{10,11... | collective-permute-start | bytes 1327112 | tf_op jit(solution)/shard_map/ppermute | solution.py:629
  48.5 2.2 %collective-permute-start.14 = (bf16[3,9,16,256]{3,2,1,0:T(8,128)(2,1)S(1)}, bf16[3,9,16,256]{3,2,1,0:T(8,128)(2,1)S(1)}, u32[]{:S(2)}, u32[]{:S(2)}) collective-permute-start(bf16[3,9,16,256]{3,2,1,0:T(8,128)(2,1)S(1)} %collective-permute-done.12.refs_13_.refs_10_), channel_id=1, source_target_pairs={{0,1},{1,0},{2,3},{3,2},{4,5},{5,4},{6,7},{7,6},{8,9},{9,8},{10,11... | collective-permute-start | bytes 663560 | tf_op jit(solution)/shard_map/ppermute | solution.py:629
  48.6 3.9 %collective-permute-start.15 = (bf16[3,9,16,256]{3,2,1,0:T(8,128)(2,1)S(1)}, bf16[3,9,16,256]{3,2,1,0:T(8,128)(2,1)S(1)}, u32[]{:S(2)}, u32[]{:S(2)}) collective-permute-start(bf16[3,9,16,256]{3,2,1,0:T(8,128)(2,1)S(1)} %collective-permute-done.13.refs_15_.refs_12_), channel_id=1, source_target_pairs={{0,1},{1,0},{2,3},{3,2},{4,5},{5,4},{6,7},{7,6},{8,9},{9,8},{10,11... | collective-permute-start | bytes 663560 | tf_op jit(solution)/shard_map/ppermute | solution.py:629
  49.1 17.4 %copy-start.21 = (bf16[3,9,32,256]{3,2,1,0:T(8,128)(2,1)}, bf16[3,9,32,256]{3,2,1,0:T(8,128)(2,1)S(1)}, u32[]{:S(2)}) copy-start(bf16[3,9,32,256]{3,2,1,0:T(8,128)(2,1)S(1)} %pad_maximum_fusion.1.refs_7_.refs_9_) | copy-start | bytes 1327108
  49.1 27.0 %collective-permute-start.24 = (bf16[3,9,32,256]{3,2,1,0:T(8,128)(2,1)S(1)}, bf16[3,9,32,256]{3,2,1,0:T(8,128)(2,1)S(1)}, u32[]{:S(2)}, u32[]{:S(2)}) collective-permute-start(bf16[3,9,32,256]{3,2,1,0:T(8,128)(2,1)S(1)} %pad_maximum_fusion.1.refs_7_.refs_9_), channel_id=1, source_target_pairs={{0,16},{16,0},{1,17},{17,1},{2,18},{18,2},{3,19},{19,3},{4,20},{20... | collective-permute-start | bytes 1327112 | tf_op jit(solution)/shard_map/ppermute | solution.py:629
  50.7 25.6 %collective-permute-start.22 = (bf16[3,9,32,256]{3,2,1,0:T(8,128)(2,1)S(1)}, bf16[3,9,32,256]{3,2,1,0:T(8,128)(2,1)S(1)}, u32[]{:S(2)}, u32[]{:S(2)}) collective-permute-start(bf16[3,9,32,256]{3,2,1,0:T(8,128)(2,1)S(1)} %pad_maximum_fusion.1.refs_7_.refs_9_), channel_id=1, source_target_pairs={{0,2},{2,0},{1,3},{3,1},{4,6},{6,4},{5,7},{7,5},{8,10},{10,8},{9,1... | collective-permute-start | bytes 1327112 | tf_op jit(solution)/shard_map/ppermute | solution.py:629
  52.5 24.3 %collective-permute-start.26 = (bf16[3,9,32,256]{3,2,1,0:T(8,128)(2,1)S(1)}, bf16[3,9,32,256]{3,2,1,0:T(8,128)(2,1)}, u32[]{:S(2)}, u32[]{:S(2)}) collective-permute-start(bf16[3,9,32,256]{3,2,1,0:T(8,128)(2,1)S(1)} %pad_maximum_fusion.1.refs_7_.refs_9_), channel_id=1, source_target_pairs={{0,18},{2,16},{16,2},{18,0},{1,19},{3,17},{17,3},{19,1},{4,22},{6,... | collective-permute-start | bytes 1327112 | tf_op jit(solution)/shard_map/ppermute | solution.py:633
  60.3 16.5 %all-to-all-start = ((f32[32,2,640]{2,1,0:T(2,128)}), f32[32,2,640]{2,1,0:T(2,128)S(1)}, u32[]{:S(2)}, u32[]{:S(2)}) async-start(f32[32,2,640]{2,1,0:T(2,128)} %get-tuple-element.81.refs_16_), calls=%async_computation | async-start | bytes 327680 | tf_op jit(solution)/shard_map/all_to_all | solution.py:853
  66.3 13.6 %copy-start.18 = (bf16[560,512]{1,0:T(8,128)(2,1)S(1)}, bf16[560,512]{1,0:T(8,128)(2,1)}, u32[]{:S(2)}) copy-start(bf16[560,512]{1,0:T(8,128)(2,1)} %get-tuple-element.99.refs_0_.refs_5_.refs_4_) | copy-start | bytes 1720324
  66.4 17.7 %copy-start.1 = (f32[544,128]{1,0:T(8,128)S(1)}, f32[544,128]{1,0:T(8,128)}, u32[]{:S(2)}) copy-start(f32[544,128]{1,0:T(8,128)} %copy-done) | copy-start | bytes 835588
  66.4 10.5 %collective-permute-start.16 = (bf16[1,9,32,512]{3,2,1,0:T(8,128)(2,1)S(1)}, bf16[1,9,32,512]{3,2,1,0:T(8,128)(2,1)}, u32[]{:S(2)}, u32[]{:S(2)}) collective-permute-start(bf16[1,9,32,512]{3,2,1,0:T(8,128)(2,1)S(1)} %bitcast.73), channel_id=1, source_target_pairs={{0,1},{1,0},{2,3},{3,2},{4,5},{5,4},{6,7},{7,6},{8,9},{9,8},{10,11... | collective-permute-start | bytes 884744 | tf_op jit(solution)/shard_map/ppermute | solution.py:629
  66.5 15.9 %collective-permute-start.21 = (bf16[3,9,32,256]{3,2,1,0:T(8,128)(2,1)S(1)}, bf16[3,9,32,256]{3,2,1,0:T(8,128)(2,1)}, u32[]{:S(2)}, u32[]{:S(2)}) collective-permute-start(bf16[3,9,32,256]{3,2,1,0:T(8,128)(2,1)S(1)} %pad_maximum_fusion.1.refs_7_.refs_9_), channel_id=1, source_target_pairs={{0,1},{1,0},{2,3},{3,2},{4,5},{5,4},{6,7},{7,6},{8,9},{9,8},{10,11... | collective-permute-start | bytes 1327112 | tf_op jit(solution)/shard_map/ppermute | solution.py:629
  76.2 6.2 %collective-permute-start.25 = (bf16[3,9,32,256]{3,2,1,0:T(8,128)(2,1)S(1)}, bf16[3,9,32,256]{3,2,1,0:T(8,128)(2,1)S(1)}, u32[]{:S(2)}, u32[]{:S(2)}) collective-permute-start(bf16[3,9,32,256]{3,2,1,0:T(8,128)(2,1)S(1)} %collective-permute-done.24.refs_11_.refs_13_), channel_id=1, source_target_pairs={{0,1},{1,0},{2,3},{3,2},{4,5},{5,4},{6,7},{7,6},{8,9},{9,8},{10,11... | collective-permute-start | bytes 1327112 | tf_op jit(solution)/shard_map/ppermute | solution.py:629
  76.3 6.1 %collective-permute-start.23 = (bf16[3,9,32,256]{3,2,1,0:T(8,128)(2,1)S(1)}, bf16[3,9,32,256]{3,2,1,0:T(8,128)(2,1)}, u32[]{:S(2)}, u32[]{:S(2)}) collective-permute-start(bf16[3,9,32,256]{3,2,1,0:T(8,128)(2,1)S(1)} %collective-permute-done.22.refs_9_.refs_11_), channel_id=1, source_target_pairs={{0,1},{1,0},{2,3},{3,2},{4,5},{5,4},{6,7},{7,6},{8,9},{9,8},{10,11... | collective-permute-start | bytes 1327112 | tf_op jit(solution)/shard_map/ppermute | solution.py:629
  76.8 5.7 %collective-permute-start.27 = (bf16[3,9,32,256]{3,2,1,0:T(8,128)(2,1)}, bf16[3,9,32,256]{3,2,1,0:T(8,128)(2,1)S(1)}, u32[]{:S(2)}, u32[]{:S(2)}) collective-permute-start(bf16[3,9,32,256]{3,2,1,0:T(8,128)(2,1)} %collective-permute-done.26.refs_13_.refs_15_), channel_id=1, source_target_pairs={{0,1},{1,0},{2,3},{3,2},{4,5},{5,4},{6,7},{7,6},{8,9},{9,8},{10,11... | collective-permute-start | bytes 1327112 | tf_op jit(solution)/shard_map/ppermute | solution.py:629
  76.9 3.1 %collective-permute-start.18 = (bf16[1,9,32,512]{3,2,1,0:T(8,128)(2,1)}, bf16[1,9,32,512]{3,2,1,0:T(8,128)(2,1)S(1)}, u32[]{:S(2)}, u32[]{:S(2)}) collective-permute-start(bf16[1,9,32,512]{3,2,1,0:T(8,128)(2,1)} %copy-done.33), channel_id=1, source_target_pairs={{0,1},{1,0},{2,3},{3,2},{4,5},{5,4},{6,7},{7,6},{8,9},{9,8},{10,11... | collective-permute-start | bytes 884744 | tf_op jit(solution)/shard_map/ppermute | solution.py:629
  80.0 29.5 %collective-permute-start.28 = (bf16[560,512]{1,0:T(8,128)(2,1)S(1)}, bf16[560,512]{1,0:T(8,128)(2,1)}, u32[]{:S(2)}, u32[]{:S(2)}) collective-permute-start(bf16[560,512]{1,0:T(8,128)(2,1)S(1)} %copy-done.18), channel_id=1, source_target_pairs={{0,18},{2,16},{16,2},{18,0},{1,19},{3,17},{17,3},{19,1},{4,22},{6,... | collective-permute-start | bytes 1720328 | tf_op jit(solution)/shard_map/ppermute | solution.py:633
  91.0 12.0 %all-to-all-start.1 = ((f32[32,2,512]{2,1,0:T(2,128)}), f32[32,2,512]{2,1,0:T(2,128)S(1)}, u32[]{:S(2)}, u32[]{:S(2)}) async-start(f32[32,2,512]{2,1,0:T(2,128)} %get-tuple-element.92.refs_5_), calls=%async_computation.1 | async-start | bytes 262144 | tf_op jit(solution)/shard_map/all_to_all | solution.py:853
  106.6 10.8 %all-to-all-start.2 = ((f32[32,2,512]{2,1,0:T(2,128)}), f32[32,2,512]{2,1,0:T(2,128)S(1)}, u32[]{:S(2)}, u32[]{:S(2)}) async-start(f32[32,2,512]{2,1,0:T(2,128)} %get-tuple-element.96.refs_4_), calls=%async_computation.2 | async-start | bytes 262144 | tf_op jit(solution)/shard_map/all_to_all | solution.py:853
  120.0 10.9 %collective-permute-start.29 = (bf16[2,64,640]{2,1,0:T(8,128)(2,1)S(1)}, bf16[2,64,640]{2,1,0:T(8,128)(2,1)S(1)}, u32[]{:S(2)}, u32[]{:S(2)}) collective-permute-start(bf16[2,64,640]{2,1,0:T(8,128)(2,1)S(1)} %get-tuple-element.102), channel_id=1, source_target_pairs={{0,2},{2,0},{1,3},{3,1},{4,6},{6,4},{5,7},{7,5},{8,10},{10,8},{9,1... | collective-permute-start | bytes 491528 | tf_op jit(solution)/shard_map/ppermute | solution.py:629
  120.6 10.3 %collective-permute-start.30 = (bf16[2,64,640]{2,1,0:T(8,128)(2,1)S(1)}, bf16[2,64,640]{2,1,0:T(8,128)(2,1)S(1)}, u32[]{:S(2)}, u32[]{:S(2)}) collective-permute-start(bf16[2,64,640]{2,1,0:T(8,128)(2,1)S(1)} %get-tuple-element.103), channel_id=1, source_target_pairs={{0,16},{16,0},{1,17},{17,1},{2,18},{18,2},{3,19},{19,3},{4,20},{20... | collective-permute-start | bytes 491528 | tf_op jit(solution)/shard_map/ppermute | solution.py:629
  121.4 9.5 %collective-permute-start.31 = (bf16[2,64,640]{2,1,0:T(8,128)(2,1)S(1)}, bf16[2,64,640]{2,1,0:T(8,128)(2,1)S(1)}, u32[]{:S(2)}, u32[]{:S(2)}) collective-permute-start(bf16[2,64,640]{2,1,0:T(8,128)(2,1)S(1)} %get-tuple-element.104), channel_id=1, source_target_pairs={{0,18},{2,16},{16,2},{18,0},{1,19},{3,17},{17,3},{19,1},{4,22},{6,... | collective-permute-start | bytes 491528 | tf_op jit(solution)/shard_map/ppermute | solution.py:633
  130.9 12.2 %all-to-all-start.3 = ((f32[32,2,512]{2,1,0:T(2,128)}), f32[32,2,512]{2,1,0:T(2,128)S(1)}, u32[]{:S(2)}, u32[]{:S(2)}) async-start(f32[32,2,512]{2,1,0:T(2,128)} %get-tuple-element.105), calls=%async_computation.3 | async-start | bytes 262144 | tf_op jit(solution)/shard_map/all_to_all | solution.py:853
  143.2 6.4 %collective-permute-start.35 = (bf16[4,9,16,512]{3,2,1,0:T(8,128)(2,1)}, bf16[4,9,16,512]{3,2,1,0:T(8,128)(2,1)S(1)}, u32[]{:S(2)}, u32[]{:S(2)}) collective-permute-start(bf16[4,9,16,512]{3,2,1,0:T(8,128)(2,1)} %get-tuple-element.117.refs_6_), channel_id=1, source_target_pairs={{0,1},{1,0},{2,3},{3,2},{4,5},{5,4},{6,7},{7,6},{8,9},{9,8},{10,11... | collective-permute-start | bytes 1769480 | tf_op jit(solution)/shard_map/ppermute | solution.py:629
  146.0 7.1 %collective-permute-start.32 = (bf16[2,64,640]{2,1,0:T(8,128)(2,1)S(1)}, bf16[2,64,640]{2,1,0:T(8,128)(2,1)S(1)}, u32[]{:S(2)}, u32[]{:S(2)}) collective-permute-start(bf16[2,64,640]{2,1,0:T(8,128)(2,1)S(1)} %get-tuple-element.114), channel_id=1, source_target_pairs={{0,2},{2,0},{1,3},{3,1},{4,6},{6,4},{5,7},{7,5},{8,10},{10,8},{9,1... | collective-permute-start | bytes 491528 | tf_op jit(solution)/shard_map/ppermute | solution.py:629
  146.5 8.9 %collective-permute-start.33 = (bf16[2,64,640]{2,1,0:T(8,128)(2,1)S(1)}, bf16[2,64,640]{2,1,0:T(8,128)(2,1)S(1)}, u32[]{:S(2)}, u32[]{:S(2)}) collective-permute-start(bf16[2,64,640]{2,1,0:T(8,128)(2,1)S(1)} %get-tuple-element.115), channel_id=1, source_target_pairs={{0,16},{16,0},{1,17},{17,1},{2,18},{18,2},{3,19},{19,3},{4,20},{20... | collective-permute-start | bytes 491528 | tf_op jit(solution)/shard_map/ppermute | solution.py:629
  148.0 8.2 %collective-permute-start.34 = (bf16[2,64,640]{2,1,0:T(8,128)(2,1)S(1)}, bf16[2,64,640]{2,1,0:T(8,128)(2,1)S(1)}, u32[]{:S(2)}, u32[]{:S(2)}) collective-permute-start(bf16[2,64,640]{2,1,0:T(8,128)(2,1)S(1)} %get-tuple-element.116), channel_id=1, source_target_pairs={{0,18},{2,16},{16,2},{18,0},{1,19},{3,17},{17,3},{19,1},{4,22},{6,... | collective-permute-start | bytes 491528 | tf_op jit(solution)/shard_map/ppermute | solution.py:633
  149.7 14.7 %collective-permute-start.36 = (bf16[9,16,512]{2,1,0:T(8,128)(2,1)S(1)}, bf16[9,16,512]{2,1,0:T(8,128)(2,1)S(1)}, u32[]{:S(2)}, u32[]{:S(2)}) collective-permute-start(bf16[9,16,512]{2,1,0:T(8,128)(2,1)S(1)} %get-tuple-element.145.refs_8_), channel_id=1, source_target_pairs={{0,4},{4,0},{8,12},{12,8},{1,5},{5,1},{9,13},{13,9},{2,6},{6,2},{1... | collective-permute-start | bytes 442376 | tf_op jit(solution)/shard_map/ppermute | solution.py:629
  150.2 14.2 %collective-permute-start.37 = (bf16[9,16,512]{2,1,0:T(8,128)(2,1)S(1)}, bf16[9,16,512]{2,1,0:T(8,128)(2,1)S(1)}, u32[]{:S(2)}, u32[]{:S(2)}) collective-permute-start(bf16[9,16,512]{2,1,0:T(8,128)(2,1)S(1)} %get-tuple-element.144.refs_9_), channel_id=1, source_target_pairs={{0,8},{4,12},{8,0},{12,4},{1,9},{5,13},{9,1},{13,5},{2,10},{6,14},... | collective-permute-start | bytes 442376 | tf_op jit(solution)/shard_map/ppermute | solution.py:629
  153.1 11.4 %collective-permute-start.38 = (bf16[9,16,512]{2,1,0:T(8,128)(2,1)S(1)}, bf16[9,16,512]{2,1,0:T(8,128)(2,1)S(1)}, u32[]{:S(2)}, u32[]{:S(2)}) collective-permute-start(bf16[9,16,512]{2,1,0:T(8,128)(2,1)S(1)} %get-tuple-element.143.refs_10_), channel_id=1, source_target_pairs={{0,12},{4,8},{8,4},{12,0},{1,13},{5,9},{9,5},{13,1},{2,14},{6,10},... | collective-permute-start | bytes 442376 | tf_op jit(solution)/shard_map/ppermute | solution.py:629
  164.5 2.3 %collective-permute-start.39 = (bf16[4,9,16,512]{3,2,1,0:T(8,128)(2,1)}, bf16[4,9,16,512]{3,2,1,0:T(8,128)(2,1)S(1)}, u32[]{:S(2)}, u32[]{:S(2)}) collective-permute-start(bf16[4,9,16,512]{3,2,1,0:T(8,128)(2,1)} %get-tuple-element.120), channel_id=1, source_target_pairs={{0,1},{1,0},{2,3},{3,2},{4,5},{5,4},{6,7},{7,6},{8,9},{9,8},{10,11... | collective-permute-start | bytes 1769480 | tf_op jit(solution)/shard_map/ppermute | solution.py:629
  166.9 14.6 %collective-permute-start.40 = (bf16[9,16,512]{2,1,0:T(8,128)(2,1)S(1)}, bf16[9,16,512]{2,1,0:T(8,128)(2,1)S(1)}, u32[]{:S(2)}, u32[]{:S(2)}) collective-permute-start(bf16[9,16,512]{2,1,0:T(8,128)(2,1)S(1)} %get-tuple-element.142.refs_5_), channel_id=1, source_target_pairs={{0,4},{4,0},{8,12},{12,8},{1,5},{5,1},{9,13},{13,9},{2,6},{6,2},{1... | collective-permute-start | bytes 442376 | tf_op jit(solution)/shard_map/ppermute | solution.py:629
  168.6 14.0 %collective-permute-start.41 = (bf16[9,16,512]{2,1,0:T(8,128)(2,1)S(1)}, bf16[9,16,512]{2,1,0:T(8,128)(2,1)S(1)}, u32[]{:S(2)}, u32[]{:S(2)}) collective-permute-start(bf16[9,16,512]{2,1,0:T(8,128)(2,1)S(1)} %get-tuple-element.141.refs_6_), channel_id=1, source_target_pairs={{0,8},{4,12},{8,0},{12,4},{1,9},{5,13},{9,1},{13,5},{2,10},{6,14},... | collective-permute-start | bytes 442376 | tf_op jit(solution)/shard_map/ppermute | solution.py:629
  170.9 11.7 %collective-permute-start.42 = (bf16[9,16,512]{2,1,0:T(8,128)(2,1)S(1)}, bf16[9,16,512]{2,1,0:T(8,128)(2,1)S(1)}, u32[]{:S(2)}, u32[]{:S(2)}) collective-permute-start(bf16[9,16,512]{2,1,0:T(8,128)(2,1)S(1)} %get-tuple-element.140.refs_7_), channel_id=1, source_target_pairs={{0,12},{4,8},{8,4},{12,0},{1,13},{5,9},{9,5},{13,1},{2,14},{6,10},... | collective-permute-start | bytes 442376 | tf_op jit(solution)/shard_map/ppermute | solution.py:629
  171.4 16.9 %copy-start.39 = (f32[2,3,3,512,32]{3,4,2,1,0:T(8,128)S(1)}, f32[2,3,3,512,32]{3,4,2,1,0:T(8,128)}, u32[]{:S(2)}) copy-start(f32[2,3,3,512,32]{3,4,2,1,0:T(8,128)} %param.26) | copy-start | bytes 3538948
  180.0 6.7 %collective-permute-start.44 = (bf16[9,16,512]{2,1,0:T(8,128)(2,1)S(1)}, bf16[9,16,512]{2,1,0:T(8,128)(2,1)S(1)}, u32[]{:S(2)}, u32[]{:S(2)}) collective-permute-start(bf16[9,16,512]{2,1,0:T(8,128)(2,1)S(1)} %add_convert_fusion), channel_id=1, source_target_pairs={{0,16},{16,0},{1,17},{17,1},{2,18},{18,2},{3,19},{19,3},{4,20},{20... | collective-permute-start | bytes 442376 | tf_op jit(solution)/shard_map/ppermute | solution.py:629
  182.7 5.6 %collective-permute-start.43 = (bf16[9,16,512]{2,1,0:T(8,128)(2,1)S(1)}, bf16[9,16,512]{2,1,0:T(8,128)(2,1)S(1)}, u32[]{:S(2)}, u32[]{:S(2)}) collective-permute-start(bf16[9,16,512]{2,1,0:T(8,128)(2,1)S(1)} %add_convert_fusion.1), channel_id=1, source_target_pairs={{0,16},{16,0},{1,17},{17,1},{2,18},{18,2},{3,19},{19,3},{4,20},{20... | collective-permute-start | bytes 442376 | tf_op jit(solution)/shard_map/ppermute | solution.py:629
  (30 other events, 142.2 us)

commit v3 on v2

--- a/solution.py
+++ b/solution.py
@@ -691,10 +691,11 @@
     axes = ("y", "z", "x", "c")
     shard_axes = ("z", "x", "c")
 
-    def weights(self, low, x, back):
-        half = low.shape[3] // 2
-        first, second = lax.dynamic_slice_in_dim(low, lax.axis_index("y") * half, half, 3)
-        one, two = Gather(low[0], first), Gather(low[1], second)
+    def weights(self, kernels, x, back):
+        half = kernels.shape[3] // 2
+        start = lax.axis_index("y") * half
+        low = [kernels[0].astype(BF16), behind(kernels[1], (x,)).astype(BF16)]
+        one, two = (Gather(part, lax.dynamic_slice_in_dim(part, start, half, 2)) for part in low)
         one.along_two()
         one.beside()
         self.pixels = x
@@ -777,7 +778,8 @@
 
     sides = corners = ()
 
-    def weights(self, low, x, back):
+    def weights(self, kernels, x, back):
+        low = kernels.astype(BF16)
         full = lax.all_gather(low, "fsdp", axis=2, tiled=True)
         first, self.second = [Whole(array, low.shape[2]) for array in full]
         return first
@@ -853,7 +855,6 @@
         return lax.all_to_all(spread, ways.axes, 0, 0, tiled=True)
 
     kernels_turned = turned(kernels)
-    low = kernels_turned.astype(BF16)
 
     buffer = pltpu.VMEM((rows, channels), F32)
     weighted = (
@@ -898,7 +899,7 @@
         (flat16,),
         (buffer,),
     )
-    weight_one = ways.weights(low, x, back)
+    weight_one = ways.weights(kernels_turned, x, back)
     sides = ways.sides
     hidden, stats = conv_call(
         forward_one,

time: 192 us -> 192 us (level)
  no operation moved by 1% of the time
where the time goes in v3:
time: 192 us; the launch traced here: 191 us
  Pallas kernels  75.6 us (39%)
  starting transfers between devices  64.3 us (33%)
  waiting for transfers between devices  39.2 us (20%)
  local copies, waits for them, and re-layouts  6.59 us (3%)
  other arithmetic  4.05 us (2%)
    pallas_call x14, Pallas kernels, call(): pl.pallas_call(kernel, out_shape=[jax.ShapeDtypeStruct(shape, dtype) for...  75.6 us
    ppermute x41, starting transfers between devices, flip(): lax.ppermute(value, axis, [(place, place ^ bit) for place in range(size)])  40.9 us
    ppermute x41, waiting for transfers between devices, flip(): lax.ppermute(value, axis, [(place, place ^ bit) for place in range(size)])  31.9 us
    all_to_all x4, starting transfers between devices, exchange(): return lax.all_to_all(spread, ways.axes, 0, 0, tiled=True)  16.8 us
    ppermute x4, starting transfers between devices, diagonal(): lax.ppermute(value, ('y', 'x'), [(place, place ^ 3) for place in range(4)])  6.64 us
    all_to_all x4, waiting for transfers between devices, exchange(): return lax.all_to_all(spread, ways.axes, 0, 0, tiled=True)  6.49 us
    unnamed x90, local copies, waits for them, and re-layouts  4 us
  transfers between devices with their start and end apart: 49, of which 18 were waited for; matrix products, arithmetic and copies ran while one was open for 1% of the time, Pallas kernels for 38%

profile of v3, /device:TPU:0, one launch (start us, length us, event | category | flops | bytes accessed | tf_op | source)
XLA Modules:
  0.0 191.1 jit_solution(492034596965440566)
XLA Ops:
  0.7 1.5 fusion.12
  2.3 3.0 %collective-permute-start.1 = (bf16[1,9,32,512]{3,2,1,0:T(8,128)(2,1)S(1)}, bf16[1,9,32,512]{3,2,1,0:T(8,128)(2,1)S(1)}, u32[]{:S(2)}, u32[]{:S(2)}) collective-permute-start(bf16[1,9,32,512]{3,2,1,0:T(8,128)(2,1)S(1)} %bitcast.81), channel_id=1, source_target_pairs={{0,2},{2,0},{1,3},{3,1},{4,6},{6,4},{5,7},{7,5},{8,10},{10,8},{9,1... | collective-permute-start | bytes 884744 | tf_op jit(solution)/shard_map/ppermute | solution.py:629
  5.3 2.7 %collective-permute-start.3 = (bf16[1,9,32,256]{3,2,1,0:T(8,128)(2,1)S(1)}, bf16[1,9,32,256]{3,2,1,0:T(8,128)(2,1)S(1)}, u32[]{:S(2)}, u32[]{:S(2)}) collective-permute-start(bf16[1,9,32,256]{3,2,1,0:T(8,128)(2,1)S(1)} %dynamic-slice_bitcast_fusion.1), channel_id=1, source_target_pairs={{0,8},{4,12},{8,0},{12,4},{1,9},{5,13},{9,1},{13,5},{2,10},{6,14},... | collective-permute-start | bytes 442376 | tf_op jit(solution)/shard_map/ppermute | solution.py:629
  8.0 2.7 %shard_map.238 = (bf16[560,512]{1,0:T(8,128)(2,1)}, f32[544,128]{1,0:T(8,128)S(1)}, f32[2,128]{1,0:T(2,128)S(1)}) custom-call(bf16[5,5,6,512]{3,2,1,0:T(8,128)(2,1)S(1)} %bitcast.72, bf16[7,7,2,512]{3,2,1,0:T(2,128)(2,1)S(1)} %bitcast.76, bf16[9,9,2,512]{3,2,1,0:T(2,128)(2,1)S(1)} %bitcast.75, f32[4,32]{1,0:T(4,128)S(1)} %copy-done.15, ...), custom_call_target="tpu_custom_call" | custom-call | tf_op jit(solution)/shard_map/pallas_call | solution.py:605
  11.2 1.5 collective-permute-start.6
  12.7 2.0 %collective-permute-done.3 = bf16[1,9,32,256]{3,2,1,0:T(8,128)(2,1)S(1)} collective-permute-done((bf16[1,9,32,256]{3,2,1,0:T(8,128)(2,1)S(1)}, bf16[1,9,32,256]{3,2,1,0:T(8,128)(2,1)S(1)}, u32[]{:S(2)}, u32[]{:S(2)}) %collective-permute-start.3) | collective-permute-done | bytes 147488 | tf_op jit(solution)/shard_map/ppermute | solution.py:629
  14.8 0.7 collective-permute-start.4
  15.5 1.2 shard_map.239.refs_6_
  16.7 6.0 %collective-permute-done.4 = bf16[2,9,32,256]{3,2,1,0:T(8,128)(2,1)S(1)} collective-permute-done((bf16[2,9,32,256]{3,2,1,0:T(8,128)(2,1)S(1)}, bf16[2,9,32,256]{3,2,1,0:T(8,128)(2,1)S(1)}, u32[]{:S(2)}, u32[]{:S(2)}) %collective-permute-start.4) | collective-permute-done | bytes 294944 | tf_op jit(solution)/shard_map/ppermute | solution.py:629
  22.8 2.3 %collective-permute-done.5.refs_17_.refs_14_.refs_3_.refs_5_ = bf16[560,512]{1,0:T(8,128)(2,1)S(1)} collective-permute-done((bf16[560,512]{1,0:T(8,128)(2,1)}, bf16[560,512]{1,0:T(8,128)(2,1)S(1)}, u32[]{:S(2)}, u32[]{:S(2)}) %collective-permute-start.5) | collective-permute-done | bytes 573472 | tf_op jit(solution)/shard_map/ppermute | solution.py:629
  25.3 1.5 collective-permute-start.10
  26.8 1.5 collective-permute-start.8
  28.3 2.2 %collective-permute-start.19 = (bf16[1,9,32,256]{3,2,1,0:T(8,128)(2,1)S(1)}, bf16[1,9,32,256]{3,2,1,0:T(8,128)(2,1)S(1)}, u32[]{:S(2)}, u32[]{:S(2)}) collective-permute-start(bf16[1,9,32,256]{3,2,1,0:T(8,128)(2,1)S(1)} %dynamic-slice_bitcast_fusion), channel_id=1, source_target_pairs={{0,8},{4,12},{8,0},{12,4},{1,9},{5,13},{9,1},{13,5},{2,10},{6,14},... | collective-permute-start | bytes 442376 | tf_op jit(solution)/shard_map/ppermute | solution.py:629
  30.8 4.7 %collective-permute-done.10.refs_11_.refs_8_ = bf16[3,9,32,256]{3,2,1,0:T(8,128)(2,1)S(1)} collective-permute-done((bf16[3,9,32,256]{3,2,1,0:T(8,128)(2,1)S(1)}, bf16[3,9,32,256]{3,2,1,0:T(8,128)(2,1)S(1)}, u32[]{:S(2)}, u32[]{:S(2)}) %collective-permute-start.10) | collective-permute-done | bytes 442400 | tf_op jit(solution)/shard_map/ppermute | solution.py:629
  35.5 2.0 %collective-permute-start.17 = (bf16[1,9,32,512]{3,2,1,0:T(8,128)(2,1)S(1)}, bf16[1,9,32,512]{3,2,1,0:T(8,128)(2,1)}, u32[]{:S(2)}, u32[]{:S(2)}) collective-permute-start(bf16[1,9,32,512]{3,2,1,0:T(8,128)(2,1)S(1)} %bitcast.68), channel_id=1, source_target_pairs={{0,2},{2,0},{1,3},{3,1},{4,6},{6,4},{5,7},{7,5},{8,10},{10,8},{9,1... | collective-permute-start | bytes 884744 | tf_op jit(solution)/shard_map/ppermute | solution.py:629
  37.9 1.7 collective-permute-start.12
  39.8 1.6 collective-permute-start.20
  41.4 6.7 %collective-permute-done.12.refs_13_.refs_10_ = bf16[3,9,16,256]{3,2,1,0:T(8,128)(2,1)S(1)} collective-permute-done((bf16[3,9,16,256]{3,2,1,0:T(8,128)(2,1)S(1)}, bf16[3,9,16,256]{3,2,1,0:T(8,128)(2,1)S(1)}, u32[]{:S(2)}, u32[]{:S(2)}) %collective-permute-start.12) | collective-permute-done | bytes 221216 | tf_op jit(solution)/shard_map/ppermute | solution.py:629
  49.2 0.7 collective-permute-start.24
  49.9 0.9 collective-permute-done.14.refs_14_.refs_11_
  50.8 1.7 collective-permute-start.22
  53.9 6.5 %shard_map.240 = (f32[544,512]{1,0:T(8,128)}, f32[32,2,640]{2,1,0:T(2,128)}) custom-call(bf16[560,512]{1,0:T(8,128)(2,1)} %get-tuple-element.101.refs_0_.refs_5_.refs_4_, f32[544,128]{1,0:T(8,128)} %copy-done, f32[2,128]{1,0:T(2,128)S(1)} %get-tuple-element.76.refs_2_, bf16[1,9,32,512]{3,2,1,0:T(8,128)(2,1)} %bitcast.84, bf16[1,9,32,512]{3,2,1,0:T(8,128)(2,1)} %copy-done.35, ...), custom_call_target="tpu_custom_call" | custom-call | tf_op jit(solution)/shard_map/pallas_call | solution.py:605
  60.4 6.0 %all-to-all-start = ((f32[32,2,640]{2,1,0:T(2,128)}), f32[32,2,640]{2,1,0:T(2,128)S(1)}, u32[]{:S(2)}, u32[]{:S(2)}) async-start(f32[32,2,640]{2,1,0:T(2,128)} %get-tuple-element.82.refs_16_), calls=%async_computation | async-start | bytes 327680 | tf_op jit(solution)/shard_map/all_to_all | solution.py:855
  67.0 9.2 %shard_map.241 = (f32[2,544,512]{2,1,0:T(8,128)}, bf16[9,512,512]{2,1,0:T(8,128)(2,1)}) custom-call(bf16[1,9,32,512]{3,2,1,0:T(8,128)(2,1)} %bitcast.85, bf16[1,9,32,512]{3,2,1,0:T(8,128)(2,1)} %copy-done.35, bf16[1,9,32,512]{3,2,1,0:T(8,128)(2,1)} %copy-done.33, bf16[1,9,32,512]{3,2,1,0:T(8,128)(2,1)} %copy-done.36, bf16[3,9,32,256]{3,2,1,0:T(8,128)(2,1)} %copy-done.19, ...), custom_call_target="tpu_custom_call" | custom-call | tf_op jit(solution)/shard_map/pallas_call | solution.py:605
  77.4 2.7 %collective-permute-done.18.refs_6_.refs_8_ = bf16[1,9,32,512]{3,2,1,0:T(8,128)(2,1)S(1)} collective-permute-done((bf16[1,9,32,512]{3,2,1,0:T(8,128)(2,1)}, bf16[1,9,32,512]{3,2,1,0:T(8,128)(2,1)S(1)}, u32[]{:S(2)}, u32[]{:S(2)}) %collective-permute-start.18) | collective-permute-done | bytes 294944 | tf_op jit(solution)/shard_map/ppermute | solution.py:629
  80.0 2.5 %collective-permute-start.28 = (bf16[560,512]{1,0:T(8,128)(2,1)S(1)}, bf16[560,512]{1,0:T(8,128)(2,1)}, u32[]{:S(2)}, u32[]{:S(2)}) collective-permute-start(bf16[560,512]{1,0:T(8,128)(2,1)S(1)} %copy-done.18), channel_id=1, source_target_pairs={{0,18},{2,16},{16,2},{18,0},{1,19},{3,17},{17,3},{19,1},{4,22},{6,... | collective-permute-start | bytes 1720328 | tf_op jit(solution)/shard_map/ppermute | solution.py:633
  82.6 0.8 copy-done.31
  83.3 0.8 copy-done.32
  84.1 7.0 %shard_map.242 = (bf16[544,512]{1,0:T(8,128)(2,1)}, f32[544,512]{1,0:T(8,128)}, f32[4,512]{1,0:T(4,128)S(1)}, f32[4,512]{1,0:T(4,128)S(1)}, f32[32,512]{1,0:T(8,128)S(1)}, /*index=5*/f32[32,2,512]{2,1,0:T(2,128)}) custom-call(f32[544,512]{1,0:T(8,128)} %get-tuple-element.81.refs_0_.refs_1_.refs_4_, f32[32,2,640]{2,1,0:T(2,128)S(1)} %all-to-all-done.refs_1_, ...), custom_call_target="tpu_custom_call" | custom-call | tf_op jit(solution)/shard_map/pallas_call | solution.py:605
  91.1 3.7 %all-to-all-start.1 = ((f32[32,2,512]{2,1,0:T(2,128)}), f32[32,2,512]{2,1,0:T(2,128)S(1)}, u32[]{:S(2)}, u32[]{:S(2)}) async-start(f32[32,2,512]{2,1,0:T(2,128)} %get-tuple-element.94.refs_5_), calls=%async_computation.1 | async-start | bytes 262144 | tf_op jit(solution)/shard_map/all_to_all | solution.py:855
  94.9 4.4 %shard_map.243.refs_7_.refs_5_ = bf16[2,544,512]{2,1,0:T(8,128)(2,1)} custom-call(f32[2,544,512]{2,1,0:T(8,128)} %get-tuple-element.90.refs_15_.refs_0_, f32[4,512]{1,0:T(4,128)S(1)} %get-tuple-element.92.refs_1_.refs_0_.refs_2_, f32[4,512]{1,0:T(4,128)S(1)} %get-tuple-element.96.refs_2_.refs_3_.refs_1_, bf16[560,512]{1,0:T(8,128)(2,1)S(1)} %copy-done.5, ...), custom_call_target="tpu_custom_call" | custom-call | tf_op jit(solution)/shard_map/pallas_call | solution.py:605
  99.3 3.8 %all-to-all-done.1.refs_1_ = f32[32,2,512]{2,1,0:T(2,128)S(1)} async-done(((f32[32,2,512]{2,1,0:T(2,128)}), f32[32,2,512]{2,1,0:T(2,128)S(1)}, u32[]{:S(2)}, u32[]{:S(2)}) %all-to-all-start.1) | async-done | bytes 131104 | tf_op jit(solution)/shard_map/all_to_all | solution.py:855
  103.1 3.6 %shard_map.244 = (bf16[544,512]{1,0:T(8,128)(2,1)}, f32[544,512]{1,0:T(8,128)}, f32[4,512]{1,0:T(4,128)S(1)}, f32[32,2,512]{2,1,0:T(2,128)}) custom-call(f32[544,512]{1,0:T(8,128)} %get-tuple-element.93.refs_0_.refs_4_, f32[32,2,512]{2,1,0:T(2,128)S(1)} %all-to-all-done.1.refs_1_, f32[32,512]{1,0:T(8,128)S(1)} %get-tuple-element.95.refs_2_, ...), custom_call_target="tpu_custom_call" | custom-call | tf_op jit(solution)/shard_map/pallas_call | solution.py:605
  106.7 2.8 %all-to-all-start.2 = ((f32[32,2,512]{2,1,0:T(2,128)}), f32[32,2,512]{2,1,0:T(2,128)S(1)}, u32[]{:S(2)}, u32[]{:S(2)}) async-start(f32[32,2,512]{2,1,0:T(2,128)} %get-tuple-element.98.refs_4_), calls=%async_computation.2 | async-start | bytes 262144 | tf_op jit(solution)/shard_map/all_to_all | solution.py:855
  109.5 5.6 %shard_map.245.refs_6_ = bf16[1,544,512]{2,1,0:T(8,128)(2,1)S(1)} custom-call(f32[4,512]{1,0:T(4,128)S(1)} %get-tuple-element.92.refs_1_.refs_0_.refs_2_, f32[4,512]{1,0:T(4,128)S(1)} %get-tuple-element.96.refs_2_.refs_3_.refs_1_, bf16[9,512,512]{2,1,0:T(8,128)(2,1)} %get-tuple-element.100.refs_2_.refs_4_, ...), custom_call_target="tpu_custom_call" | custom-call | tf_op jit(solution)/shard_map/pallas_call | solution.py:605
  115.1 0.8 copy-done.6
  115.9 1.6 all-to-all-done.2.refs_1_
  117.5 2.6 %shard_map.246 = (f32[2,512]{1,0:T(2,128)S(1)}, bf16[2,64,640]{2,1,0:T(8,128)(2,1)S(1)}, bf16[2,64,640]{2,1,0:T(8,128)(2,1)S(1)}, bf16[2,64,640]{2,1,0:T(8,128)(...) custom-call(f32[4,512]{1,0:T(4,128)S(1)} %get-tuple-element.97.refs_0_, ...), custom_call_target="tpu_custom_call" | custom-call | tf_op jit(solution)/shard_map/pallas_call | solution.py:605
  120.7 0.8 collective-permute-start.30
  121.5 2.2 %collective-permute-start.31 = (bf16[2,64,640]{2,1,0:T(8,128)(2,1)S(1)}, bf16[2,64,640]{2,1,0:T(8,128)(2,1)S(1)}, u32[]{:S(2)}, u32[]{:S(2)}) collective-permute-start(bf16[2,64,640]{2,1,0:T(8,128)(2,1)S(1)} %get-tuple-element.106), channel_id=1, source_target_pairs={{0,18},{2,16},{16,2},{18,0},{1,19},{3,17},{17,3},{19,1},{4,22},{6,... | collective-permute-start | bytes 491528 | tf_op jit(solution)/shard_map/ppermute | solution.py:633
  123.7 7.3 %shard_map.247 = (f32[544,512]{1,0:T(8,128)}, f32[32,2,512]{2,1,0:T(2,128)}) custom-call(bf16[544,512]{1,0:T(8,128)(2,1)} %get-tuple-element.102.refs_0_, f32[544,512]{1,0:T(8,128)} %get-tuple-element.81.refs_0_.refs_1_.refs_4_, f32[4,512]{1,0:T(4,128)S(1)} %get-tuple-element.92.refs_1_.refs_0_.refs_2_, ...), custom_call_target="tpu_custom_call" | custom-call | tf_op jit(solution)/shard_map/pallas_call | solution.py:605
  131.0 4.3 %all-to-all-start.3 = ((f32[32,2,512]{2,1,0:T(2,128)}), f32[32,2,512]{2,1,0:T(2,128)S(1)}, u32[]{:S(2)}, u32[]{:S(2)}) async-start(f32[32,2,512]{2,1,0:T(2,128)} %get-tuple-element.107), calls=%async_computation.3 | async-start | bytes 262144 | tf_op jit(solution)/shard_map/all_to_all | solution.py:855
  135.3 6.9 %shard_map.248 = (bf16[4,9,16,512]{3,2,1,0:T(8,128)(2,1)}, bf16[4,9,16,512]{3,2,1,0:T(8,128)(2,1)}) custom-call(bf16[2,64,640]{2,1,0:T(8,128)(2,1)S(1)} %get-tuple-element.109.refs_0_, bf16[2,64,640]{2,1,0:T(8,128)(2,1)S(1)} %collective-permute-done.29.refs_1_, bf16[2,64,640]{2,1,0:T(8,128)(2,1)S(1)} %collective-permute-done.30.refs_2_, ...), custom_call_target="tpu_custom_call" | custom-call | tf_op jit(solution)/shard_map/pallas_call | solution.py:605
  142.2 1.0 all-to-all-done.3.refs_1_
  143.5 2.6 %shard_map.249 = (f32[2,512]{1,0:T(2,128)S(1)}, bf16[2,64,640]{2,1,0:T(8,128)(2,1)S(1)}, bf16[2,64,640]{2,1,0:T(8,128)(2,1)S(1)}, bf16[2,64,640]{2,1,0:T(8,128)(...) custom-call(f32[4,512]{1,0:T(4,128)S(1)} %get-tuple-element.92.refs_1_.refs_0_.refs_2_, ...), custom_call_target="tpu_custom_call" | custom-call | tf_op jit(solution)/shard_map/pallas_call | solution.py:605
  146.6 1.5 collective-permute-start.33
  148.1 1.6 collective-permute-start.34
  150.4 2.4 %collective-permute-start.37 = (bf16[9,16,512]{2,1,0:T(8,128)(2,1)S(1)}, bf16[9,16,512]{2,1,0:T(8,128)(2,1)S(1)}, u32[]{:S(2)}, u32[]{:S(2)}) collective-permute-start(bf16[9,16,512]{2,1,0:T(8,128)(2,1)S(1)} %get-tuple-element.146.refs_9_), channel_id=1, source_target_pairs={{0,8},{4,12},{8,0},{12,4},{1,9},{5,13},{9,1},{13,5},{2,10},{6,14},... | collective-permute-start | bytes 442376 | tf_op jit(solution)/shard_map/ppermute | solution.py:629
  153.2 2.3 %collective-permute-start.38 = (bf16[9,16,512]{2,1,0:T(8,128)(2,1)S(1)}, bf16[9,16,512]{2,1,0:T(8,128)(2,1)S(1)}, u32[]{:S(2)}, u32[]{:S(2)}) collective-permute-start(bf16[9,16,512]{2,1,0:T(8,128)(2,1)S(1)} %get-tuple-element.145.refs_10_), channel_id=1, source_target_pairs={{0,12},{4,8},{8,4},{12,0},{1,13},{5,9},{9,5},{13,1},{2,14},{6,10},... | collective-permute-start | bytes 442376 | tf_op jit(solution)/shard_map/ppermute | solution.py:629
  155.5 0.8 collective-permute-done.34.refs_3_
  156.3 0.7 copy-done.42
  157.0 7.6 %shard_map.250 = (bf16[4,9,16,512]{3,2,1,0:T(8,128)(2,1)}, bf16[4,9,16,512]{3,2,1,0:T(8,128)(2,1)}) custom-call(bf16[2,64,640]{2,1,0:T(8,128)(2,1)S(1)} %get-tuple-element.115.refs_0_, bf16[2,64,640]{2,1,0:T(8,128)(2,1)S(1)} %collective-permute-done.32.refs_1_, bf16[2,64,640]{2,1,0:T(8,128)(2,1)S(1)} %collective-permute-done.33.refs_2_, ...), custom_call_target="tpu_custom_call" | custom-call | tf_op jit(solution)/shard_map/pallas_call | solution.py:605
  164.7 1.0 slice_bitcast_fusion.3
  165.7 1.2 collective-permute-done.39
  167.1 1.7 collective-permute-start.40
  168.8 2.2 %collective-permute-start.41 = (bf16[9,16,512]{2,1,0:T(8,128)(2,1)S(1)}, bf16[9,16,512]{2,1,0:T(8,128)(2,1)S(1)}, u32[]{:S(2)}, u32[]{:S(2)}) collective-permute-start(bf16[9,16,512]{2,1,0:T(8,128)(2,1)S(1)} %get-tuple-element.143.refs_6_), channel_id=1, source_target_pairs={{0,8},{4,12},{8,0},{12,4},{1,9},{5,13},{9,1},{13,5},{2,10},{6,14},... | collective-permute-start | bytes 442376 | tf_op jit(solution)/shard_map/ppermute | solution.py:629
  171.5 8.4 %shard_map.251 = (bf16[5,5,6,512]{3,2,1,0:T(8,128)(2,1)}, bf16[7,7,2,512]{3,2,1,0:T(2,128)(2,1)}, bf16[9,9,2,512]{3,2,1,0:T(2,128)(2,1)}, f32[5,5,6,512]{3,2,1,0...) custom-call(bf16[544,512]{1,0:T(8,128)(2,1)} %get-tuple-element.113.refs_0_, ...), custom_call_target="tpu_custom_call" | custom-call | tf_op jit(solution)/shard_map/pallas_call | solution.py:605
  180.1 1.5 collective-permute-start.44
  181.7 1.0 collective-permute-done.41
  182.8 1.5 collective-permute-start.43
  184.4 0.7 multiply_subtract_fusion
  185.0 1.8 collective-permute-done.44
  186.8 1.6 collective-permute-done.43
  188.5 2.7 %fusion.2 = (f32[2,3,3,512,32]{3,4,2,1,0:T(8,128)}, f32[2,3,3,512,32]{3,4,2,1,0:T(8,128)}, f32[2,3,3,512,32]{3,4,2,1,0:T(8,128)}) fusion(f32[2,3,3,512,32]{3,4,2,1,0:T(8,128)S(1)} %copy-done.38, bf16[1,3,3,16,512]{4,3,2,1,0:T(8,128)(2,1)S(1)} %bitcast.88, bf16[1,3,3,16,512]{4,3,2,1,0:T(8,128)(2,1)S(1)} %bitcast.87, ...), kind=kLoop, calls=%fused_computation.5 | loop fusion | flops 6488064 | bytes 7667712 | tf_op jit(solution)/shard_map/transpose | solution.py:1023
  (158 shorter events, 9.2 us)
Async XLA Ops:
  0.7 14.8 %copy-start.8 = (bf16[6,5,5,512]{3,0,2,1:T(8,128)(2,1)S(1)}, bf16[6,5,5,512]{3,0,2,1:T(8,128)(2,1)}, u32[]{:S(2)}) copy-start(bf16[6,5,5,512]{3,0,2,1:T(8,128)(2,1)} %param.21) | copy-start | bytes 460804
  0.7 14.8 %copy-start.9 = (bf16[2,9,9,512]{3,0,2,1:T(2,128)(2,1)S(1)}, bf16[2,9,9,512]{3,0,2,1:T(2,128)(2,1)}, u32[]{:S(2)}) copy-start(bf16[2,9,9,512]{3,0,2,1:T(2,128)(2,1)} %param.23) | copy-start | bytes 497668
  0.7 14.8 %copy-start.12 = (bf16[2,7,7,512]{3,0,2,1:T(2,128)(2,1)S(1)}, bf16[2,7,7,512]{3,0,2,1:T(2,128)(2,1)}, u32[]{:S(2)}) copy-start(bf16[2,7,7,512]{3,0,2,1:T(2,128)(2,1)} %param.22) | copy-start | bytes 301060
  2.3 26.1 %copy-start.21 = (bf16[1,3,3,32,512]{4,3,2,1,0:T(8,128)(2,1)}, bf16[1,3,3,32,512]{4,3,2,1,0:T(8,128)(2,1)S(1)}, u32[]{:S(2)}) copy-start(bf16[1,3,3,32,512]{4,3,2,1,0:T(8,128)(2,1)S(1)} %get-tuple-element.149) | copy-start | bytes 884740
  2.3 12.5 %collective-permute-start.1 = (bf16[1,9,32,512]{3,2,1,0:T(8,128)(2,1)S(1)}, bf16[1,9,32,512]{3,2,1,0:T(8,128)(2,1)S(1)}, u32[]{:S(2)}, u32[]{:S(2)}) collective-permute-start(bf16[1,9,32,512]{3,2,1,0:T(8,128)(2,1)S(1)} %bitcast.81), channel_id=1, source_target_pairs={{0,2},{2,0},{1,3},{3,1},{4,6},{6,4},{5,7},{7,5},{8,10},{10,8},{9,1... | collective-permute-start | bytes 884744 | tf_op jit(solution)/shard_map/ppermute | solution.py:629
  5.3 9.4 %collective-permute-start.3 = (bf16[1,9,32,256]{3,2,1,0:T(8,128)(2,1)S(1)}, bf16[1,9,32,256]{3,2,1,0:T(8,128)(2,1)S(1)}, u32[]{:S(2)}, u32[]{:S(2)}) collective-permute-start(bf16[1,9,32,256]{3,2,1,0:T(8,128)(2,1)S(1)} %dynamic-slice_bitcast_fusion.1), channel_id=1, source_target_pairs={{0,8},{4,12},{8,0},{12,4},{1,9},{5,13},{9,1},{13,5},{2,10},{6,14},... | collective-permute-start | bytes 442376 | tf_op jit(solution)/shard_map/ppermute | solution.py:629
  10.7 12.1 %copy-start = (f32[544,128]{1,0:T(8,128)}, f32[544,128]{1,0:T(8,128)S(1)}, u32[]{:S(2)}) copy-start(f32[544,128]{1,0:T(8,128)S(1)} %get-tuple-element.75.refs_1_.refs_2_.refs_4_.refs_5_) | copy-start | bytes 835588
  10.7 14.4 %collective-permute-start.5 = (bf16[560,512]{1,0:T(8,128)(2,1)}, bf16[560,512]{1,0:T(8,128)(2,1)S(1)}, u32[]{:S(2)}, u32[]{:S(2)}) collective-permute-start(bf16[560,512]{1,0:T(8,128)(2,1)} %get-tuple-element.101.refs_0_.refs_5_.refs_4_), channel_id=1, source_target_pairs={{0,2},{2,0},{1,3},{3,1},{4,6},{6,4},{5,7},{7,5},{8,10},{10,8},{9,1... | collective-permute-start | bytes 1720328 | tf_op jit(solution)/shard_map/ppermute | solution.py:629
  11.2 14.1 %collective-permute-start.6 = (bf16[560,512]{1,0:T(8,128)(2,1)}, bf16[560,512]{1,0:T(8,128)(2,1)S(1)}, u32[]{:S(2)}, u32[]{:S(2)}) collective-permute-start(bf16[560,512]{1,0:T(8,128)(2,1)} %get-tuple-element.101.refs_0_.refs_5_.refs_4_), channel_id=1, source_target_pairs={{0,16},{16,0},{1,17},{17,1},{2,18},{18,2},{3,19},{19,3},{4,20},{20... | collective-permute-start | bytes 1720328 | tf_op jit(solution)/shard_map/ppermute | solution.py:629
  14.8 7.9 %collective-permute-start.4 = (bf16[2,9,32,256]{3,2,1,0:T(8,128)(2,1)S(1)}, bf16[2,9,32,256]{3,2,1,0:T(8,128)(2,1)S(1)}, u32[]{:S(2)}, u32[]{:S(2)}) collective-permute-start(bf16[2,9,32,256]{3,2,1,0:T(8,128)(2,1)S(1)} %pad_maximum_fusion.2), channel_id=1, source_target_pairs={{0,4},{4,0},{8,12},{12,8},{1,5},{5,1},{9,13},{13,9},{2,6},{6,2},{1... | collective-permute-start | bytes 884744 | tf_op jit(solution)/shard_map/ppermute | solution.py:629
  22.8 26.4 %copy-start.19 = (bf16[3,9,32,256]{3,2,1,0:T(8,128)(2,1)}, bf16[3,9,32,256]{3,2,1,0:T(8,128)(2,1)S(1)}, u32[]{:S(2)}) copy-start(bf16[3,9,32,256]{3,2,1,0:T(8,128)(2,1)S(1)} %pad_maximum_fusion.refs_7_.refs_4_) | copy-start | bytes 1327108
  25.0 24.1 %copy-start.4 = (bf16[560,512]{1,0:T(8,128)(2,1)}, bf16[560,512]{1,0:T(8,128)(2,1)S(1)}, u32[]{:S(2)}) copy-start(bf16[560,512]{1,0:T(8,128)(2,1)S(1)} %collective-permute-done.5.refs_17_.refs_14_.refs_3_.refs_5_) | copy-start | bytes 1720324
  25.3 23.9 %copy-start.17 = (bf16[560,512]{1,0:T(8,128)(2,1)}, bf16[560,512]{1,0:T(8,128)(2,1)S(1)}, u32[]{:S(2)}) copy-start(bf16[560,512]{1,0:T(8,128)(2,1)S(1)} %collective-permute-done.6.refs_18_.refs_15_.refs_4_.refs_6_) | copy-start | bytes 1720324
  25.3 10.2 %collective-permute-start.10 = (bf16[3,9,32,256]{3,2,1,0:T(8,128)(2,1)S(1)}, bf16[3,9,32,256]{3,2,1,0:T(8,128)(2,1)S(1)}, u32[]{:S(2)}, u32[]{:S(2)}) collective-permute-start(bf16[3,9,32,256]{3,2,1,0:T(8,128)(2,1)S(1)} %pad_maximum_fusion.refs_7_.refs_4_), channel_id=1, source_target_pairs={{0,16},{16,0},{1,17},{17,1},{2,18},{18,2},{3,19},{19,3},{4,20},{20... | collective-permute-start | bytes 1327112 | tf_op jit(solution)/shard_map/ppermute | solution.py:629
  26.8 11.0 %collective-permute-start.8 = (bf16[3,9,32,256]{3,2,1,0:T(8,128)(2,1)S(1)}, bf16[3,9,32,256]{3,2,1,0:T(8,128)(2,1)S(1)}, u32[]{:S(2)}, u32[]{:S(2)}) collective-permute-start(bf16[3,9,32,256]{3,2,1,0:T(8,128)(2,1)S(1)} %pad_maximum_fusion.refs_7_.refs_4_), channel_id=1, source_target_pairs={{0,2},{2,0},{1,3},{3,1},{4,6},{6,4},{5,7},{7,5},{8,10},{10,8},{9,1... | collective-permute-start | bytes 1327112 | tf_op jit(solution)/shard_map/ppermute | solution.py:629
  28.3 11.4 %collective-permute-start = (bf16[1,9,32,512]{3,2,1,0:T(8,128)(2,1)S(1)}, bf16[1,9,32,512]{3,2,1,0:T(8,128)(2,1)S(1)}, u32[]{:S(2)}, u32[]{:S(2)}) collective-permute-start(bf16[1,9,32,512]{3,2,1,0:T(8,128)(2,1)S(1)} %bitcast.83), channel_id=1, source_target_pairs={{0,1},{1,0},{2,3},{3,2},{4,5},{5,4},{6,7},{7,6},{8,9},{9,8},{10,11... | collective-permute-start | bytes 884744 | tf_op jit(solution)/shard_map/ppermute | solution.py:629
  28.3 11.3 %collective-permute-start.19 = (bf16[1,9,32,256]{3,2,1,0:T(8,128)(2,1)S(1)}, bf16[1,9,32,256]{3,2,1,0:T(8,128)(2,1)S(1)}, u32[]{:S(2)}, u32[]{:S(2)}) collective-permute-start(bf16[1,9,32,256]{3,2,1,0:T(8,128)(2,1)S(1)} %dynamic-slice_bitcast_fusion), channel_id=1, source_target_pairs={{0,8},{4,12},{8,0},{12,4},{1,9},{5,13},{9,1},{13,5},{2,10},{6,14},... | collective-permute-start | bytes 442376 | tf_op jit(solution)/shard_map/ppermute | solution.py:629
  30.6 10.8 %collective-permute-start.2 = (bf16[1,9,32,512]{3,2,1,0:T(8,128)(2,1)S(1)}, bf16[1,9,32,512]{3,2,1,0:T(8,128)(2,1)S(1)}, u32[]{:S(2)}, u32[]{:S(2)}) collective-permute-start(bf16[1,9,32,512]{3,2,1,0:T(8,128)(2,1)S(1)} %copy-done.34), channel_id=1, source_target_pairs={{0,1},{1,0},{2,3},{3,2},{4,5},{5,4},{6,7},{7,6},{8,9},{9,8},{10,11... | collective-permute-start | bytes 884744 | tf_op jit(solution)/shard_map/ppermute | solution.py:629
  35.5 13.7 %copy-start.22 = (bf16[3,9,32,256]{3,2,1,0:T(8,128)(2,1)}, bf16[3,9,32,256]{3,2,1,0:T(8,128)(2,1)S(1)}, u32[]{:S(2)}) copy-start(bf16[3,9,32,256]{3,2,1,0:T(8,128)(2,1)S(1)} %collective-permute-done.10.refs_11_.refs_8_) | copy-start | bytes 1327108
  35.5 13.1 %collective-permute-start.17 = (bf16[1,9,32,512]{3,2,1,0:T(8,128)(2,1)S(1)}, bf16[1,9,32,512]{3,2,1,0:T(8,128)(2,1)}, u32[]{:S(2)}, u32[]{:S(2)}) collective-permute-start(bf16[1,9,32,512]{3,2,1,0:T(8,128)(2,1)S(1)} %bitcast.68), channel_id=1, source_target_pairs={{0,2},{2,0},{1,3},{3,1},{4,6},{6,4},{5,7},{7,5},{8,10},{10,8},{9,1... | collective-permute-start | bytes 884744 | tf_op jit(solution)/shard_map/ppermute | solution.py:629
  37.9 15.1 %copy-start.23 = (bf16[3,9,32,256]{3,2,1,0:T(8,128)(2,1)}, bf16[3,9,32,256]{3,2,1,0:T(8,128)(2,1)S(1)}, u32[]{:S(2)}) copy-start(bf16[3,9,32,256]{3,2,1,0:T(8,128)(2,1)S(1)} %collective-permute-done.8.refs_9_.refs_6_) | copy-start | bytes 1327108
  37.9 10.2 %collective-permute-start.12 = (bf16[3,9,16,256]{3,2,1,0:T(8,128)(2,1)S(1)}, bf16[3,9,16,256]{3,2,1,0:T(8,128)(2,1)S(1)}, u32[]{:S(2)}, u32[]{:S(2)}) collective-permute-start(bf16[3,9,16,256]{3,2,1,0:T(8,128)(2,1)S(1)} %slice.83), channel_id=1, source_target_pairs={{0,2},{2,0},{1,3},{3,1},{4,6},{6,4},{5,7},{7,5},{8,10},{10,8},{9,1... | collective-permute-start | bytes 663560 | tf_op jit(solution)/shard_map/ppermute | solution.py:629
  39.6 8.5 %collective-permute-start.13 = (bf16[3,9,16,256]{3,2,1,0:T(8,128)(2,1)S(1)}, bf16[3,9,16,256]{3,2,1,0:T(8,128)(2,1)S(1)}, u32[]{:S(2)}, u32[]{:S(2)}) collective-permute-start(bf16[3,9,16,256]{3,2,1,0:T(8,128)(2,1)S(1)} %slice.84), channel_id=1, source_target_pairs={{0,16},{16,0},{1,17},{17,1},{2,18},{18,2},{3,19},{19,3},{4,20},{20... | collective-permute-start | bytes 663560 | tf_op jit(solution)/shard_map/ppermute | solution.py:629
  39.8 13.2 %copy-start.35 = (bf16[1,9,32,512]{3,2,1,0:T(8,128)(2,1)}, bf16[1,9,32,512]{3,2,1,0:T(8,128)(2,1)S(1)}, u32[]{:S(2)}) copy-start(bf16[1,9,32,512]{3,2,1,0:T(8,128)(2,1)S(1)} %collective-permute-done.refs_4_.refs_1_) | copy-start | bytes 884740
  39.8 8.9 %collective-permute-start.20 = (bf16[2,9,32,256]{3,2,1,0:T(8,128)(2,1)S(1)}, bf16[2,9,32,256]{3,2,1,0:T(8,128)(2,1)S(1)}, u32[]{:S(2)}, u32[]{:S(2)}) collective-permute-start(bf16[2,9,32,256]{3,2,1,0:T(8,128)(2,1)S(1)} %pad_maximum_fusion.3), channel_id=1, source_target_pairs={{0,4},{4,0},{8,12},{12,8},{1,5},{5,1},{9,13},{13,9},{2,6},{6,2},{1... | collective-permute-start | bytes 884744 | tf_op jit(solution)/shard_map/ppermute | solution.py:629
  41.4 7.8 %collective-permute-start.7 = (bf16[3,9,32,256]{3,2,1,0:T(8,128)(2,1)S(1)}, bf16[3,9,32,256]{3,2,1,0:T(8,128)(2,1)S(1)}, u32[]{:S(2)}, u32[]{:S(2)}) collective-permute-start(bf16[3,9,32,256]{3,2,1,0:T(8,128)(2,1)S(1)} %pad_maximum_fusion.refs_7_.refs_4_), channel_id=1, source_target_pairs={{0,1},{1,0},{2,3},{3,2},{4,5},{5,4},{6,7},{7,6},{8,9},{9,8},{10,11... | collective-permute-start | bytes 1327112 | tf_op jit(solution)/shard_map/ppermute | solution.py:629
  48.1 4.9 %collective-permute-start.11 = (bf16[3,9,32,256]{3,2,1,0:T(8,128)(2,1)S(1)}, bf16[3,9,32,256]{3,2,1,0:T(8,128)(2,1)S(1)}, u32[]{:S(2)}, u32[]{:S(2)}) collective-permute-start(bf16[3,9,32,256]{3,2,1,0:T(8,128)(2,1)S(1)} %collective-permute-done.10.refs_11_.refs_8_), channel_id=1, source_target_pairs={{0,1},{1,0},{2,3},{3,2},{4,5},{5,4},{6,7},{7,6},{8,9},{9,8},{10,11... | collective-permute-start | bytes 1327112 | tf_op jit(solution)/shard_map/ppermute | solution.py:629
  48.1 4.9 %collective-permute-start.9 = (bf16[3,9,32,256]{3,2,1,0:T(8,128)(2,1)S(1)}, bf16[3,9,32,256]{3,2,1,0:T(8,128)(2,1)S(1)}, u32[]{:S(2)}, u32[]{:S(2)}) collective-permute-start(bf16[3,9,32,256]{3,2,1,0:T(8,128)(2,1)S(1)} %collective-permute-done.8.refs_9_.refs_6_), channel_id=1, source_target_pairs={{0,1},{1,0},{2,3},{3,2},{4,5},{5,4},{6,7},{7,6},{8,9},{9,8},{10,11... | collective-permute-start | bytes 1327112 | tf_op jit(solution)/shard_map/ppermute | solution.py:629
  48.6 2.2 %collective-permute-start.14 = (bf16[3,9,16,256]{3,2,1,0:T(8,128)(2,1)S(1)}, bf16[3,9,16,256]{3,2,1,0:T(8,128)(2,1)S(1)}, u32[]{:S(2)}, u32[]{:S(2)}) collective-permute-start(bf16[3,9,16,256]{3,2,1,0:T(8,128)(2,1)S(1)} %collective-permute-done.12.refs_13_.refs_10_), channel_id=1, source_target_pairs={{0,1},{1,0},{2,3},{3,2},{4,5},{5,4},{6,7},{7,6},{8,9},{9,8},{10,11... | collective-permute-start | bytes 663560 | tf_op jit(solution)/shard_map/ppermute | solution.py:629
  48.7 3.9 %collective-permute-start.15 = (bf16[3,9,16,256]{3,2,1,0:T(8,128)(2,1)S(1)}, bf16[3,9,16,256]{3,2,1,0:T(8,128)(2,1)S(1)}, u32[]{:S(2)}, u32[]{:S(2)}) collective-permute-start(bf16[3,9,16,256]{3,2,1,0:T(8,128)(2,1)S(1)} %collective-permute-done.13.refs_15_.refs_12_), channel_id=1, source_target_pairs={{0,1},{1,0},{2,3},{3,2},{4,5},{5,4},{6,7},{7,6},{8,9},{9,8},{10,11... | collective-permute-start | bytes 663560 | tf_op jit(solution)/shard_map/ppermute | solution.py:629
  49.2 17.4 %copy-start.20 = (bf16[3,9,32,256]{3,2,1,0:T(8,128)(2,1)}, bf16[3,9,32,256]{3,2,1,0:T(8,128)(2,1)S(1)}, u32[]{:S(2)}) copy-start(bf16[3,9,32,256]{3,2,1,0:T(8,128)(2,1)S(1)} %pad_maximum_fusion.1.refs_7_.refs_9_) | copy-start | bytes 1327108
  49.2 27.0 %collective-permute-start.24 = (bf16[3,9,32,256]{3,2,1,0:T(8,128)(2,1)S(1)}, bf16[3,9,32,256]{3,2,1,0:T(8,128)(2,1)S(1)}, u32[]{:S(2)}, u32[]{:S(2)}) collective-permute-start(bf16[3,9,32,256]{3,2,1,0:T(8,128)(2,1)S(1)} %pad_maximum_fusion.1.refs_7_.refs_9_), channel_id=1, source_target_pairs={{0,16},{16,0},{1,17},{17,1},{2,18},{18,2},{3,19},{19,3},{4,20},{20... | collective-permute-start | bytes 1327112 | tf_op jit(solution)/shard_map/ppermute | solution.py:629
  50.8 25.6 %collective-permute-start.22 = (bf16[3,9,32,256]{3,2,1,0:T(8,128)(2,1)S(1)}, bf16[3,9,32,256]{3,2,1,0:T(8,128)(2,1)S(1)}, u32[]{:S(2)}, u32[]{:S(2)}) collective-permute-start(bf16[3,9,32,256]{3,2,1,0:T(8,128)(2,1)S(1)} %pad_maximum_fusion.1.refs_7_.refs_9_), channel_id=1, source_target_pairs={{0,2},{2,0},{1,3},{3,1},{4,6},{6,4},{5,7},{7,5},{8,10},{10,8},{9,1... | collective-permute-start | bytes 1327112 | tf_op jit(solution)/shard_map/ppermute | solution.py:629
  52.6 24.3 %collective-permute-start.26 = (bf16[3,9,32,256]{3,2,1,0:T(8,128)(2,1)S(1)}, bf16[3,9,32,256]{3,2,1,0:T(8,128)(2,1)}, u32[]{:S(2)}, u32[]{:S(2)}) collective-permute-start(bf16[3,9,32,256]{3,2,1,0:T(8,128)(2,1)S(1)} %pad_maximum_fusion.1.refs_7_.refs_9_), channel_id=1, source_target_pairs={{0,18},{2,16},{16,2},{18,0},{1,19},{3,17},{17,3},{19,1},{4,22},{6,... | collective-permute-start | bytes 1327112 | tf_op jit(solution)/shard_map/ppermute | solution.py:633
  60.4 16.5 %all-to-all-start = ((f32[32,2,640]{2,1,0:T(2,128)}), f32[32,2,640]{2,1,0:T(2,128)S(1)}, u32[]{:S(2)}, u32[]{:S(2)}) async-start(f32[32,2,640]{2,1,0:T(2,128)} %get-tuple-element.82.refs_16_), calls=%async_computation | async-start | bytes 327680 | tf_op jit(solution)/shard_map/all_to_all | solution.py:855
  66.4 13.6 %copy-start.18 = (bf16[560,512]{1,0:T(8,128)(2,1)S(1)}, bf16[560,512]{1,0:T(8,128)(2,1)}, u32[]{:S(2)}) copy-start(bf16[560,512]{1,0:T(8,128)(2,1)} %get-tuple-element.101.refs_0_.refs_5_.refs_4_) | copy-start | bytes 1720324
  66.4 17.7 %copy-start.1 = (f32[544,128]{1,0:T(8,128)S(1)}, f32[544,128]{1,0:T(8,128)}, u32[]{:S(2)}) copy-start(f32[544,128]{1,0:T(8,128)} %copy-done) | copy-start | bytes 835588
  66.4 10.5 %collective-permute-start.16 = (bf16[1,9,32,512]{3,2,1,0:T(8,128)(2,1)S(1)}, bf16[1,9,32,512]{3,2,1,0:T(8,128)(2,1)}, u32[]{:S(2)}, u32[]{:S(2)}) collective-permute-start(bf16[1,9,32,512]{3,2,1,0:T(8,128)(2,1)S(1)} %bitcast.69), channel_id=1, source_target_pairs={{0,1},{1,0},{2,3},{3,2},{4,5},{5,4},{6,7},{7,6},{8,9},{9,8},{10,11... | collective-permute-start | bytes 884744 | tf_op jit(solution)/shard_map/ppermute | solution.py:629
  66.6 15.9 %collective-permute-start.21 = (bf16[3,9,32,256]{3,2,1,0:T(8,128)(2,1)S(1)}, bf16[3,9,32,256]{3,2,1,0:T(8,128)(2,1)}, u32[]{:S(2)}, u32[]{:S(2)}) collective-permute-start(bf16[3,9,32,256]{3,2,1,0:T(8,128)(2,1)S(1)} %pad_maximum_fusion.1.refs_7_.refs_9_), channel_id=1, source_target_pairs={{0,1},{1,0},{2,3},{3,2},{4,5},{5,4},{6,7},{7,6},{8,9},{9,8},{10,11... | collective-permute-start | bytes 1327112 | tf_op jit(solution)/shard_map/ppermute | solution.py:629
  76.3 6.3 %collective-permute-start.25 = (bf16[3,9,32,256]{3,2,1,0:T(8,128)(2,1)S(1)}, bf16[3,9,32,256]{3,2,1,0:T(8,128)(2,1)S(1)}, u32[]{:S(2)}, u32[]{:S(2)}) collective-permute-start(bf16[3,9,32,256]{3,2,1,0:T(8,128)(2,1)S(1)} %collective-permute-done.24.refs_11_.refs_13_), channel_id=1, source_target_pairs={{0,1},{1,0},{2,3},{3,2},{4,5},{5,4},{6,7},{7,6},{8,9},{9,8},{10,11... | collective-permute-start | bytes 1327112 | tf_op jit(solution)/shard_map/ppermute | solution.py:629
  76.4 6.1 %collective-permute-start.23 = (bf16[3,9,32,256]{3,2,1,0:T(8,128)(2,1)S(1)}, bf16[3,9,32,256]{3,2,1,0:T(8,128)(2,1)}, u32[]{:S(2)}, u32[]{:S(2)}) collective-permute-start(bf16[3,9,32,256]{3,2,1,0:T(8,128)(2,1)S(1)} %collective-permute-done.22.refs_9_.refs_11_), channel_id=1, source_target_pairs={{0,1},{1,0},{2,3},{3,2},{4,5},{5,4},{6,7},{7,6},{8,9},{9,8},{10,11... | collective-permute-start | bytes 1327112 | tf_op jit(solution)/shard_map/ppermute | solution.py:629
  76.9 5.7 %collective-permute-start.27 = (bf16[3,9,32,256]{3,2,1,0:T(8,128)(2,1)}, bf16[3,9,32,256]{3,2,1,0:T(8,128)(2,1)S(1)}, u32[]{:S(2)}, u32[]{:S(2)}) collective-permute-start(bf16[3,9,32,256]{3,2,1,0:T(8,128)(2,1)} %collective-permute-done.26.refs_13_.refs_15_), channel_id=1, source_target_pairs={{0,1},{1,0},{2,3},{3,2},{4,5},{5,4},{6,7},{7,6},{8,9},{9,8},{10,11... | collective-permute-start | bytes 1327112 | tf_op jit(solution)/shard_map/ppermute | solution.py:629
  77.0 3.1 %collective-permute-start.18 = (bf16[1,9,32,512]{3,2,1,0:T(8,128)(2,1)}, bf16[1,9,32,512]{3,2,1,0:T(8,128)(2,1)S(1)}, u32[]{:S(2)}, u32[]{:S(2)}) collective-permute-start(bf16[1,9,32,512]{3,2,1,0:T(8,128)(2,1)} %collective-permute-done.17.refs_5_.refs_7_), channel_id=1, source_target_pairs={{0,1},{1,0},{2,3},{3,2},{4,5},{5,4},{6,7},{7,6},{8,9},{9,8},{10,11... | collective-permute-start | bytes 884744 | tf_op jit(solution)/shard_map/ppermute | solution.py:629
  80.0 29.5 %collective-permute-start.28 = (bf16[560,512]{1,0:T(8,128)(2,1)S(1)}, bf16[560,512]{1,0:T(8,128)(2,1)}, u32[]{:S(2)}, u32[]{:S(2)}) collective-permute-start(bf16[560,512]{1,0:T(8,128)(2,1)S(1)} %copy-done.18), channel_id=1, source_target_pairs={{0,18},{2,16},{16,2},{18,0},{1,19},{3,17},{17,3},{19,1},{4,22},{6,... | collective-permute-start | bytes 1720328 | tf_op jit(solution)/shard_map/ppermute | solution.py:633
  91.1 12.0 %all-to-all-start.1 = ((f32[32,2,512]{2,1,0:T(2,128)}), f32[32,2,512]{2,1,0:T(2,128)S(1)}, u32[]{:S(2)}, u32[]{:S(2)}) async-start(f32[32,2,512]{2,1,0:T(2,128)} %get-tuple-element.94.refs_5_), calls=%async_computation.1 | async-start | bytes 262144 | tf_op jit(solution)/shard_map/all_to_all | solution.py:855
  106.7 10.8 %all-to-all-start.2 = ((f32[32,2,512]{2,1,0:T(2,128)}), f32[32,2,512]{2,1,0:T(2,128)S(1)}, u32[]{:S(2)}, u32[]{:S(2)}) async-start(f32[32,2,512]{2,1,0:T(2,128)} %get-tuple-element.98.refs_4_), calls=%async_computation.2 | async-start | bytes 262144 | tf_op jit(solution)/shard_map/all_to_all | solution.py:855
  120.1 10.9 %collective-permute-start.29 = (bf16[2,64,640]{2,1,0:T(8,128)(2,1)S(1)}, bf16[2,64,640]{2,1,0:T(8,128)(2,1)S(1)}, u32[]{:S(2)}, u32[]{:S(2)}) collective-permute-start(bf16[2,64,640]{2,1,0:T(8,128)(2,1)S(1)} %get-tuple-element.104), channel_id=1, source_target_pairs={{0,2},{2,0},{1,3},{3,1},{4,6},{6,4},{5,7},{7,5},{8,10},{10,8},{9,1... | collective-permute-start | bytes 491528 | tf_op jit(solution)/shard_map/ppermute | solution.py:629
  120.7 10.3 %collective-permute-start.30 = (bf16[2,64,640]{2,1,0:T(8,128)(2,1)S(1)}, bf16[2,64,640]{2,1,0:T(8,128)(2,1)S(1)}, u32[]{:S(2)}, u32[]{:S(2)}) collective-permute-start(bf16[2,64,640]{2,1,0:T(8,128)(2,1)S(1)} %get-tuple-element.105), channel_id=1, source_target_pairs={{0,16},{16,0},{1,17},{17,1},{2,18},{18,2},{3,19},{19,3},{4,20},{20... | collective-permute-start | bytes 491528 | tf_op jit(solution)/shard_map/ppermute | solution.py:629
  121.5 9.5 %collective-permute-start.31 = (bf16[2,64,640]{2,1,0:T(8,128)(2,1)S(1)}, bf16[2,64,640]{2,1,0:T(8,128)(2,1)S(1)}, u32[]{:S(2)}, u32[]{:S(2)}) collective-permute-start(bf16[2,64,640]{2,1,0:T(8,128)(2,1)S(1)} %get-tuple-element.106), channel_id=1, source_target_pairs={{0,18},{2,16},{16,2},{18,0},{1,19},{3,17},{17,3},{19,1},{4,22},{6,... | collective-permute-start | bytes 491528 | tf_op jit(solution)/shard_map/ppermute | solution.py:633
  131.0 12.3 %all-to-all-start.3 = ((f32[32,2,512]{2,1,0:T(2,128)}), f32[32,2,512]{2,1,0:T(2,128)S(1)}, u32[]{:S(2)}, u32[]{:S(2)}) async-start(f32[32,2,512]{2,1,0:T(2,128)} %get-tuple-element.107), calls=%async_computation.3 | async-start | bytes 262144 | tf_op jit(solution)/shard_map/all_to_all | solution.py:855
  143.3 6.4 %collective-permute-start.35 = (bf16[4,9,16,512]{3,2,1,0:T(8,128)(2,1)}, bf16[4,9,16,512]{3,2,1,0:T(8,128)(2,1)S(1)}, u32[]{:S(2)}, u32[]{:S(2)}) collective-permute-start(bf16[4,9,16,512]{3,2,1,0:T(8,128)(2,1)} %get-tuple-element.119.refs_6_), channel_id=1, source_target_pairs={{0,1},{1,0},{2,3},{3,2},{4,5},{5,4},{6,7},{7,6},{8,9},{9,8},{10,11... | collective-permute-start | bytes 1769480 | tf_op jit(solution)/shard_map/ppermute | solution.py:629
  146.1 7.1 %collective-permute-start.32 = (bf16[2,64,640]{2,1,0:T(8,128)(2,1)S(1)}, bf16[2,64,640]{2,1,0:T(8,128)(2,1)S(1)}, u32[]{:S(2)}, u32[]{:S(2)}) collective-permute-start(bf16[2,64,640]{2,1,0:T(8,128)(2,1)S(1)} %get-tuple-element.116), channel_id=1, source_target_pairs={{0,2},{2,0},{1,3},{3,1},{4,6},{6,4},{5,7},{7,5},{8,10},{10,8},{9,1... | collective-permute-start | bytes 491528 | tf_op jit(solution)/shard_map/ppermute | solution.py:629
  146.6 8.9 %collective-permute-start.33 = (bf16[2,64,640]{2,1,0:T(8,128)(2,1)S(1)}, bf16[2,64,640]{2,1,0:T(8,128)(2,1)S(1)}, u32[]{:S(2)}, u32[]{:S(2)}) collective-permute-start(bf16[2,64,640]{2,1,0:T(8,128)(2,1)S(1)} %get-tuple-element.117), channel_id=1, source_target_pairs={{0,16},{16,0},{1,17},{17,1},{2,18},{18,2},{3,19},{19,3},{4,20},{20... | collective-permute-start | bytes 491528 | tf_op jit(solution)/shard_map/ppermute | solution.py:629
  148.1 8.2 %collective-permute-start.34 = (bf16[2,64,640]{2,1,0:T(8,128)(2,1)S(1)}, bf16[2,64,640]{2,1,0:T(8,128)(2,1)S(1)}, u32[]{:S(2)}, u32[]{:S(2)}) collective-permute-start(bf16[2,64,640]{2,1,0:T(8,128)(2,1)S(1)} %get-tuple-element.118), channel_id=1, source_target_pairs={{0,18},{2,16},{16,2},{18,0},{1,19},{3,17},{17,3},{19,1},{4,22},{6,... | collective-permute-start | bytes 491528 | tf_op jit(solution)/shard_map/ppermute | solution.py:633
  149.8 14.7 %collective-permute-start.36 = (bf16[9,16,512]{2,1,0:T(8,128)(2,1)S(1)}, bf16[9,16,512]{2,1,0:T(8,128)(2,1)S(1)}, u32[]{:S(2)}, u32[]{:S(2)}) collective-permute-start(bf16[9,16,512]{2,1,0:T(8,128)(2,1)S(1)} %get-tuple-element.147.refs_8_), channel_id=1, source_target_pairs={{0,4},{4,0},{8,12},{12,8},{1,5},{5,1},{9,13},{13,9},{2,6},{6,2},{1... | collective-permute-start | bytes 442376 | tf_op jit(solution)/shard_map/ppermute | solution.py:629
  150.4 14.2 %collective-permute-start.37 = (bf16[9,16,512]{2,1,0:T(8,128)(2,1)S(1)}, bf16[9,16,512]{2,1,0:T(8,128)(2,1)S(1)}, u32[]{:S(2)}, u32[]{:S(2)}) collective-permute-start(bf16[9,16,512]{2,1,0:T(8,128)(2,1)S(1)} %get-tuple-element.146.refs_9_), channel_id=1, source_target_pairs={{0,8},{4,12},{8,0},{12,4},{1,9},{5,13},{9,1},{13,5},{2,10},{6,14},... | collective-permute-start | bytes 442376 | tf_op jit(solution)/shard_map/ppermute | solution.py:629
  153.2 11.4 %collective-permute-start.38 = (bf16[9,16,512]{2,1,0:T(8,128)(2,1)S(1)}, bf16[9,16,512]{2,1,0:T(8,128)(2,1)S(1)}, u32[]{:S(2)}, u32[]{:S(2)}) collective-permute-start(bf16[9,16,512]{2,1,0:T(8,128)(2,1)S(1)} %get-tuple-element.145.refs_10_), channel_id=1, source_target_pairs={{0,12},{4,8},{8,4},{12,0},{1,13},{5,9},{9,5},{13,1},{2,14},{6,10},... | collective-permute-start | bytes 442376 | tf_op jit(solution)/shard_map/ppermute | solution.py:629
  164.6 2.3 %collective-permute-start.39 = (bf16[4,9,16,512]{3,2,1,0:T(8,128)(2,1)}, bf16[4,9,16,512]{3,2,1,0:T(8,128)(2,1)S(1)}, u32[]{:S(2)}, u32[]{:S(2)}) collective-permute-start(bf16[4,9,16,512]{3,2,1,0:T(8,128)(2,1)} %get-tuple-element.122), channel_id=1, source_target_pairs={{0,1},{1,0},{2,3},{3,2},{4,5},{5,4},{6,7},{7,6},{8,9},{9,8},{10,11... | collective-permute-start | bytes 1769480 | tf_op jit(solution)/shard_map/ppermute | solution.py:629
  167.1 14.6 %collective-permute-start.40 = (bf16[9,16,512]{2,1,0:T(8,128)(2,1)S(1)}, bf16[9,16,512]{2,1,0:T(8,128)(2,1)S(1)}, u32[]{:S(2)}, u32[]{:S(2)}) collective-permute-start(bf16[9,16,512]{2,1,0:T(8,128)(2,1)S(1)} %get-tuple-element.144.refs_5_), channel_id=1, source_target_pairs={{0,4},{4,0},{8,12},{12,8},{1,5},{5,1},{9,13},{13,9},{2,6},{6,2},{1... | collective-permute-start | bytes 442376 | tf_op jit(solution)/shard_map/ppermute | solution.py:629
  168.8 13.9 %collective-permute-start.41 = (bf16[9,16,512]{2,1,0:T(8,128)(2,1)S(1)}, bf16[9,16,512]{2,1,0:T(8,128)(2,1)S(1)}, u32[]{:S(2)}, u32[]{:S(2)}) collective-permute-start(bf16[9,16,512]{2,1,0:T(8,128)(2,1)S(1)} %get-tuple-element.143.refs_6_), channel_id=1, source_target_pairs={{0,8},{4,12},{8,0},{12,4},{1,9},{5,13},{9,1},{13,5},{2,10},{6,14},... | collective-permute-start | bytes 442376 | tf_op jit(solution)/shard_map/ppermute | solution.py:629
  171.0 11.7 %collective-permute-start.42 = (bf16[9,16,512]{2,1,0:T(8,128)(2,1)S(1)}, bf16[9,16,512]{2,1,0:T(8,128)(2,1)S(1)}, u32[]{:S(2)}, u32[]{:S(2)}) collective-permute-start(bf16[9,16,512]{2,1,0:T(8,128)(2,1)S(1)} %get-tuple-element.142.refs_7_), channel_id=1, source_target_pairs={{0,12},{4,8},{8,4},{12,0},{1,13},{5,9},{9,5},{13,1},{2,14},{6,10},... | collective-permute-start | bytes 442376 | tf_op jit(solution)/shard_map/ppermute | solution.py:629
  171.5 16.9 %copy-start.39 = (f32[2,3,3,512,32]{3,4,2,1,0:T(8,128)S(1)}, f32[2,3,3,512,32]{3,4,2,1,0:T(8,128)}, u32[]{:S(2)}) copy-start(f32[2,3,3,512,32]{3,4,2,1,0:T(8,128)} %param.26) | copy-start | bytes 3538948
  180.1 6.7 %collective-permute-start.44 = (bf16[9,16,512]{2,1,0:T(8,128)(2,1)S(1)}, bf16[9,16,512]{2,1,0:T(8,128)(2,1)S(1)}, u32[]{:S(2)}, u32[]{:S(2)}) collective-permute-start(bf16[9,16,512]{2,1,0:T(8,128)(2,1)S(1)} %add_convert_fusion), channel_id=1, source_target_pairs={{0,16},{16,0},{1,17},{17,1},{2,18},{18,2},{3,19},{19,3},{4,20},{20... | collective-permute-start | bytes 442376 | tf_op jit(solution)/shard_map/ppermute | solution.py:629
  182.8 5.6 %collective-permute-start.43 = (bf16[9,16,512]{2,1,0:T(8,128)(2,1)S(1)}, bf16[9,16,512]{2,1,0:T(8,128)(2,1)S(1)}, u32[]{:S(2)}, u32[]{:S(2)}) collective-permute-start(bf16[9,16,512]{2,1,0:T(8,128)(2,1)S(1)} %add_convert_fusion.1), channel_id=1, source_target_pairs={{0,16},{16,0},{1,17},{17,1},{2,18},{18,2},{3,19},{19,3},{4,20},{20... | collective-permute-start | bytes 442376 | tf_op jit(solution)/shard_map/ppermute | solution.py:629
  (30 other events, 156.0 us)
